TPU v7x, 128 devices: a whole 4x4x4 slice. The times are simulated.
128 devices in a mesh: brick: 32 (over z, y, core), ana: 4 (over x).
Axes of the slice: x: 4, y: 4, z: 4, core: 2. Of those that a mesh axis runs over, the one named last changes fastest.
Arguments:
- provisional: float32 [4, 3, 512, 128, 256], P(None, None, 'brick', 'ana'), may hold values from -120 to 120
- sample_index: int32 [32, 4, 32768], P('brick', 'ana'), may hold values from 0 to 131071, as said below
- owner_table: int32 [32, 32], replicated, may hold values from 0 to 31, each once within a row
- weighted_basis: float32 [16, 3, 4194304], P(None, None, ('brick', 'ana')), may hold values from -200 to 200
Outputs:
- new_basis: float32 [20, 3, 4194304], P(None, None, ('brick', 'ana'))
- core_factor: float32 [20, 20], replicated
Inputs may be any that keep to these rules, and one draw needn't show every extreme that they name: sample_index[b, a, j] lies between 4 j and 4 j + 3. `owner_table`: each row names every brick index once.
All inputs are finite; a program needn't handle non-finite values.
Results may differ from a plain program's by a relative error of at most 0.00021.
Values sent between devices are 32-bit elements; how exact they have to be, the bound alone decides.
No kernel may reach another device: no remote copies, remote signals or barrier semaphores. Data moves between devices by JAX's collectives and lax.ppermute only.
A program may use at most 128 MiB of HBM per device.

v0:
```python
import jax
import jax.numpy as jnp
from jax import lax
from jax.sharding import PartitionSpec as P


def padded_2(shard, sides, width):
    for axis, dim in sides:
        devices, length = (lax.axis_size(axis), shard.shape[dim])
        up = [(i, (i + 1) % devices) for i in range(devices - 1)]
        down = [(j, i) for i, j in up]
        last = lax.slice_in_dim(shard, length - width, length, axis=dim)
        first = lax.slice_in_dim(shard, 0, width, axis=dim)
        before = lax.ppermute(last, axis, up)
        after = lax.ppermute(first, axis, down)
        shard = jnp.concatenate([before, shard, after], axis=dim)
    return shard


def depth_difference(grid_field):
    padded = jnp.pad(grid_field, [(0, 0)] * (grid_field.ndim - 1) + [(1, 1)])
    return 0.5 * (padded[..., 2:] - padded[..., :-2])


def depth_neighbours(grid_field):
    padded = jnp.pad(grid_field, [(0, 0)] * (grid_field.ndim - 1) + [(1, 1)])
    return padded[..., 2:] + padded[..., :-2]


def divergence(padded):
    return (
        0.5 * (padded[:, 0, 2:, 1:-1] - padded[:, 0, :-2, 1:-1])
        + 0.5 * (padded[:, 1, 1:-1, 2:] - padded[:, 1, 1:-1, :-2])
        + depth_difference(padded[:, 2, 1:-1, 1:-1])
    )


def neighbour_sum(padded):
    return (
        padded[:, 2:, 1:-1]
        + padded[:, :-2, 1:-1]
        + padded[:, 1:-1, 2:]
        + padded[:, 1:-1, :-2]
        + depth_neighbours(padded[:, 1:-1, 1:-1])
    )


def pressure_gradient(padded):
    return jnp.stack(
        [
            0.5 * (padded[:, 2:, 1:-1] - padded[:, :-2, 1:-1]),
            0.5 * (padded[:, 1:-1, 2:] - padded[:, 1:-1, :-2]),
            depth_difference(padded[:, 1:-1, 1:-1]),
        ],
        axis=1,
    )


def select_samples(projected, chosen, samples_dev):
    snaps = projected.shape[0]
    depth = projected.shape[-1]
    offset = chosen - 4 * jnp.arange(samples_dev, dtype=jnp.int32)
    cell_mask = (offset[:, None] == jnp.arange(4, dtype=jnp.int32)[None, :]).reshape(-1, depth)
    grid_rows = projected.reshape(snaps, 3, -1, depth)
    kept = jnp.where(cell_mask[None, None], grid_rows, 0.0)
    pooling = (jnp.arange(depth)[:, None] // 4 == jnp.arange(depth // 4)[None, :]).astype(
        jnp.float32
    )
    picked = jnp.einsum("scrd,dk->scrk", kept, pooling, precision=lax.Precision.HIGHEST)
    return picked.reshape(snaps, 3, samples_dev)


def per_device(provisional, sample_index, owner_table, weighted_basis):
    snaps = provisional.shape[0]
    rank_count = weighted_basis.shape[0]
    samples_dev = sample_index.shape[2]
    bricks = lax.axis_size("brick")
    total_rows = 3.0 * samples_dev * bricks * lax.axis_size("ana")
    padded = padded_2(provisional, (("brick", 2), ("ana", 3)), 1)
    forcing = -divergence(padded)
    first_sweep = forcing / 6.0
    first_pad = padded_2(first_sweep, (("brick", 1), ("ana", 2)), 1)
    pressure = (forcing + neighbour_sum(first_pad)) / 6.0
    pressure_pad = padded_2(pressure, (("brick", 1), ("ana", 2)), 1)
    projected = provisional - pressure_gradient(pressure_pad)
    picked = select_samples(projected, sample_index[0, 0], samples_dev)
    owner_row = lax.dynamic_index_in_dim(owner_table, lax.axis_index("brick"), 0, keepdims=False)
    send_order = jnp.argsort(owner_row)
    blocks = picked.reshape(snaps, 3, bricks, samples_dev // bricks)
    basis_rows = weighted_basis.reshape(rank_count, 3 * samples_dev)
    outgoing = jnp.take(blocks, send_order, axis=2)
    arrived = lax.all_to_all(outgoing, "brick", split_axis=2, concat_axis=2, tiled=True)
    owned = arrived.reshape(snaps, 3 * samples_dev)
    stacked = jnp.concatenate([basis_rows, owned], axis=0)
    gram_matrix = lax.psum(
        jnp.dot(stacked, stacked.T, precision=lax.Precision.HIGHEST), ("brick", "ana")
    )
    gram_matrix = gram_matrix / total_rows
    lower_factor = jnp.linalg.cholesky(gram_matrix)
    new_basis = jax.scipy.linalg.solve_triangular(lower_factor, stacked, lower=True)
    return (new_basis.reshape(rank_count + snaps, 3, samples_dev), lower_factor.T)


def solution(mesh):
    placed = (
        P(None, None, "brick", "ana", None),
        P("brick", "ana", None),
        P(),
        P(None, None, ("brick", "ana")),
    )
    return jax.shard_map(
        per_device,
        mesh=mesh,
        in_specs=placed,
        out_specs=(P(None, None, ("brick", "ana")), P()),
        check_vma=False,
    )
```

profile of v0, /device:TPU:1, one launch (start us, length us, event | category | flops | bytes accessed | tf_op | source)
XLA Modules:
  0.0 235.2 jit_solution(17862394554159448518)
XLA Ops:
  1.8 4.6 %collective-permute-start.1 = (f32[4,3,1,32,256]{4,3,2,0,1:T(8,128)S(1)}, f32[4,3,1,32,256]{4,3,2,0,1:T(8,128)S(1)}, u32[]{:S(2)}, u32[]{:S(2)}) collective-permute-start(f32[4,3,1,32,256]{4,3,2,0,1:T(8,128)S(1)} %get-tuple-element.19), channel_id=1, source_target_pairs={{0,4},{4,8},{8,12},{12,16},{16,20},{20,24},{24,28},{28,32},{32,36}... | collective-permute-start | bytes 1179656 | tf_op jit(solution)/shard_map/ppermute | solution.py:14
  6.4 1.9 collective-permute-start
  8.9 1.9 reduce.9
  13.1 4.5 %constant_dynamic-update-slice_fusion.1 = f32[4,3,18,32,256]{4,3,2,0,1:T(8,128)S(1)} fusion(f32[4,3,18,32,256]{4,3,2,0,1:T(8,128)S(1)} %constant_dynamic-update-slice_fusion.2, f32[4,3,16,32,256]{4,3,2,1,0:T(8,128)} %param.4), kind=kLoop, calls=%fused_computation.79 | loop fusion | bytes 12582912
  19.3 4.0 %collective-permute-start.3 = (f32[4,3,18,1,256]{4,2,3,1,0:T(8,128)S(1)}, f32[4,3,18,1,256]{4,2,3,1,0:T(8,128)S(1)}, u32[]{:S(2)}, u32[]{:S(2)}) collective-permute-start(f32[4,3,18,1,256]{4,2,3,1,0:T(8,128)S(1)} %copy.68), channel_id=1, source_target_pairs={{0,1},{1,2},{2,3},{4,5},{5,6},{6,7},{8,9},{9,10},{10,11},{12,13},{... | collective-permute-start | bytes 663560 | tf_op jit(solution)/shard_map/ppermute | solution.py:14
  23.6 3.0 %collective-permute-done.2 = f32[4,3,18,1,256]{4,2,3,1,0:T(8,128)S(1)} collective-permute-done((f32[4,3,18,1,256]{4,2,3,1,0:T(8,128)S(1)}, f32[4,3,18,1,256]{4,2,3,1,0:T(8,128)S(1)}, u32[]{:S(2)}, u32[]{:S(2)}) %collective-permute-start.2) | collective-permute-done | bytes 221216 | tf_op jit(solution)/shard_map/ppermute | solution.py:15
  30.4 1.9 collective-permute-start.4
  32.3 5.2 %collective-permute-start.5 = (f32[4,1,32,256]{3,2,1,0:T(8,128)S(1)}, f32[4,1,32,256]{3,2,1,0:T(8,128)S(1)}, u32[]{:S(2)}, u32[]{:S(2)}) collective-permute-start(f32[4,1,32,256]{3,2,1,0:T(8,128)S(1)} %get-tuple-element.29), channel_id=1, source_target_pairs={{0,4},{4,8},{8,12},{12,16},{16,20},{20,24},{24,28},{28,32},{32,36}... | collective-permute-start | bytes 393224 | tf_op jit(solution)/shard_map/ppermute | solution.py:14
  40.9 4.7 %collective-permute-start.7 = (f32[4,18,1,256]{3,2,1,0:T(1,128)S(1)}, f32[4,18,1,256]{3,2,1,0:T(1,128)S(1)}, u32[]{:S(2)}, u32[]{:S(2)}) collective-permute-start(f32[4,18,1,256]{3,2,1,0:T(1,128)S(1)} %get-tuple-element.25), channel_id=1, source_target_pairs={{0,1},{1,2},{2,3},{4,5},{5,6},{6,7},{8,9},{9,10},{10,11},{12,13},{... | collective-permute-start | bytes 221192 | tf_op jit(solution)/shard_map/ppermute | solution.py:14
  47.0 1.8 fusion.9
  50.2 1.9 collective-permute-start.8
  52.1 5.2 %collective-permute-start.9 = (f32[4,1,32,256]{3,2,1,0:T(8,128)S(1)}, f32[4,1,32,256]{3,2,1,0:T(8,128)S(1)}, u32[]{:S(2)}, u32[]{:S(2)}) collective-permute-start(f32[4,1,32,256]{3,2,1,0:T(8,128)S(1)} %get-tuple-element.27), channel_id=1, source_target_pairs={{0,4},{4,8},{8,12},{12,16},{16,20},{20,24},{24,28},{28,32},{32,36}... | collective-permute-start | bytes 393224 | tf_op jit(solution)/shard_map/ppermute | solution.py:14
  57.7 6.0 %copy.86 = f32[3,2,8,32768]{3,2,0,1:T(8,128)} copy(f32[3,2,8,32768]{3,2,1,0:T(8,128)} %bitcast.62) | data formatting | bytes 12582912 | tf_op jit(solution)/shard_map/reshape | solution.py:90
  65.1 4.8 %collective-permute-start.11 = (f32[4,18,1,256]{3,2,1,0:T(1,128)S(1)}, f32[4,18,1,256]{3,2,1,0:T(1,128)S(1)}, u32[]{:S(2)}, u32[]{:S(2)}) collective-permute-start(f32[4,18,1,256]{3,2,1,0:T(1,128)S(1)} %get-tuple-element.23), channel_id=1, source_target_pairs={{0,1},{1,2},{2,3},{4,5},{5,6},{6,7},{8,9},{9,10},{10,11},{12,13},{... | collective-permute-start | bytes 221192 | tf_op jit(solution)/shard_map/ppermute | solution.py:14
  71.1 2.7 %fusion.18 = (f32[4,1,16,32,256]{4,3,2,1,0:T(8,128)S(1)}, f32[4,1,16,32,256]{4,3,2,1,0:T(8,128)S(1)}, f32[4,1,16,32,256]{4,3,2,1,0:T(8,128)S(1)}) fusion(f32[4,16,32,256]{3,2,1,0:T(8,128)S(1)} %copy-done.3, f32[4,1,32,256]{3,2,1,0:T(8,128)S(1)} %collective-permute-done.9, f32[4,1,32,256]{3,2,1,0:T(8,128)S(1)} %collective-permute-done.8, ...), kind=kLoop, calls=%fused_computation.34 | loop fusion | flops 7340032 | bytes 8798208 | tf_op jit(solution)/shard_map/stack | solution.py:49
  76.4 2.9 %fusion.27 = f32[4,3,512,64]{3,2,1,0:T(8,128)S(1)} fusion(f32[4,3,512,256]{3,2,1,0:T(8,128)S(1)} %bitcast_select_fusion, s32[256]{0:T(256)S(1)} %and_select_fusion), kind=kOutput, calls=%fused_computation.68 | convolution fusion | flops 1207975936 | bytes 7865344 | tf_op jit(solution)/shard_map/scrd,dk->scrk/dot_general | solution.py:69
  81.1 2.4 %copy.74 = f32[4,3,32,1024]{3,0,2,1:T(4,128)S(1)} copy(f32[4,3,32,1024]{3,2,1,0:T(8,128)} %reshape_reshape.3) | data formatting | bytes 3145728 | tf_op jit(solution)/shard_map/reshape;reshape | solution.py:89
  86.6 10.3 %all-to-all-start = ((f32[4,3,32,1024]{3,0,1,2:T(4,128)}), f32[4,3,32,1024]{3,0,1,2:T(4,128)S(1)}, u32[]{:S(2)}, u32[]{:S(2)}) async-start(f32[4,3,32,1024]{3,0,1,2:T(4,128)} %select_bitcast_fusion), calls=%async_computation | async-start | bytes 3145728 | tf_op jit(solution)/shard_map/all_to_all | solution.py:92
  97.0 5.9 %constant_dynamic-update-slice_fusion.4 = f32[20,98304]{1,0:T(8,128)} fusion(f32[16,98304]{1,0:T(8,128)} %bitcast.61), kind=kLoop, calls=%fused_computation.82 | loop fusion | bytes 12582912
  102.9 16.2 %all-to-all-done = f32[4,3,32,1024]{3,0,1,2:T(4,128)S(1)} async-done(((f32[4,3,32,1024]{3,0,1,2:T(4,128)}), f32[4,3,32,1024]{3,0,1,2:T(4,128)S(1)}, u32[]{:S(2)}, u32[]{:S(2)}) %all-to-all-start) | async-done | bytes 1572896 | tf_op jit(solution)/shard_map/all_to_all | solution.py:92
  122.4 13.3 %fusion.38 = f32[20,20]{0,1:T(8,128)S(1)} fusion(f32[20,98304]{1,0:T(8,128)} %constant_dynamic-update-slice_fusion.3), kind=kOutput, calls=%fused_computation.98 | convolution fusion | flops 471859200 | bytes 7865920 | tf_op jit(solution)/shard_map/dot_general | solution.py:96
  135.7 66.9 %psum.7 = f32[20,20]{0,1:T(8,128)S(1)} all-reduce(f32[20,20]{0,1:T(8,128)S(1)} %fusion.38), channel_id=1, replica_groups=mesh['brick'=32,'ana'=4] {'brick','ana'}, use_global_device_ids=true, to_apply=%region_1.2 | all-reduce | flops 400 | bytes 3200 | tf_op jit(solution)/shard_map/psum | solution.py:95
  207.4 10.4 %triangular_solve.39 = f32[3,32768,20]{1,0,2:T(4,128)} reshape(f32[98304,20]{0,1:T(8,128)} %bitcast.56) | data formatting | bytes 15728640 | tf_op jit(solution)/shard_map/jit(_solve_triangular)/triangular_solve | solution.py:100
  218.5 16.6 %fusion = f32[20,3,32768]{2,0,1:T(8,128)} fusion(f32[3,32768,20]{1,0,2:T(4,128)} %triangular_solve.39, f32[1,20,20]{1,2,0:T(8,128)S(1)} %custom-call.7), kind=kOutput, calls=%fused_computation.1 | convolution fusion | flops 471859200 | bytes 15730240 | tf_op jit(solution)/shard_map/jit(_solve_triangular)/triangular_solve | solution.py:100
  (80 shorter events, 34.8 us)
Async XLA Ops:
  0.6 10.8 %copy-start = (s32[32,32]{1,0:T(8,128)S(1)}, s32[32,32]{1,0:T(8,128)}, u32[]{:S(2)}) copy-start(s32[32,32]{1,0:T(8,128)} %param.6) | copy-start | bytes 12292
  1.8 11.2 %collective-permute-start.1 = (f32[4,3,1,32,256]{4,3,2,0,1:T(8,128)S(1)}, f32[4,3,1,32,256]{4,3,2,0,1:T(8,128)S(1)}, u32[]{:S(2)}, u32[]{:S(2)}) collective-permute-start(f32[4,3,1,32,256]{4,3,2,0,1:T(8,128)S(1)} %get-tuple-element.19), channel_id=1, source_target_pairs={{0,4},{4,8},{8,12},{12,16},{16,20},{20,24},{24,28},{28,32},{32,36}... | collective-permute-start | bytes 1179656 | tf_op jit(solution)/shard_map/ppermute | solution.py:14
  6.4 11.2 %collective-permute-start = (f32[4,3,1,32,256]{4,3,2,0,1:T(8,128)S(1)}, f32[4,3,1,32,256]{4,3,2,0,1:T(8,128)S(1)}, u32[]{:S(2)}, u32[]{:S(2)}) collective-permute-start(f32[4,3,1,32,256]{4,3,2,0,1:T(8,128)S(1)} %get-tuple-element.18), channel_id=1, source_target_pairs={{4,0},{8,4},{12,8},{16,12},{20,16},{24,20},{28,24},{32,28},{36,32}... | collective-permute-start | bytes 1179656 | tf_op jit(solution)/shard_map/ppermute | solution.py:15
  13.1 10.3 %slice-start = ((s8[6291456]{0:T(1024)(128)(4,1)}), s8[4194304]{0:T(1024)(128)(4,1)S(1)}, s32[]{:S(2)}) async-start(s8[6291456]{0:T(1024)(128)(4,1)} %bitcast.57), calls=%async_computation.1 | async-start | bytes 8388608
  13.1 10.2 %slice-start.1 = ((s8[6291456]{0:T(1024)(128)(4,1)}), s8[2097152]{0:T(1024)(128)(4,1)S(1)}, s32[]{:S(2)}) async-start(s8[6291456]{0:T(1024)(128)(4,1)} %bitcast.57), calls=%async_computation.2 | async-start | bytes 4194304
  18.0 8.6 %collective-permute-start.2 = (f32[4,3,18,1,256]{4,2,3,1,0:T(8,128)S(1)}, f32[4,3,18,1,256]{4,2,3,1,0:T(8,128)S(1)}, u32[]{:S(2)}, u32[]{:S(2)}) collective-permute-start(f32[4,3,18,1,256]{4,2,3,1,0:T(8,128)S(1)} %copy.66), channel_id=1, source_target_pairs={{1,0},{2,1},{3,2},{5,4},{6,5},{7,6},{9,8},{10,9},{11,10},{13,12},{... | collective-permute-start | bytes 663560 | tf_op jit(solution)/shard_map/ppermute | solution.py:15
  19.3 9.1 %collective-permute-start.3 = (f32[4,3,18,1,256]{4,2,3,1,0:T(8,128)S(1)}, f32[4,3,18,1,256]{4,2,3,1,0:T(8,128)S(1)}, u32[]{:S(2)}, u32[]{:S(2)}) collective-permute-start(f32[4,3,18,1,256]{4,2,3,1,0:T(8,128)S(1)} %copy.68), channel_id=1, source_target_pairs={{0,1},{1,2},{2,3},{4,5},{5,6},{6,7},{8,9},{9,10},{10,11},{12,13},{... | collective-permute-start | bytes 663560 | tf_op jit(solution)/shard_map/ppermute | solution.py:14
  30.4 7.9 %collective-permute-start.4 = (f32[4,1,32,256]{3,2,1,0:T(8,128)S(1)}, f32[4,1,32,256]{3,2,1,0:T(8,128)S(1)}, u32[]{:S(2)}, u32[]{:S(2)}) collective-permute-start(f32[4,1,32,256]{3,2,1,0:T(8,128)S(1)} %get-tuple-element.30), channel_id=1, source_target_pairs={{4,0},{8,4},{12,8},{16,12},{20,16},{24,20},{28,24},{32,28},{36,32}... | collective-permute-start | bytes 393224 | tf_op jit(solution)/shard_map/ppermute | solution.py:15
  32.3 7.2 %collective-permute-start.5 = (f32[4,1,32,256]{3,2,1,0:T(8,128)S(1)}, f32[4,1,32,256]{3,2,1,0:T(8,128)S(1)}, u32[]{:S(2)}, u32[]{:S(2)}) collective-permute-start(f32[4,1,32,256]{3,2,1,0:T(8,128)S(1)} %get-tuple-element.29), channel_id=1, source_target_pairs={{0,4},{4,8},{8,12},{12,16},{16,20},{20,24},{24,28},{28,32},{32,36}... | collective-permute-start | bytes 393224 | tf_op jit(solution)/shard_map/ppermute | solution.py:14
  39.6 6.1 %collective-permute-start.6 = (f32[4,18,1,256]{3,2,1,0:T(1,128)S(1)}, f32[4,18,1,256]{3,2,1,0:T(1,128)S(1)}, u32[]{:S(2)}, u32[]{:S(2)}) collective-permute-start(f32[4,18,1,256]{3,2,1,0:T(1,128)S(1)} %get-tuple-element.24), channel_id=1, source_target_pairs={{1,0},{2,1},{3,2},{5,4},{6,5},{7,6},{9,8},{10,9},{11,10},{13,12},{... | collective-permute-start | bytes 221192 | tf_op jit(solution)/shard_map/ppermute | solution.py:15
  40.9 6.1 %collective-permute-start.7 = (f32[4,18,1,256]{3,2,1,0:T(1,128)S(1)}, f32[4,18,1,256]{3,2,1,0:T(1,128)S(1)}, u32[]{:S(2)}, u32[]{:S(2)}) collective-permute-start(f32[4,18,1,256]{3,2,1,0:T(1,128)S(1)} %get-tuple-element.25), channel_id=1, source_target_pairs={{0,1},{1,2},{2,3},{4,5},{5,6},{6,7},{8,9},{9,10},{10,11},{12,13},{... | collective-permute-start | bytes 221192 | tf_op jit(solution)/shard_map/ppermute | solution.py:14
  47.0 26.8 %slice-start.2 = ((s8[6291456]{0:T(1024)(128)(4,1)}), s8[2097152]{0:T(1024)(128)(4,1)S(1)}, s32[]{:S(2)}) async-start(s8[6291456]{0:T(1024)(128)(4,1)} %bitcast.59), calls=%async_computation.3 | async-start | bytes 4194304
  48.9 1.3 copy-start.2
  50.2 13.5 %collective-permute-start.8 = (f32[4,1,32,256]{3,2,1,0:T(8,128)S(1)}, f32[4,1,32,256]{3,2,1,0:T(8,128)S(1)}, u32[]{:S(2)}, u32[]{:S(2)}) collective-permute-start(f32[4,1,32,256]{3,2,1,0:T(8,128)S(1)} %get-tuple-element.28), channel_id=1, source_target_pairs={{4,0},{8,4},{12,8},{16,12},{20,16},{24,20},{28,24},{32,28},{36,32}... | collective-permute-start | bytes 393224 | tf_op jit(solution)/shard_map/ppermute | solution.py:15
  52.1 11.5 %collective-permute-start.9 = (f32[4,1,32,256]{3,2,1,0:T(8,128)S(1)}, f32[4,1,32,256]{3,2,1,0:T(8,128)S(1)}, u32[]{:S(2)}, u32[]{:S(2)}) collective-permute-start(f32[4,1,32,256]{3,2,1,0:T(8,128)S(1)} %get-tuple-element.27), channel_id=1, source_target_pairs={{0,4},{4,8},{8,12},{12,16},{16,20},{20,24},{24,28},{28,32},{32,36}... | collective-permute-start | bytes 393224 | tf_op jit(solution)/shard_map/ppermute | solution.py:14
  57.6 6.0 %copy-start.3 = (f32[4,16,32,256]{3,2,1,0:T(8,128)S(1)}, f32[4,16,32,256]{3,2,1,0:T(8,128)}, u32[]{:S(2)}) copy-start(f32[4,16,32,256]{3,2,1,0:T(8,128)} %copy-done.2) | copy-start | bytes 6291460
  57.6 16.2 %slice-start.3 = ((s8[6291456]{0:T(1024)(128)(4,1)}), s8[4194304]{0:T(1024)(128)(4,1)S(1)}, s32[]{:S(2)}) async-start(s8[6291456]{0:T(1024)(128)(4,1)} %bitcast.59), calls=%async_computation.4 | async-start | bytes 8388608
  63.8 6.1 %collective-permute-start.10 = (f32[4,18,1,256]{3,2,1,0:T(1,128)S(1)}, f32[4,18,1,256]{3,2,1,0:T(1,128)S(1)}, u32[]{:S(2)}, u32[]{:S(2)}) collective-permute-start(f32[4,18,1,256]{3,2,1,0:T(1,128)S(1)} %get-tuple-element.22), channel_id=1, source_target_pairs={{1,0},{2,1},{3,2},{5,4},{6,5},{7,6},{9,8},{10,9},{11,10},{13,12},{... | collective-permute-start | bytes 221192 | tf_op jit(solution)/shard_map/ppermute | solution.py:15
  65.1 6.0 %collective-permute-start.11 = (f32[4,18,1,256]{3,2,1,0:T(1,128)S(1)}, f32[4,18,1,256]{3,2,1,0:T(1,128)S(1)}, u32[]{:S(2)}, u32[]{:S(2)}) collective-permute-start(f32[4,18,1,256]{3,2,1,0:T(1,128)S(1)} %get-tuple-element.23), channel_id=1, source_target_pairs={{0,1},{1,2},{2,3},{4,5},{5,6},{6,7},{8,9},{9,10},{10,11},{12,13},{... | collective-permute-start | bytes 221192 | tf_op jit(solution)/shard_map/ppermute | solution.py:14
  86.6 32.4 %all-to-all-start = ((f32[4,3,32,1024]{3,0,1,2:T(4,128)}), f32[4,3,32,1024]{3,0,1,2:T(4,128)S(1)}, u32[]{:S(2)}, u32[]{:S(2)}) async-start(f32[4,3,32,1024]{3,0,1,2:T(4,128)} %select_bitcast_fusion), calls=%async_computation | async-start | bytes 3145728 | tf_op jit(solution)/shard_map/all_to_all | solution.py:92
  218.5 16.6 %copy-start.1 = (s32[32,32]{1,0:T(8,128)S(1)}, s32[32,32]{1,0:T(8,128)}, u32[]{:S(2)}) copy-start(s32[32,32]{1,0:T(8,128)} %param.6) | copy-start | bytes 12292
where the time goes:
time: 236 us; the launch traced here: 235 us
  blocking collectives  66.9 us (28%)
  starting transfers between devices  48.6 us (21%)
  local copies, waits for them, and re-layouts  41.7 us (18%)
  matrix products  32.8 us (14%)
  waiting for transfers between devices  25.1 us (11%)
  other arithmetic  19 us (8%)
    psum x1, blocking collectives, per_device(): lax.psum(jnp.dot(stacked, stacked.T, precision=lax.Precision.HIGHEST), ('...  66.9 us
    ppermute x6, starting transfers between devices, padded_2(): before = lax.ppermute(last, axis, up)  28.6 us
    another operation x1, matrix products, per_device(): jax.scipy.linalg.solve_triangular(lower_factor, stacked, lower=True)  16.6 us
    all_to_all x1, waiting for transfers between devices, per_device(): lax.all_to_all(outgoing, 'brick', split_axis=2, concat_axis=2, tiled=True)  16.2 us
    unnamed x22, local copies, waits for them, and re-layouts  14 us
    dot_general x1, matrix products, per_device(): jnp.dot(stacked, stacked.T, precision=lax.Precision.HIGHEST)  13.3 us
    another operation x1, local copies, waits for them, and re-layouts, per_device(): jax.scipy.linalg.solve_triangular(lower_factor, stacked, lower=True)  10.4 us
    all_to_all x1, starting transfers between devices, per_device(): lax.all_to_all(outgoing, 'brick', split_axis=2, concat_axis=2, tiled=True)  10.3 us
  transfers between devices with their start and end apart: 13, of which 7 were waited for; matrix products, arithmetic and copies ran while one was open for 9% of the time, Pallas kernels for 0%

commit v1 on v0

--- a/solution.py
+++ b/solution.py
@@ -1,7 +1,142 @@
+import functools
 import jax
 import jax.numpy as jnp
 from jax import lax
+from jax.experimental import pallas as pl
+from jax.experimental.pallas import tpu as pltpu
 from jax.sharding import PartitionSpec as P
+
+LANES = 128
+PACK = 24
+PARTS = 2
+WIDTH = 8192
+
+
+def split_rows(block, parts):
+    pieces = []
+    rest = block
+    for step in range(parts):
+        piece = rest.astype(jnp.bfloat16)
+        pieces.append(piece)
+        if step < parts - 1:
+            rest = rest - piece.astype(jnp.float32)
+    return jnp.concatenate(pieces, axis=0)
+
+
+def sample_rows(arrived_ref):
+    pieces = []
+    for b in range(arrived_ref.shape[0]):
+        for jj in range(8):
+            pieces.append(arrived_ref[b, 0, 4 * jj : 4 * jj + 4, :])
+    return jnp.concatenate(pieces, axis=1)
+
+
+def stacked_block(basis_ref, arrived_ref):
+    rows = sample_rows(arrived_ref)
+    return jnp.concatenate([basis_ref[0], rows, jnp.zeros_like(rows)], axis=0)
+
+
+def gram_kernel(parts, scale, basis_ref, arrived_ref, out_ref, total_ref):
+    step = pl.program_id(0) * pl.num_programs(1) + pl.program_id(1)
+
+    @pl.when(step == 0)
+    def _():
+        total_ref[...] = jnp.zeros_like(total_ref)
+
+    pieces = split_rows(stacked_block(basis_ref, arrived_ref), parts)
+    total_ref[...] += lax.dot_general(
+        pieces, pieces, (((1,), (1,)), ((), ())), preferred_element_type=jnp.float32
+    )
+
+    @pl.when(step == pl.num_programs(0) * pl.num_programs(1) - 1)
+    def _():
+        total = total_ref[...]
+        rows = sum(total[PACK * p : PACK * (p + 1)] for p in range(parts))
+        gram = sum(rows[:, PACK * p : PACK * (p + 1)] for p in range(parts)) * scale
+        gram = jnp.concatenate([gram, jnp.zeros((PACK, LANES - PACK), jnp.float32)], axis=1)
+        packed = gram[0:8]
+        packed = packed + pltpu.roll(gram[8:16], PACK, 1)
+        packed = packed + pltpu.roll(gram[16:24], 2 * PACK, 1)
+        out_ref[...] = jnp.broadcast_to(packed[None], out_ref.shape)
+
+
+def factor(gram, count):
+    row_at = lax.broadcasted_iota(jnp.int32, (PACK, LANES), 0)
+    lane_at = lax.broadcasted_iota(jnp.int32, (PACK, LANES), 1)
+    work = jnp.where(lane_at < PACK, gram, 0.0) + jnp.where(lane_at == row_at + 32, 1.0, 0.0)
+    for j in range(count):
+        pivot_row = work[j : j + 1]
+        pivot = pivot_row[:, j : j + 1]
+        ratio = work[:, j : j + 1] / pivot
+        ratio = jnp.where(row_at[:, :1] > j, ratio, 0.0)
+        work = work - ratio * pivot_row
+    diagonal = jnp.sum(jnp.where(lane_at == row_at, work, 0.0), axis=1, keepdims=True)
+    root = jnp.sqrt(jnp.where(row_at[:, :1] < count, diagonal, 1.0))
+    work = work / root
+    upper = jnp.where((lane_at >= row_at) & (lane_at < PACK), work, 0.0)
+    inverse = pltpu.roll(work, LANES - 32, 1)[:, :PACK]
+    return upper, inverse
+
+
+def apply_kernel(parts, count, basis_ref, arrived_ref, packed_ref, out_ref, core_ref, left_ref):
+    step = pl.program_id(0) * pl.num_programs(1) + pl.program_id(1)
+
+    @pl.when(step == 0)
+    def _():
+        packed = jnp.sum(packed_ref[...], axis=0)
+        gram = jnp.concatenate(
+            [packed, pltpu.roll(packed, LANES - PACK, 1), pltpu.roll(packed, LANES - 2 * PACK, 1)],
+            axis=0,
+        )
+        upper, inverse = factor(gram, count)
+        core_ref[...] = upper
+        left = split_rows(inverse, parts)
+        left_ref[...] = jnp.concatenate([left] * parts, axis=1)
+
+    pieces = split_rows(stacked_block(basis_ref, arrived_ref), parts)
+    product = jnp.dot(left_ref[...], pieces, preferred_element_type=jnp.float32)
+    result = sum(product[PACK * p : PACK * (p + 1)] for p in range(parts))
+    out_ref[0] = result[: out_ref.shape[1]]
+
+
+def tail(basis, arrived, parts, width, total_rows, devices):
+    comps, rank_count, rows = basis.shape
+    grid = (comps, rows // width)
+    basis_spec = pl.BlockSpec((1, rank_count, width), lambda c, n: (c, 0, n))
+    arrived_spec = pl.BlockSpec((width // 1024, 1, 32, LANES), lambda c, n: (n, c, 0, 0))
+    params = pltpu.CompilerParams(vmem_limit_bytes=48 * 1024 * 1024)
+    copies = pl.pallas_call(
+        functools.partial(gram_kernel, parts, 1.0 / total_rows),
+        grid=grid,
+        in_specs=[basis_spec, arrived_spec],
+        out_specs=pl.BlockSpec((devices, 8, LANES), lambda c, n: (0, 0, 0)),
+        out_shape=jax.ShapeDtypeStruct((devices, 8, LANES), jnp.float32),
+        scratch_shapes=[pltpu.VMEM((PACK * parts, PACK * parts), jnp.float32)],
+        compiler_params=params,
+        name="gram",
+    )(basis, arrived)
+    partial_sums = lax.all_to_all(copies, ("brick", "ana"), 0, 0, tiled=True)
+    count = rank_count + 4
+    return pl.pallas_call(
+        functools.partial(apply_kernel, parts, count),
+        grid=grid,
+        in_specs=[
+            basis_spec,
+            arrived_spec,
+            pl.BlockSpec((devices, 8, LANES), lambda c, n: (0, 0, 0)),
+        ],
+        out_specs=[
+            pl.BlockSpec((1, count, width), lambda c, n: (c, 0, n)),
+            pl.BlockSpec((PACK, LANES), lambda c, n: (0, 0)),
+        ],
+        out_shape=[
+            jax.ShapeDtypeStruct((comps, count, rows), jnp.float32),
+            jax.ShapeDtypeStruct((PACK, LANES), jnp.float32),
+        ],
+        scratch_shapes=[pltpu.VMEM((PACK * parts, PACK * parts), jnp.bfloat16)],
+        compiler_params=params,
+        name="apply",
+    )(basis, arrived, partial_sums)
 
 
 def padded_2(shard, sides, width):
@@ -87,18 +222,15 @@
     owner_row = lax.dynamic_index_in_dim(owner_table, lax.axis_index("brick"), 0, keepdims=False)
     send_order = jnp.argsort(owner_row)
     blocks = picked.reshape(snaps, 3, bricks, samples_dev // bricks)
-    basis_rows = weighted_basis.reshape(rank_count, 3 * samples_dev)
     outgoing = jnp.take(blocks, send_order, axis=2)
-    arrived = lax.all_to_all(outgoing, "brick", split_axis=2, concat_axis=2, tiled=True)
-    owned = arrived.reshape(snaps, 3 * samples_dev)
-    stacked = jnp.concatenate([basis_rows, owned], axis=0)
-    gram_matrix = lax.psum(
-        jnp.dot(stacked, stacked.T, precision=lax.Precision.HIGHEST), ("brick", "ana")
-    )
-    gram_matrix = gram_matrix / total_rows
-    lower_factor = jnp.linalg.cholesky(gram_matrix)
-    new_basis = jax.scipy.linalg.solve_triangular(lower_factor, stacked, lower=True)
-    return (new_basis.reshape(rank_count + snaps, 3, samples_dev), lower_factor.T)
+    outgoing = outgoing.reshape(snaps, 3, bricks, 8, LANES).transpose(2, 1, 3, 0, 4)
+    outgoing = outgoing.reshape(bricks, 3, 32, LANES)
+    arrived = lax.all_to_all(outgoing, "brick", split_axis=0, concat_axis=0, tiled=True)
+    basis = jnp.transpose(weighted_basis, (1, 0, 2))
+    devices = bricks * lax.axis_size("ana")
+    new_basis, core = tail(basis, arrived, PARTS, WIDTH, total_rows, devices)
+    count = rank_count + snaps
+    return (jnp.transpose(new_basis, (1, 0, 2)), core[:count, :count])
 
 
 def solution(mesh):

time: 236 us -> 169 us (0.72)
  matrix products: 32.8 us -> 2.9 us
  local copies, waits for them, and re-layouts: 41.7 us -> 16.9 us
  Pallas kernels: 0 us -> 22.8 us
  waiting for transfers between devices: 25.1 us -> 10.5 us
  blocking collectives: 66.9 us -> 56.6 us
  starting transfers between devices: 48.6 us -> 38.3 us
    psum x1 -> x0, blocking collectives: 66.9 us -> none  [per_device(): lax.psum(jnp.dot(stacked, stacked.T, precision=lax.Precision.HIGHEST), ('...]
    all_to_all x0 -> x2, blocking collectives: none -> 56.6 us  [the longest x1 35.2 us: per_device(): lax.all_to_all(outgoing, 'brick', split_axis=0, concat_axis=0, tiled=True)]
    pallas_call x0 -> x2, Pallas kernels: none -> 22.8 us  [the longest x1 13.6 us: tail(): pl.pallas_call(functools.partial(apply_kernel, parts, count), grid=grid,...]
    another operation x1 -> x0, matrix products: 16.6 us -> none  [per_device(): jax.scipy.linalg.solve_triangular(lower_factor, stacked, lower=True)]
    all_to_all x1 -> x0, waiting for transfers between devices: 16.2 us -> none  [per_device(): lax.all_to_all(outgoing, 'brick', split_axis=2, concat_axis=2, tiled=True)]
    dot_general x1 -> x0, matrix products: 13.3 us -> none  [per_device(): jnp.dot(stacked, stacked.T, precision=lax.Precision.HIGHEST)]
    another operation x1 -> x0, local copies, waits for them, and re-layouts: 10.4 us -> none  [per_device(): jax.scipy.linalg.solve_triangular(lower_factor, stacked, lower=True)]
    all_to_all x1 -> x0, starting transfers between devices: 10.3 us -> none  [per_device(): lax.all_to_all(outgoing, 'brick', split_axis=2, concat_axis=2, tiled=True)]
  transfers between devices with their start and end apart: 13 -> 12, of which waited for: 7 -> 8; matrix products, arithmetic and copies ran while one was open for 9% -> 6% of each run, Pallas kernels for 0% -> 0%
where the time goes in v1:
time: 169 us; the launch traced here: 168 us
  blocking collectives  56.6 us (33%)
  starting transfers between devices  38.3 us (23%)
  Pallas kernels  22.8 us (13%)
  other arithmetic  18.7 us (11%)
  local copies, waits for them, and re-layouts  16.9 us (10%)
  waiting for transfers between devices  10.5 us (6%)
  matrix products  2.9 us (2%)
    all_to_all x1, blocking collectives, per_device(): lax.all_to_all(outgoing, 'brick', split_axis=0, concat_axis=0, tiled=True)  35.2 us
    ppermute x6, starting transfers between devices, padded_2(): before = lax.ppermute(last, axis, up)  28.6 us
    all_to_all x1, blocking collectives, tail(): partial_sums = lax.all_to_all(copies, ('brick', 'ana'), 0, 0, tiled=True)  21.4 us
    pallas_call x1, Pallas kernels, tail(): pl.pallas_call(functools.partial(apply_kernel, parts, count), grid=grid,...  13.6 us
    ppermute x6, starting transfers between devices, padded_2(): after = lax.ppermute(first, axis, down)  9.77 us
    pallas_call x1, Pallas kernels, tail(): pl.pallas_call(functools.partial(gram_kernel, parts, 1.0 / total_rows), g...  9.25 us
    another operation x1, other arithmetic, pressure_gradient(): jnp.stack([0.5 * (padded[:, 2:, 1:-1] - padded[:, :-2, 1:-1]), 0.5 * (pad...  7.34 us
    ppermute x6, waiting for transfers between devices, padded_2(): before = lax.ppermute(last, axis, up)  6.53 us
  transfers between devices with their start and end apart: 12, of which 8 were waited for; matrix products, arithmetic and copies ran while one was open for 6% of the time, Pallas kernels for 0%

profile of v1, /device:TPU:1, one launch (start us, length us, event | category | flops | bytes accessed | tf_op | source)
XLA Modules:
  0.0 167.9 jit_solution(18410501804399251302)
XLA Ops:
  1.8 4.6 %collective-permute-start.1 = (f32[4,3,1,32,256]{4,3,2,0,1:T(8,128)S(1)}, f32[4,3,1,32,256]{4,3,2,0,1:T(8,128)S(1)}, u32[]{:S(2)}, u32[]{:S(2)}) collective-permute-start(f32[4,3,1,32,256]{4,3,2,0,1:T(8,128)S(1)} %get-tuple-element.13), channel_id=1, source_target_pairs={{0,4},{4,8},{8,12},{12,16},{16,20},{20,24},{24,28},{28,32},{32,36}... | collective-permute-start | bytes 1179656 | tf_op jit(solution)/shard_map/ppermute | solution.py:149
  6.4 1.9 %collective-permute-start = (f32[4,3,1,32,256]{4,3,2,0,1:T(8,128)S(1)}, f32[4,3,1,32,256]{4,3,2,0,1:T(8,128)S(1)}, u32[]{:S(2)}, u32[]{:S(2)}) collective-permute-start(f32[4,3,1,32,256]{4,3,2,0,1:T(8,128)S(1)} %get-tuple-element.12), channel_id=1, source_target_pairs={{4,0},{8,4},{12,8},{16,12},{20,16},{24,20},{28,24},{32,28},{36,32}... | collective-permute-start | bytes 1179656 | tf_op jit(solution)/shard_map/ppermute | solution.py:150
  8.9 1.9 %reduce.3 = s32[32768]{0:T(1024)S(1)} reduce(s32[1,1,32768]{2,1,0:T(1,128)} %param.5, s32[]{:T(128)} %broadcast.88), dimensions={0,1}, to_apply=%param.5.reduce_sub_computation.3 | reduce | bytes 262148 | tf_op args[1]
  11.5 1.6 sort.17
  13.1 4.5 %constant_dynamic-update-slice_fusion.1 = f32[4,3,18,32,256]{4,3,2,0,1:T(8,128)S(1)} fusion(f32[4,3,18,32,256]{4,3,2,0,1:T(8,128)S(1)} %constant_dynamic-update-slice_fusion.2, f32[4,3,16,32,256]{4,3,2,1,0:T(8,128)} %param.4), kind=kLoop, calls=%fused_computation.70 | loop fusion | bytes 12582912
  19.3 4.0 %collective-permute-start.3 = (f32[4,3,18,1,256]{4,2,3,1,0:T(8,128)S(1)}, f32[4,3,18,1,256]{4,2,3,1,0:T(8,128)S(1)}, u32[]{:S(2)}, u32[]{:S(2)}) collective-permute-start(f32[4,3,18,1,256]{4,2,3,1,0:T(8,128)S(1)} %copy.40), channel_id=1, source_target_pairs={{0,1},{1,2},{2,3},{4,5},{5,6},{6,7},{8,9},{9,10},{10,11},{12,13},{... | collective-permute-start | bytes 663560 | tf_op jit(solution)/shard_map/ppermute | solution.py:149
  23.6 3.0 %collective-permute-done.2 = f32[4,3,18,1,256]{4,2,3,1,0:T(8,128)S(1)} collective-permute-done((f32[4,3,18,1,256]{4,2,3,1,0:T(8,128)S(1)}, f32[4,3,18,1,256]{4,2,3,1,0:T(8,128)S(1)}, u32[]{:S(2)}, u32[]{:S(2)}) %collective-permute-start.2) | collective-permute-done | bytes 221216 | tf_op jit(solution)/shard_map/ppermute | solution.py:150
  26.8 1.6 collective-permute-done.3
  28.6 1.7 %broadcast_multiply_fusion = (f32[4,16,32,256]{3,2,1,0:T(8,128)S(1)}, f32[4,16,32,256]{3,2,1,0:T(8,128)S(1)}) fusion(f32[4,16,32,256]{3,2,1,0:T(8,128)S(1)} %slice_bitcast_fusion, f32[4,3,18,32,256]{4,3,2,0,1:T(8,128)S(1)} %constant_dynamic-update-slice_fusion, f32[4,3,18,1,256]{4,3,2,0,1:T(1,128)S(1)} %copy.41, f32[4,3,18,1,256]{4,3,2,0,1:T(1,128)S(1)} %copy.39, ...), kind=kLoop, calls=%fused_computation.56 | loop fusion | flops 6291456 | bytes 20889600 | tf_op jit(solution)/shard_map/div | solution.py:216
  30.4 1.9 %collective-permute-start.4 = (f32[4,1,32,256]{3,2,1,0:T(8,128)S(1)}, f32[4,1,32,256]{3,2,1,0:T(8,128)S(1)}, u32[]{:S(2)}, u32[]{:S(2)}) collective-permute-start(f32[4,1,32,256]{3,2,1,0:T(8,128)S(1)} %get-tuple-element.24), channel_id=1, source_target_pairs={{4,0},{8,4},{12,8},{16,12},{20,16},{24,20},{28,24},{32,28},{36,32}... | collective-permute-start | bytes 393224 | tf_op jit(solution)/shard_map/ppermute | solution.py:150
  32.3 5.2 %collective-permute-start.5 = (f32[4,1,32,256]{3,2,1,0:T(8,128)S(1)}, f32[4,1,32,256]{3,2,1,0:T(8,128)S(1)}, u32[]{:S(2)}, u32[]{:S(2)}) collective-permute-start(f32[4,1,32,256]{3,2,1,0:T(8,128)S(1)} %get-tuple-element.23), channel_id=1, source_target_pairs={{0,4},{4,8},{8,12},{12,16},{16,20},{20,24},{24,28},{28,32},{32,36}... | collective-permute-start | bytes 393224 | tf_op jit(solution)/shard_map/ppermute | solution.py:149
  40.9 4.7 %collective-permute-start.7 = (f32[4,18,1,256]{3,2,1,0:T(1,128)S(1)}, f32[4,18,1,256]{3,2,1,0:T(1,128)S(1)}, u32[]{:S(2)}, u32[]{:S(2)}) collective-permute-start(f32[4,18,1,256]{3,2,1,0:T(1,128)S(1)} %get-tuple-element.19), channel_id=1, source_target_pairs={{0,1},{1,2},{2,3},{4,5},{5,6},{6,7},{8,9},{9,10},{10,11},{12,13},{... | collective-permute-start | bytes 221192 | tf_op jit(solution)/shard_map/ppermute | solution.py:149
  47.0 1.8 %fusion.7 = f32[4,16,32,256]{3,2,1,0:T(8,128)S(1)} fusion(f32[4,16,32,256]{3,2,1,0:T(8,128)S(1)} %get-tuple-element.9, f32[4,16,32,256]{3,2,1,0:T(8,128)S(1)} %get-tuple-element.8, f32[4,18,1,256]{3,2,1,0:T(1,128)S(1)} %collective-permute-done.7, f32[4,1,32,256]{3,2,1,0:T(8,128)S(1)} %collective-permute-done.4, ...), kind=kLoop, calls=%fused_computation.16 | loop fusion | flops 7864320 | bytes 6701056 | tf_op jit(solution)/shard_map/div | solution.py:218
  50.2 2.1 %collective-permute-start.8 = (f32[4,1,32,256]{3,2,1,0:T(8,128)S(1)}, f32[4,1,32,256]{3,2,1,0:T(8,128)S(1)}, u32[]{:S(2)}, u32[]{:S(2)}) collective-permute-start(f32[4,1,32,256]{3,2,1,0:T(8,128)S(1)} %get-tuple-element.22), channel_id=1, source_target_pairs={{4,0},{8,4},{12,8},{16,12},{20,16},{24,20},{28,24},{32,28},{36,32}... | collective-permute-start | bytes 393224 | tf_op jit(solution)/shard_map/ppermute | solution.py:150
  52.3 5.2 %collective-permute-start.9 = (f32[4,1,32,256]{3,2,1,0:T(8,128)S(1)}, f32[4,1,32,256]{3,2,1,0:T(8,128)S(1)}, u32[]{:S(2)}, u32[]{:S(2)}) collective-permute-start(f32[4,1,32,256]{3,2,1,0:T(8,128)S(1)} %get-tuple-element.21), channel_id=1, source_target_pairs={{0,4},{4,8},{8,12},{12,16},{16,20},{20,24},{24,28},{28,32},{32,36}... | collective-permute-start | bytes 393224 | tf_op jit(solution)/shard_map/ppermute | solution.py:149
  62.0 4.8 %collective-permute-start.11 = (f32[4,18,1,256]{3,2,1,0:T(1,128)S(1)}, f32[4,18,1,256]{3,2,1,0:T(1,128)S(1)}, u32[]{:S(2)}, u32[]{:S(2)}) collective-permute-start(f32[4,18,1,256]{3,2,1,0:T(1,128)S(1)} %get-tuple-element.17), channel_id=1, source_target_pairs={{0,1},{1,2},{2,3},{4,5},{5,6},{6,7},{8,9},{9,10},{10,11},{12,13},{... | collective-permute-start | bytes 221192 | tf_op jit(solution)/shard_map/ppermute | solution.py:149
  68.1 7.3 %fusion.16 = (f32[4,1,16,32,256]{4,3,2,1,0:T(8,128)S(1)}, f32[4,1,16,32,256]{4,3,2,1,0:T(8,128)S(1)}, f32[4,1,16,32,256]{4,3,2,1,0:T(8,128)S(1)}) fusion(f32[4,16,32,256]{3,2,1,0:T(8,128)} %copy-done.2, f32[4,1,32,256]{3,2,1,0:T(8,128)S(1)} %collective-permute-done.9, f32[4,1,32,256]{3,2,1,0:T(8,128)S(1)} %collective-permute-done.8, ...), kind=kLoop, calls=%fused_computation.32 | loop fusion | flops 7340032 | bytes 8798208 | tf_op jit(solution)/shard_map/stack | solution.py:184
  77.9 2.9 %fusion.26 = f32[4,3,512,64]{3,2,1,0:T(8,128)S(1)} fusion(f32[4,3,512,256]{3,2,1,0:T(8,128)S(1)} %bitcast_select_fusion, s32[256]{0:T(256)S(1)} %and_select_fusion), kind=kOutput, calls=%fused_computation.67 | convolution fusion | flops 1207975936 | bytes 7865344 | tf_op jit(solution)/shard_map/scrd,dk->scrk/dot_general | solution.py:204
  80.8 1.8 %reshape_reshape.3 = f32[4,3,32,1024]{3,2,1,0:T(8,128)} reshape(f32[4,3,512,64]{3,2,1,0:T(8,128)S(1)} %fusion.26) | data formatting | bytes 3145728 | tf_op jit(solution)/shard_map/reshape;reshape | solution.py:224
  82.6 2.4 %copy.46 = f32[4,3,32,1024]{3,0,2,1:T(4,128)S(1)} copy(f32[4,3,32,1024]{3,2,1,0:T(8,128)} %reshape_reshape.3) | data formatting | bytes 3145728 | tf_op jit(solution)/shard_map/reshape;reshape | solution.py:224
  88.4 35.2 %all_to_all.10.arrived_ref = f32[32,3,32,128]{3,2,1,0:T(8,128)S(1)} all-to-all(f32[32,3,32,128]{3,2,1,0:T(8,128)S(1)} %bitcast.46), channel_id=1, replica_groups=mesh['brick'=32,'ana'=4] {'brick'}, dimensions={0} | all-to-all | bytes 3145728 | tf_op jit(solution)/shard_map/all_to_all | solution.py:228
  123.7 9.3 %gram.1 = f32[128,8,128]{2,1,0:T(8,128)S(1)} custom-call(f32[3,16,32768]{2,1,0:T(8,128)} %bitcast.44, f32[32,3,32,128]{3,2,1,0:T(8,128)S(1)} %all_to_all.10.arrived_ref), custom_call_target="tpu_custom_call" | custom-call | tf_op jit(solution)/shard_map/gram/pallas_call | solution.py:108
  132.9 21.4 %all_to_all.11.packed_ref = f32[128,8,128]{2,1,0:T(8,128)S(1)} all-to-all(f32[128,8,128]{2,1,0:T(8,128)S(1)} %gram.1), channel_id=1, replica_groups=mesh['brick'=32,'ana'=4] {'brick','ana'}, dimensions={0} | all-to-all | bytes 1048576 | tf_op jit(solution)/shard_map/all_to_all | solution.py:118
  154.3 13.6 %apply.1 = (f32[3,20,32768]{2,1,0:T(8,128)}, f32[24,128]{1,0:T(8,128)}) custom-call(f32[3,16,32768]{2,1,0:T(8,128)} %bitcast.45, f32[32,3,32,128]{3,2,1,0:T(8,128)S(1)} %all_to_all.10.arrived_ref, f32[128,8,128]{2,1,0:T(8,128)S(1)} %all_to_all.11.packed_ref), custom_call_target="tpu_custom_call" | custom-call | tf_op jit(solution)/shard_map/apply/pallas_call | solution.py:120
  (64 shorter events, 22.4 us)
Async XLA Ops:
  0.6 10.8 %copy-start = (s32[32,32]{1,0:T(8,128)S(1)}, s32[32,32]{1,0:T(8,128)}, u32[]{:S(2)}) copy-start(s32[32,32]{1,0:T(8,128)} %param.6) | copy-start | bytes 12292
  1.8 11.2 %collective-permute-start.1 = (f32[4,3,1,32,256]{4,3,2,0,1:T(8,128)S(1)}, f32[4,3,1,32,256]{4,3,2,0,1:T(8,128)S(1)}, u32[]{:S(2)}, u32[]{:S(2)}) collective-permute-start(f32[4,3,1,32,256]{4,3,2,0,1:T(8,128)S(1)} %get-tuple-element.13), channel_id=1, source_target_pairs={{0,4},{4,8},{8,12},{12,16},{16,20},{20,24},{24,28},{28,32},{32,36}... | collective-permute-start | bytes 1179656 | tf_op jit(solution)/shard_map/ppermute | solution.py:149
  6.4 11.2 %collective-permute-start = (f32[4,3,1,32,256]{4,3,2,0,1:T(8,128)S(1)}, f32[4,3,1,32,256]{4,3,2,0,1:T(8,128)S(1)}, u32[]{:S(2)}, u32[]{:S(2)}) collective-permute-start(f32[4,3,1,32,256]{4,3,2,0,1:T(8,128)S(1)} %get-tuple-element.12), channel_id=1, source_target_pairs={{4,0},{8,4},{12,8},{16,12},{20,16},{24,20},{28,24},{32,28},{36,32}... | collective-permute-start | bytes 1179656 | tf_op jit(solution)/shard_map/ppermute | solution.py:150
  13.1 10.3 %slice-start = ((s8[6291456]{0:T(1024)(128)(4,1)}), s8[4194304]{0:T(1024)(128)(4,1)S(1)}, s32[]{:S(2)}) async-start(s8[6291456]{0:T(1024)(128)(4,1)} %bitcast.40), calls=%async_computation.2 | async-start | bytes 8388608
  13.1 10.2 %slice-start.1 = ((s8[6291456]{0:T(1024)(128)(4,1)}), s8[2097152]{0:T(1024)(128)(4,1)S(1)}, s32[]{:S(2)}) async-start(s8[6291456]{0:T(1024)(128)(4,1)} %bitcast.40), calls=%async_computation.3 | async-start | bytes 4194304
  18.0 8.6 %collective-permute-start.2 = (f32[4,3,18,1,256]{4,2,3,1,0:T(8,128)S(1)}, f32[4,3,18,1,256]{4,2,3,1,0:T(8,128)S(1)}, u32[]{:S(2)}, u32[]{:S(2)}) collective-permute-start(f32[4,3,18,1,256]{4,2,3,1,0:T(8,128)S(1)} %copy.38), channel_id=1, source_target_pairs={{1,0},{2,1},{3,2},{5,4},{6,5},{7,6},{9,8},{10,9},{11,10},{13,12},{... | collective-permute-start | bytes 663560 | tf_op jit(solution)/shard_map/ppermute | solution.py:150
  19.3 9.1 %collective-permute-start.3 = (f32[4,3,18,1,256]{4,2,3,1,0:T(8,128)S(1)}, f32[4,3,18,1,256]{4,2,3,1,0:T(8,128)S(1)}, u32[]{:S(2)}, u32[]{:S(2)}) collective-permute-start(f32[4,3,18,1,256]{4,2,3,1,0:T(8,128)S(1)} %copy.40), channel_id=1, source_target_pairs={{0,1},{1,2},{2,3},{4,5},{5,6},{6,7},{8,9},{9,10},{10,11},{12,13},{... | collective-permute-start | bytes 663560 | tf_op jit(solution)/shard_map/ppermute | solution.py:149
  30.4 7.9 %collective-permute-start.4 = (f32[4,1,32,256]{3,2,1,0:T(8,128)S(1)}, f32[4,1,32,256]{3,2,1,0:T(8,128)S(1)}, u32[]{:S(2)}, u32[]{:S(2)}) collective-permute-start(f32[4,1,32,256]{3,2,1,0:T(8,128)S(1)} %get-tuple-element.24), channel_id=1, source_target_pairs={{4,0},{8,4},{12,8},{16,12},{20,16},{24,20},{28,24},{32,28},{36,32}... | collective-permute-start | bytes 393224 | tf_op jit(solution)/shard_map/ppermute | solution.py:150
  32.3 7.2 %collective-permute-start.5 = (f32[4,1,32,256]{3,2,1,0:T(8,128)S(1)}, f32[4,1,32,256]{3,2,1,0:T(8,128)S(1)}, u32[]{:S(2)}, u32[]{:S(2)}) collective-permute-start(f32[4,1,32,256]{3,2,1,0:T(8,128)S(1)} %get-tuple-element.23), channel_id=1, source_target_pairs={{0,4},{4,8},{8,12},{12,16},{16,20},{20,24},{24,28},{28,32},{32,36}... | collective-permute-start | bytes 393224 | tf_op jit(solution)/shard_map/ppermute | solution.py:149
  39.6 6.1 %collective-permute-start.6 = (f32[4,18,1,256]{3,2,1,0:T(1,128)S(1)}, f32[4,18,1,256]{3,2,1,0:T(1,128)S(1)}, u32[]{:S(2)}, u32[]{:S(2)}) collective-permute-start(f32[4,18,1,256]{3,2,1,0:T(1,128)S(1)} %get-tuple-element.18), channel_id=1, source_target_pairs={{1,0},{2,1},{3,2},{5,4},{6,5},{7,6},{9,8},{10,9},{11,10},{13,12},{... | collective-permute-start | bytes 221192 | tf_op jit(solution)/shard_map/ppermute | solution.py:150
  40.9 6.1 %collective-permute-start.7 = (f32[4,18,1,256]{3,2,1,0:T(1,128)S(1)}, f32[4,18,1,256]{3,2,1,0:T(1,128)S(1)}, u32[]{:S(2)}, u32[]{:S(2)}) collective-permute-start(f32[4,18,1,256]{3,2,1,0:T(1,128)S(1)} %get-tuple-element.19), channel_id=1, source_target_pairs={{0,1},{1,2},{2,3},{4,5},{5,6},{6,7},{8,9},{9,10},{10,11},{12,13},{... | collective-permute-start | bytes 221192 | tf_op jit(solution)/shard_map/ppermute | solution.py:149
  48.9 1.3 copy-start.2
  50.2 25.2 %slice-start.2 = ((s8[6291456]{0:T(1024)(128)(4,1)}), s8[2097152]{0:T(1024)(128)(4,1)S(1)}, s32[]{:S(2)}) async-start(s8[6291456]{0:T(1024)(128)(4,1)} %bitcast.42), calls=%async_computation.4 | async-start | bytes 4194304
  50.2 8.0 %collective-permute-start.8 = (f32[4,1,32,256]{3,2,1,0:T(8,128)S(1)}, f32[4,1,32,256]{3,2,1,0:T(8,128)S(1)}, u32[]{:S(2)}, u32[]{:S(2)}) collective-permute-start(f32[4,1,32,256]{3,2,1,0:T(8,128)S(1)} %get-tuple-element.22), channel_id=1, source_target_pairs={{4,0},{8,4},{12,8},{16,12},{20,16},{24,20},{28,24},{32,28},{36,32}... | collective-permute-start | bytes 393224 | tf_op jit(solution)/shard_map/ppermute | solution.py:150
  52.3 7.1 %collective-permute-start.9 = (f32[4,1,32,256]{3,2,1,0:T(8,128)S(1)}, f32[4,1,32,256]{3,2,1,0:T(8,128)S(1)}, u32[]{:S(2)}, u32[]{:S(2)}) collective-permute-start(f32[4,1,32,256]{3,2,1,0:T(8,128)S(1)} %get-tuple-element.21), channel_id=1, source_target_pairs={{0,4},{4,8},{8,12},{12,16},{16,20},{20,24},{24,28},{28,32},{32,36}... | collective-permute-start | bytes 393224 | tf_op jit(solution)/shard_map/ppermute | solution.py:149
  60.7 6.1 %collective-permute-start.10 = (f32[4,18,1,256]{3,2,1,0:T(1,128)S(1)}, f32[4,18,1,256]{3,2,1,0:T(1,128)S(1)}, u32[]{:S(2)}, u32[]{:S(2)}) collective-permute-start(f32[4,18,1,256]{3,2,1,0:T(1,128)S(1)} %get-tuple-element.16), channel_id=1, source_target_pairs={{1,0},{2,1},{3,2},{5,4},{6,5},{7,6},{9,8},{10,9},{11,10},{13,12},{... | collective-permute-start | bytes 221192 | tf_op jit(solution)/shard_map/ppermute | solution.py:150
  62.0 6.0 %collective-permute-start.11 = (f32[4,18,1,256]{3,2,1,0:T(1,128)S(1)}, f32[4,18,1,256]{3,2,1,0:T(1,128)S(1)}, u32[]{:S(2)}, u32[]{:S(2)}) collective-permute-start(f32[4,18,1,256]{3,2,1,0:T(1,128)S(1)} %get-tuple-element.17), channel_id=1, source_target_pairs={{0,1},{1,2},{2,3},{4,5},{5,6},{6,7},{8,9},{9,10},{10,11},{12,13},{... | collective-permute-start | bytes 221192 | tf_op jit(solution)/shard_map/ppermute | solution.py:149
  66.9 8.6 %slice-start.3 = ((s8[6291456]{0:T(1024)(128)(4,1)}), s8[4194304]{0:T(1024)(128)(4,1)S(1)}, s32[]{:S(2)}) async-start(s8[6291456]{0:T(1024)(128)(4,1)} %bitcast.42), calls=%async_computation.5 | async-start | bytes 8388608
  154.3 13.6 %copy-start.1 = (s32[32,32]{1,0:T(8,128)S(1)}, s32[32,32]{1,0:T(8,128)}, u32[]{:S(2)}) copy-start(s32[32,32]{1,0:T(8,128)} %param.6) | copy-start | bytes 12292

commit v2 on v1

--- a/solution.py
+++ b/solution.py
@@ -9,6 +9,7 @@
 LANES = 128
 PACK = 24
 PARTS = 2
+POOL_PARTS = 2
 WIDTH = 8192
 
 
@@ -139,95 +140,324 @@
     )(basis, arrived, partial_sums)
 
 
-def padded_2(shard, sides, width):
-    for axis, dim in sides:
-        devices, length = (lax.axis_size(axis), shard.shape[dim])
-        up = [(i, (i + 1) % devices) for i in range(devices - 1)]
-        down = [(j, i) for i, j in up]
-        last = lax.slice_in_dim(shard, length - width, length, axis=dim)
-        first = lax.slice_in_dim(shard, 0, width, axis=dim)
-        before = lax.ppermute(last, axis, up)
-        after = lax.ppermute(first, axis, down)
-        shard = jnp.concatenate([before, shard, after], axis=dim)
-    return shard
-
-
-def depth_difference(grid_field):
-    padded = jnp.pad(grid_field, [(0, 0)] * (grid_field.ndim - 1) + [(1, 1)])
-    return 0.5 * (padded[..., 2:] - padded[..., :-2])
-
-
-def depth_neighbours(grid_field):
-    padded = jnp.pad(grid_field, [(0, 0)] * (grid_field.ndim - 1) + [(1, 1)])
-    return padded[..., 2:] + padded[..., :-2]
-
-
-def divergence(padded):
-    return (
-        0.5 * (padded[:, 0, 2:, 1:-1] - padded[:, 0, :-2, 1:-1])
-        + 0.5 * (padded[:, 1, 1:-1, 2:] - padded[:, 1, 1:-1, :-2])
-        + depth_difference(padded[:, 2, 1:-1, 1:-1])
+ANA_ROWS = 56
+BRICK_ROWS = 104
+
+
+def depth_pair(field):
+    lanes = field.shape[-1]
+    lane_at = lax.broadcasted_iota(jnp.int32, field.shape, field.ndim - 1)
+    after = jnp.where(lane_at == lanes - 1, 0.0, pltpu.roll(field, lanes - 1, field.ndim - 1))
+    before = jnp.where(lane_at == 0, 0.0, pltpu.roll(field, 1, field.ndim - 1))
+    return after, before
+
+
+def row_pair(field, after_row, before_row):
+    rows = field.shape[0]
+    row_at = lax.broadcasted_iota(jnp.int32, field.shape, 0)
+    after = jnp.where(row_at == rows - 1, after_row, pltpu.roll(field, rows - 1, 0))
+    before = jnp.where(row_at == 0, before_row, pltpu.roll(field, 1, 0))
+    return after, before
+
+
+def difference(pair):
+    return pair[0] - pair[1]
+
+
+def ana_edge_kernel(low_ref, high_ref, to_low_ref, to_high_ref):
+    snaps = to_low_ref.shape[0]
+    comps, layers, rows, lanes = low_ref.shape
+    flat = (comps * layers * rows, lanes)
+    low, high = low_ref.reshape(*flat), high_ref.reshape(*flat)
+
+    def column(ref, s, c, j):
+        start = (s * 3 + c) * layers * rows + j
+        return jnp.concatenate(
+            [ref[pl.ds(start + 8 * half, layers, stride=rows), :] for half in range(2)], axis=1
+        )
+
+    zero_row = jnp.zeros((1, 2 * lanes), jnp.float32)
+    for s in range(snaps):
+        for ref, out_ref, edge, second, third, sign in (
+            (low, to_low_ref, 0, 1, 2, 1.0),
+            (high, to_high_ref, 7, 6, 5, -1.0),
+        ):
+            speed = [column(ref, s, 0, j) for j in (edge, second)]
+            cross = [column(ref, s, 1, j) for j in (edge, second, third)]
+            deep = [column(ref, s, 2, j) for j in (edge, second)]
+            beside = (sign * cross[1], sign * (cross[2] - cross[0]))
+            out_ref[s, 0:16, :] = cross[0]
+            for n in range(2):
+                along = difference(row_pair(speed[n], zero_row, zero_row))
+                out_ref[s, 16 + 16 * n : 32 + 16 * n, :] = -0.5 * (
+                    along + beside[n] + difference(depth_pair(deep[n]))
+                )
+            out_ref[s, 48:56, :] = jnp.concatenate(
+                [speed[0][0:1], speed[1][0:1], speed[0][15:16], speed[1][15:16]] + [zero_row] * 4,
+                axis=0,
+            )
+
+
+def brick_edge_kernel(bounds_ref, first_ref, last_ref, from_low_ref, from_high_ref, to_low_ref, to_high_ref):
+    keep_low, keep_high = bounds_ref[2] > 0, bounds_ref[3] > 0
+    for s in range(to_low_ref.shape[0]):
+        for ref, out_ref, edge, second, third, sign, layer, pillar in (
+            (first_ref, to_low_ref, 0, 1, 2, 1.0, 0, 48),
+            (last_ref, to_high_ref, 3, 2, 1, -1.0, 15, 50),
+        ):
+            other = layer + 1 if layer == 0 else layer - 1
+
+            def halo(side_ref, keep, row):
+                return jnp.where(keep, side_ref[s, row : row + 1, :], 0.0)
+
+            def force(at, i, along):
+                cross = ref[3 * s + 1, at]
+                pair = row_pair(cross, halo(from_high_ref, keep_high, i), halo(from_low_ref, keep_low, i))
+                return -0.5 * (along + difference(pair) + difference(depth_pair(ref[3 * s + 2, at])))
+
+            speed = ref[3 * s, edge]
+            cross = ref[3 * s + 1, edge]
+            out_ref[s, 0:32, :] = force(second, other, sign * (ref[3 * s, third] - speed))
+            out_ref[s, 32:64, :] = force(edge, layer, sign * ref[3 * s, second])
+            out_ref[s, 64:96, :] = speed
+            below = jnp.where(keep_low, from_low_ref[s, 16 + layer : 17 + layer, :] - 0.5 * cross[0:1], 0.0)
+            above = jnp.where(keep_high, from_high_ref[s, 16 + layer : 17 + layer, :] + 0.5 * cross[31:32], 0.0)
+            out_ref[s, 96:104, :] = jnp.concatenate(
+                [
+                    halo(from_low_ref, keep_low, pillar + 1),
+                    halo(from_low_ref, keep_low, pillar),
+                    halo(from_high_ref, keep_high, pillar),
+                    halo(from_high_ref, keep_high, pillar + 1),
+                    below,
+                    above,
+                    jnp.zeros_like(below),
+                    jnp.zeros_like(below),
+                ],
+                axis=0,
+            )
+
+
+def project_kernel(
+    parts, bounds_ref, owner_ref, velocity_ref, weight_ref, pool_ref,
+    low_ref, high_ref, before_ref, after_ref, out_ref,
+    force_ref, press_ref, side_force_ref, side_press_ref, split_ref, pooled_ref,
+):
+    s = pl.program_id(0)
+    layers = velocity_ref.shape[1]
+    keep_before, keep_after = bounds_ref[0] > 0, bounds_ref[1] > 0
+    keep_low, keep_high = bounds_ref[2] > 0, bounds_ref[3] > 0
+
+    def halo(ref, keep, start, size=1):
+        return jnp.where(keep, ref[0, start : start + size, :], 0.0)
+
+    for i in range(layers):
+        ahead = velocity_ref[0, i + 1] if i < layers - 1 else halo(after_ref, keep_after, 64, 32)
+        behind = velocity_ref[0, i - 1] if i > 0 else halo(before_ref, keep_before, 64, 32)
+        cross = row_pair(velocity_ref[1, i], halo(high_ref, keep_high, i), halo(low_ref, keep_low, i))
+        force_ref[i + 2] = -0.5 * (
+            (ahead - behind) + difference(cross) + difference(depth_pair(velocity_ref[2, i]))
+        )
+    force_ref[0] = halo(before_ref, keep_before, 0, 32)
+    force_ref[1] = jnp.where(keep_before, before_ref[0, 32:64, :] - 0.5 * velocity_ref[0, 0], 0.0)
+    force_ref[layers + 2] = jnp.where(
+        keep_after, after_ref[0, 32:64, :] + 0.5 * velocity_ref[0, layers - 1], 0.0
     )
-
-
-def neighbour_sum(padded):
-    return (
-        padded[:, 2:, 1:-1]
-        + padded[:, :-2, 1:-1]
-        + padded[:, 1:-1, 2:]
-        + padded[:, 1:-1, :-2]
-        + depth_neighbours(padded[:, 1:-1, 1:-1])
-    )
-
-
-def pressure_gradient(padded):
-    return jnp.stack(
-        [
-            0.5 * (padded[:, 2:, 1:-1] - padded[:, :-2, 1:-1]),
-            0.5 * (padded[:, 1:-1, 2:] - padded[:, 1:-1, :-2]),
-            depth_difference(padded[:, 1:-1, 1:-1]),
+    force_ref[layers + 3] = halo(after_ref, keep_after, 0, 32)
+
+    for side, ref, keep, pillar, far, near, corner, row, sign in (
+        (0, low_ref, keep_low, 48, 96, 97, 100, 0, -0.5),
+        (1, high_ref, keep_high, 48, 99, 98, 101, 31, 0.5),
+    ):
+        own_cross = jnp.concatenate([velocity_ref[1, i, row : row + 1, :] for i in range(layers)], axis=0)
+        own_force = jnp.concatenate([force_ref[i + 2, row : row + 1, :] for i in range(layers)], axis=0)
+        row_at = lax.broadcasted_iota(jnp.int32, own_force.shape, 0)
+
+        def ends(before_row, after_row):
+            first = 0.5 * halo(before_ref, keep_before, before_row)
+            last = -0.5 * halo(after_ref, keep_after, after_row)
+            return jnp.where(row_at == 0, first, 0.0) + jnp.where(row_at == layers - 1, last, 0.0)
+
+        edge = jnp.where(keep, ref[0, 16:32, :] + sign * own_cross + ends(near, near), 0.0)
+        beyond = jnp.where(keep, ref[0, 32:48, :] + ends(far, far), 0.0)
+        corner_before = jnp.where(
+            keep_before, halo(before_ref, keep, corner) - 0.5 * halo(ref, keep, pillar), 0.0
+        )
+        corner_after = jnp.where(
+            keep_after, halo(after_ref, keep, corner) + 0.5 * halo(ref, keep, pillar + 2), 0.0
+        )
+        around = sum(row_pair(edge, corner_after, corner_before)) + beyond + own_force
+        around = around + sum(depth_pair(edge))
+        press = (edge + around * (1.0 / 6.0)) * (1.0 / 6.0)
+        side_press_ref[side] = jnp.where(keep, press, 0.0)
+        side_force_ref[side, 8:24, :] = edge
+        side_force_ref[side, 7:8, :] = corner_before
+        side_force_ref[side, 24:25, :] = corner_after
+
+    for i in range(-1, layers + 1):
+        field = force_ref[i + 2]
+        beside = row_pair(field, side_force_ref[1, 8 + i : 9 + i, :], side_force_ref[0, 8 + i : 9 + i, :])
+        around = (force_ref[i + 3] + force_ref[i + 1]) + sum(beside) + sum(depth_pair(field))
+        press = (field + around * (1.0 / 6.0)) * (1.0 / 6.0)
+        if i == -1:
+            press = jnp.where(keep_before, press, 0.0)
+        if i == layers:
+            press = jnp.where(keep_after, press, 0.0)
+        press_ref[i + 1] = press
+
+    for i in range(layers):
+        press = press_ref[i + 1]
+        beside = row_pair(press, side_press_ref[1, i : i + 1, :], side_press_ref[0, i : i + 1, :])
+        gradient = (press_ref[i + 2] - press_ref[i], difference(beside), difference(depth_pair(press)))
+        weight = weight_ref[32 * i : 32 * i + 32, :]
+        for c in range(3):
+            kept = (velocity_ref[c, i] - 0.5 * gradient[c]) * weight
+            for p in range(parts):
+                piece = kept.astype(jnp.bfloat16)
+                split_ref[32 * i : 32 * i + 32, 256 * p : 256 * p + 256] = piece
+                if p < parts - 1:
+                    kept = kept - piece.astype(jnp.float32)
+            split = split_ref[32 * i : 32 * i + 32, :]
+            pooled = jnp.dot(split, pool_ref[...], preferred_element_type=jnp.float32)
+            pooled_ref[0, c, 32 * i : 32 * i + 32, :] = pooled[:, :LANES]
+            pooled_ref[1, c, 32 * i : 32 * i + 32, :] = pooled[:, LANES:]
+
+    flat = pooled_ref.reshape(2 * 3 * 32 * layers, LANES)
+    out_flat = out_ref.reshape(out_ref.shape[0] * 3 * 32, LANES)
+    for k in range(2 * layers):
+        owner = owner_ref[k]
+        for c in range(3):
+            start = c * 32 * layers + 16 * k
+            tile = flat[pl.ds(start, 8, stride=2), :] + flat[pl.ds(start + 3 * 32 * layers + 1, 8, stride=2), :]
+            out_flat[pl.ds((owner * 3 + c) * 32 + s, 8, stride=4), :] = tile
+
+
+def weight_kernel(index_ref, out_ref, wide_ref):
+    rows = index_ref.shape[0]
+    at = lax.broadcasted_iota(jnp.int32, (rows, LANES), 0) * LANES + lax.broadcasted_iota(jnp.int32, (rows, LANES), 1)
+    offset = (index_ref[...] - 4 * at).astype(jnp.float32).astype(jnp.bfloat16)
+    source = lax.broadcasted_iota(jnp.int32, (LANES, 512), 0)
+    target = lax.broadcasted_iota(jnp.int32, (LANES, 512), 1)
+    expand = jnp.where(target // 4 == source, 1.0, 0.0).astype(jnp.bfloat16)
+    wide = jnp.dot(offset, expand, preferred_element_type=jnp.float32)
+    lane_at = lax.broadcasted_iota(jnp.int32, wide.shape, 1)
+    hit = jnp.where(wide == (lane_at % 4).astype(jnp.float32), 1.0, 0.0)
+    for half in range(2):
+        for kt in range(2):
+            wide_ref[kt, pl.ds(half, rows, stride=2), :] = hit[:, 256 * half + 128 * kt : 256 * half + 128 * kt + 128]
+    for kt in range(2):
+        out_ref[:, 128 * kt : 128 * kt + 128] = wide_ref[kt]
+
+
+def pooling(parts):
+    source = lax.broadcasted_iota(jnp.int32, (256 * parts, 256), 0) % 256
+    target = lax.broadcasted_iota(jnp.int32, (256 * parts, 256), 1)
+    low = (target < 64) & (source // 4 == target)
+    high = (target >= 192) & (source // 4 == target - 192)
+    return jnp.where(low | high, 1.0, 0.0).astype(jnp.bfloat16)
+
+
+def ring(devices):
+    up = [(i, (i + 1) % devices) for i in range(devices)]
+    return up, [(j, i) for i, j in up]
+
+
+def exchange(to_before, to_after, axis):
+    up, down = ring(lax.axis_size(axis))
+    return lax.ppermute(to_after, axis, up), lax.ppermute(to_before, axis, down)
+
+
+def whole(shape):
+    return pl.BlockSpec(shape, lambda *_: (0,) * len(shape))
+
+
+def front(provisional, sample_index, owner_table):
+    snaps, comps, layers, columns, depth = provisional.shape
+    bricks, anas = lax.axis_size("brick"), lax.axis_size("ana")
+    b, a = lax.axis_index("brick"), lax.axis_index("ana")
+    bounds = jnp.stack([b, bricks - 1 - b, a, anas - 1 - a]).astype(jnp.int32)
+    owner = lax.dynamic_index_in_dim(owner_table, b, 0, keepdims=False)
+    params = pltpu.CompilerParams(vmem_limit_bytes=48 * 1024 * 1024)
+    smem = pl.BlockSpec(memory_space=pltpu.SMEM)
+    samples = layers * columns * depth // 4
+    fields = provisional.reshape(snaps * comps, layers, columns, depth)
+
+    tiles = fields.reshape(snaps * comps, layers, columns // 8, 8, 2, LANES)
+    tiles = tiles.transpose(0, 1, 2, 4, 3, 5).reshape(snaps * comps, layers, columns // 8, 16, LANES)
+    tile_spec = lambda at: pl.BlockSpec((snaps * comps, layers, None, 16, LANES), lambda n: (0, 0, at, 0, 0))
+    ana_shape = jax.ShapeDtypeStruct((snaps, ANA_ROWS, depth), jnp.float32)
+    to_low, to_high = pl.pallas_call(
+        ana_edge_kernel,
+        grid=(1,),
+        in_specs=[tile_spec(0), tile_spec(columns // 8 - 1)],
+        out_specs=[whole(ana_shape.shape)] * 2,
+        out_shape=[ana_shape] * 2,
+        compiler_params=params,
+        name="ana_edges",
+    )(tiles, tiles)
+    from_low, from_high = exchange(to_low, to_high, "ana")
+
+    weight = pl.pallas_call(
+        weight_kernel,
+        in_specs=[whole((samples // LANES, LANES))],
+        out_specs=whole((layers * columns, depth)),
+        out_shape=jax.ShapeDtypeStruct((layers * columns, depth), jnp.float32),
+        grid=(1,),
+        scratch_shapes=[pltpu.VMEM((2, layers * columns, LANES), jnp.float32)],
+        compiler_params=params,
+        name="weights",
+    )(sample_index.reshape(samples // LANES, LANES))
+
+    brick_shape = jax.ShapeDtypeStruct((snaps, BRICK_ROWS, depth), jnp.float32)
+    layer_spec = lambda at: pl.BlockSpec((snaps * comps, 4, columns, depth), lambda n: (0, at, 0, 0))
+    to_before, to_after = pl.pallas_call(
+        brick_edge_kernel,
+        grid=(1,),
+        in_specs=[smem, layer_spec(0), layer_spec(layers // 4 - 1), whole(ana_shape.shape), whole(ana_shape.shape)],
+        out_specs=[whole(brick_shape.shape)] * 2,
+        out_shape=[brick_shape] * 2,
+        compiler_params=params,
+        name="brick_edges",
+    )(bounds, fields, fields, from_low, from_high)
+    from_before, from_after = exchange(to_before, to_after, "brick")
+
+    one = lambda shape: pl.BlockSpec((1,) + shape[1:], lambda n: (n, 0, 0))
+    return pl.pallas_call(
+        functools.partial(project_kernel, POOL_PARTS),
+        grid=(snaps,),
+        in_specs=[
+            smem,
+            smem,
+            pl.BlockSpec((comps, layers, columns, depth), lambda n: (n, 0, 0, 0)),
+            whole((layers * columns, depth)),
+            whole((256 * POOL_PARTS, 256)),
+            one(ana_shape.shape),
+            one(ana_shape.shape),
+            one(brick_shape.shape),
+            one(brick_shape.shape),
         ],
-        axis=1,
-    )
-
-
-def select_samples(projected, chosen, samples_dev):
-    snaps = projected.shape[0]
-    depth = projected.shape[-1]
-    offset = chosen - 4 * jnp.arange(samples_dev, dtype=jnp.int32)
-    cell_mask = (offset[:, None] == jnp.arange(4, dtype=jnp.int32)[None, :]).reshape(-1, depth)
-    grid_rows = projected.reshape(snaps, 3, -1, depth)
-    kept = jnp.where(cell_mask[None, None], grid_rows, 0.0)
-    pooling = (jnp.arange(depth)[:, None] // 4 == jnp.arange(depth // 4)[None, :]).astype(
-        jnp.float32
-    )
-    picked = jnp.einsum("scrd,dk->scrk", kept, pooling, precision=lax.Precision.HIGHEST)
-    return picked.reshape(snaps, 3, samples_dev)
+        out_specs=whole((bricks, comps, 32, LANES)),
+        out_shape=jax.ShapeDtypeStruct((bricks, comps, 32, LANES), jnp.float32),
+        scratch_shapes=[
+            pltpu.VMEM((layers + 4, columns, depth), jnp.float32),
+            pltpu.VMEM((layers + 2, columns, depth), jnp.float32),
+            pltpu.VMEM((2, 32, depth), jnp.float32),
+            pltpu.VMEM((2, layers, depth), jnp.float32),
+            pltpu.VMEM((layers * columns, 256 * POOL_PARTS), jnp.bfloat16),
+            pltpu.VMEM((2, comps, layers * columns, LANES), jnp.float32),
+        ],
+        compiler_params=params,
+        name="project",
+    )(bounds, owner, fields, weight, pooling(POOL_PARTS), from_low, from_high, from_before, from_after)
 
 
 def per_device(provisional, sample_index, owner_table, weighted_basis):
     snaps = provisional.shape[0]
     rank_count = weighted_basis.shape[0]
-    samples_dev = sample_index.shape[2]
-    bricks = lax.axis_size("brick")
-    total_rows = 3.0 * samples_dev * bricks * lax.axis_size("ana")
-    padded = padded_2(provisional, (("brick", 2), ("ana", 3)), 1)
-    forcing = -divergence(padded)
-    first_sweep = forcing / 6.0
-    first_pad = padded_2(first_sweep, (("brick", 1), ("ana", 2)), 1)
-    pressure = (forcing + neighbour_sum(first_pad)) / 6.0
-    pressure_pad = padded_2(pressure, (("brick", 1), ("ana", 2)), 1)
-    projected = provisional - pressure_gradient(pressure_pad)
-    picked = select_samples(projected, sample_index[0, 0], samples_dev)
-    owner_row = lax.dynamic_index_in_dim(owner_table, lax.axis_index("brick"), 0, keepdims=False)
-    send_order = jnp.argsort(owner_row)
-    blocks = picked.reshape(snaps, 3, bricks, samples_dev // bricks)
-    outgoing = jnp.take(blocks, send_order, axis=2)
-    outgoing = outgoing.reshape(snaps, 3, bricks, 8, LANES).transpose(2, 1, 3, 0, 4)
-    outgoing = outgoing.reshape(bricks, 3, 32, LANES)
+    devices = lax.axis_size("brick") * lax.axis_size("ana")
+    total_rows = 3.0 * sample_index.shape[2] * devices
+    outgoing = front(provisional, sample_index, owner_table)
     arrived = lax.all_to_all(outgoing, "brick", split_axis=0, concat_axis=0, tiled=True)
     basis = jnp.transpose(weighted_basis, (1, 0, 2))
-    devices = bricks * lax.axis_size("ana")
     new_basis, core = tail(basis, arrived, PARTS, WIDTH, total_rows, devices)
     count = rank_count + snaps
     return (jnp.transpose(new_basis, (1, 0, 2)), core[:count, :count])

time: 169 us -> 111 us (0.66)
  starting transfers between devices: 38.3 us -> 6.58 us
  other arithmetic: 18.7 us -> 0.49 us
  local copies, waits for them, and re-layouts: 16.9 us -> 0.02 us
  Pallas kernels: 22.8 us -> 39.1 us
  blocking collectives: 56.6 us -> 51.4 us
  matrix products: 2.9 us -> 0 us
    ppermute x12 -> x4, starting transfers between devices: 38.3 us -> 6.58 us  [the longest x2 5.23 us: exchange(): lax.ppermute(to_after, axis, up)]
    pallas_call x0 -> x4, Pallas kernels: none -> 16.3 us  [the longest x1 11.5 us: front(): pl.pallas_call(functools.partial(project_kernel, POOL_PARTS), grid=(snaps...]
    another operation x1, other arithmetic: 7.34 us -> 0.08 us  [front(): bounds = jnp.stack([b, bricks - 1 - b, a, anas - 1 - a]).astype(jnp.int32)]
    unnamed x17 -> x4, local copies, waits for them, and re-layouts: 6.36 us -> 0.01 us
    another operation x2 -> x0, local copies, waits for them, and re-layouts: 4.22 us -> none  [per_device(): blocks = picked.reshape(snaps, 3, bricks, samples_dev // bricks)]
    div x2 -> x0, other arithmetic: 3.56 us -> none  [the longest x1 1.85 us: per_device(): pressure = (forcing + neighbour_sum(first_pad)) / 6.0]
    all_to_all x1, blocking collectives: 35.2 us -> 32 us  [per_device(): lax.all_to_all(outgoing, 'brick', split_axis=0, concat_axis=0, tiled=True)]
    dot_general x1 -> x0, matrix products: 2.9 us -> none  [select_samples(): jnp.einsum('scrd,dk->scrk', kept, pooling, precision=lax.Precision.HIGHEST)]
  transfers between devices with their start and end apart: 12 -> 4, of which waited for: 8 -> 3; matrix products, arithmetic and copies ran while one was open for 6% -> 0% of each run, Pallas kernels for 0% -> 0%
where the time goes in v2:
time: 111 us; the launch traced here: 110 us
  blocking collectives  51.4 us (46%)
  Pallas kernels  39.1 us (35%)
  waiting for transfers between devices  11.9 us (11%)
  starting transfers between devices  6.58 us (6%)
    all_to_all x1, blocking collectives, per_device(): lax.all_to_all(outgoing, 'brick', split_axis=0, concat_axis=0, tiled=True)  32 us
    all_to_all x1, blocking collectives, tail(): partial_sums = lax.all_to_all(copies, ('brick', 'ana'), 0, 0, tiled=True)  19.4 us
    pallas_call x1, Pallas kernels, tail(): pl.pallas_call(functools.partial(apply_kernel, parts, count), grid=grid,...  13.6 us
    pallas_call x1, Pallas kernels, front(): pl.pallas_call(functools.partial(project_kernel, POOL_PARTS), grid=(snaps...  11.5 us
    pallas_call x1, Pallas kernels, tail(): pl.pallas_call(functools.partial(gram_kernel, parts, 1.0 / total_rows), g...  9.26 us
    ppermute x2, waiting for transfers between devices, exchange(): lax.ppermute(to_after, axis, up)  9.09 us
    ppermute x2, starting transfers between devices, exchange(): lax.ppermute(to_after, axis, up)  5.23 us
    ppermute x2, waiting for transfers between devices, exchange(): lax.ppermute(to_before, axis, down)  2.78 us
  transfers between devices with their start and end apart: 4, of which 3 were waited for; matrix products, arithmetic and copies ran while one was open for 0% of the time, Pallas kernels for 0%

profile of v2, /device:TPU:1, one launch (start us, length us, event | category | flops | bytes accessed | tf_op | source)
XLA Modules:
  0.0 110.2 jit_solution(8031804723005564311)
XLA Ops:
  0.6 0.0 copy-start
  0.6 0.0 copy-start.1
  0.7 2.3 %ana_edges.1 = (f32[4,56,256]{2,1,0:T(8,128)S(1)}, f32[4,56,256]{2,1,0:T(8,128)S(1)}) custom-call(f32[12,16,4,16,128]{4,3,2,1,0:T(8,128)} %bitcast.17, f32[12,16,4,16,128]{4,3,2,1,0:T(8,128)} %bitcast.18), custom_call_target="tpu_custom_call" | custom-call | tf_op jit(solution)/shard_map/ana_edges/pallas_call | solution.py:388
  2.9 2.1 %collective-permute-start = (f32[4,56,256]{2,1,0:T(8,128)S(1)}, f32[4,56,256]{2,1,0:T(8,128)S(1)}, u32[]{:S(2)}, u32[]{:S(2)}) collective-permute-start(f32[4,56,256]{2,1,0:T(8,128)S(1)} %get-tuple-element.8), channel_id=1, source_target_pairs={{0,1},{1,2},{2,3},{3,0},{4,5},{5,6},{6,7},{7,4},{8,9},{9,10},{10,1... | collective-permute-start | bytes 688136 | tf_op jit(solution)/shard_map/ppermute | solution.py:366
  5.1 1.3 %collective-permute-start.1 = (f32[4,56,256]{2,1,0:T(8,128)S(1)}, f32[4,56,256]{2,1,0:T(8,128)S(1)}, u32[]{:S(2)}, u32[]{:S(2)}) collective-permute-start(f32[4,56,256]{2,1,0:T(8,128)S(1)} %get-tuple-element.9), channel_id=1, source_target_pairs={{1,0},{2,1},{3,2},{0,3},{5,4},{6,5},{7,6},{4,7},{9,8},{10,9},{11,1... | collective-permute-start | bytes 688136 | tf_op jit(solution)/shard_map/ppermute | solution.py:366
  6.4 0.1 pad_add_fusion.bounds_ref
  6.5 0.0 copy-done.1
  6.5 0.2 weights.1.weight_ref
  6.8 4.5 %collective-permute-done.from_low_ref.low_ref = f32[4,56,256]{2,1,0:T(8,128)S(1)} collective-permute-done((f32[4,56,256]{2,1,0:T(8,128)S(1)}, f32[4,56,256]{2,1,0:T(8,128)S(1)}, u32[]{:S(2)}, u32[]{:S(2)}) %collective-permute-start) | collective-permute-done | bytes 229408 | tf_op jit(solution)/shard_map/ppermute | solution.py:366
  11.2 0.0 collective-permute-done.1.from_high_ref.high_ref
  11.2 2.2 %brick_edges.1 = (f32[4,104,256]{2,1,0:T(8,128)S(1)}, f32[4,104,256]{2,1,0:T(8,128)S(1)}) custom-call(s32[4]{0:T(128)S(1)} %pad_add_fusion.bounds_ref, f32[12,16,32,256]{3,2,1,0:T(8,128)} %bitcast.19, f32[12,16,32,256]{3,2,1,0:T(8,128)} %bitcast.20, f32[4,56,256]{2,1,0:T(8,128)S(1)} %collective-permute-done.from_low_ref.low_ref, ...), custom_call_target="tpu_custom_call" | custom-call | tf_op jit(solution)/shard_map/brick_edges/pallas_call | solution.py:412
  13.4 3.1 %collective-permute-start.2 = (f32[4,104,256]{2,1,0:T(8,128)S(1)}, f32[4,104,256]{2,1,0:T(8,128)S(1)}, u32[]{:S(2)}, u32[]{:S(2)}) collective-permute-start(f32[4,104,256]{2,1,0:T(8,128)S(1)} %get-tuple-element.10), channel_id=1, source_target_pairs={{0,4},{4,8},{8,12},{12,16},{16,20},{20,24},{24,28},{28,32},{32,36}... | collective-permute-start | bytes 1277960 | tf_op jit(solution)/shard_map/ppermute | solution.py:366
  16.6 0.0 collective-permute-start.3
  16.6 0.0 copy-done
  16.6 0.4 select_convert_fusion.pool_ref
  17.0 4.6 %collective-permute-done.2.before_ref = f32[4,104,256]{2,1,0:T(8,128)S(1)} collective-permute-done((f32[4,104,256]{2,1,0:T(8,128)S(1)}, f32[4,104,256]{2,1,0:T(8,128)S(1)}, u32[]{:S(2)}, u32[]{:S(2)}) %collective-permute-start.2) | collective-permute-done | bytes 426016 | tf_op jit(solution)/shard_map/ppermute | solution.py:366
  21.6 2.8 %collective-permute-done.3.after_ref = f32[4,104,256]{2,1,0:T(8,128)S(1)} collective-permute-done((f32[4,104,256]{2,1,0:T(8,128)S(1)}, f32[4,104,256]{2,1,0:T(8,128)S(1)}, u32[]{:S(2)}, u32[]{:S(2)}) %collective-permute-start.3) | collective-permute-done | bytes 426016 | tf_op jit(solution)/shard_map/ppermute | solution.py:366
  24.4 11.5 %project.1 = f32[32,3,32,128]{3,2,1,0:T(8,128)S(1)} custom-call(s32[4]{0:T(128)S(1)} %pad_add_fusion.bounds_ref, s32[32]{0:T(128)S(1)} %dynamic-slice_bitcast_fusion.owner_ref, f32[12,16,32,256]{3,2,1,0:T(8,128)} %bitcast.21, f32[512,256]{1,0:T(8,128)S(1)} %weights.1.weight_ref, bf16[512,256]{1,0:T(8,128)(2,1)S(1)} %select_convert_fusion.pool_ref, ...), custom_call_target="tpu_custom_call" | custom-call | tf_op jit(solution)/shard_map/project/pallas_call | solution.py:424
  36.0 32.0 %all_to_all.10.arrived_ref = f32[32,3,32,128]{3,2,1,0:T(8,128)S(1)} all-to-all(f32[32,3,32,128]{3,2,1,0:T(8,128)S(1)} %project.1), channel_id=1, replica_groups=mesh['brick'=32,'ana'=4] {'brick'}, dimensions={0} | all-to-all | bytes 3145728 | tf_op jit(solution)/shard_map/all_to_all | solution.py:459
  68.0 9.3 %gram.1 = f32[128,8,128]{2,1,0:T(8,128)S(1)} custom-call(f32[3,16,32768]{2,1,0:T(8,128)} %bitcast.22, f32[32,3,32,128]{3,2,1,0:T(8,128)S(1)} %all_to_all.10.arrived_ref), custom_call_target="tpu_custom_call" | custom-call | tf_op jit(solution)/shard_map/gram/pallas_call | solution.py:109
  77.2 19.4 %all_to_all.11.packed_ref = f32[128,8,128]{2,1,0:T(8,128)S(1)} all-to-all(f32[128,8,128]{2,1,0:T(8,128)S(1)} %gram.1), channel_id=1, replica_groups=mesh['brick'=32,'ana'=4] {'brick','ana'}, dimensions={0} | all-to-all | bytes 1048576 | tf_op jit(solution)/shard_map/all_to_all | solution.py:119
  96.6 13.6 %apply.1 = (f32[3,20,32768]{2,1,0:T(8,128)}, f32[24,128]{1,0:T(8,128)}) custom-call(f32[3,16,32768]{2,1,0:T(8,128)} %bitcast.23, f32[32,3,32,128]{3,2,1,0:T(8,128)S(1)} %all_to_all.10.arrived_ref, f32[128,8,128]{2,1,0:T(8,128)S(1)} %all_to_all.11.packed_ref), custom_call_target="tpu_custom_call" | custom-call | tf_op jit(solution)/shard_map/apply/pallas_call | solution.py:121
  (5 shorter events, 0.0 us)
Async XLA Ops:
  0.6 15.9 %copy-start = (s32[32,32]{1,0:T(8,128)S(1)}, s32[32,32]{1,0:T(8,128)}, u32[]{:S(2)}) copy-start(s32[32,32]{1,0:T(8,128)} %param.6) | copy-start | bytes 12292
  0.6 5.8 %copy-start.1 = (s32[1,1,32768]{2,1,0:T(1,128)S(1)}, s32[1,1,32768]{2,1,0:T(1,128)}, u32[]{:S(2)}) copy-start(s32[1,1,32768]{2,1,0:T(1,128)} %param.5) | copy-start | bytes 393220
  2.9 8.3 %collective-permute-start = (f32[4,56,256]{2,1,0:T(8,128)S(1)}, f32[4,56,256]{2,1,0:T(8,128)S(1)}, u32[]{:S(2)}, u32[]{:S(2)}) collective-permute-start(f32[4,56,256]{2,1,0:T(8,128)S(1)} %get-tuple-element.8), channel_id=1, source_target_pairs={{0,1},{1,2},{2,3},{3,0},{4,5},{5,6},{6,7},{7,4},{8,9},{9,10},{10,1... | collective-permute-start | bytes 688136 | tf_op jit(solution)/shard_map/ppermute | solution.py:366
  5.1 6.2 %collective-permute-start.1 = (f32[4,56,256]{2,1,0:T(8,128)S(1)}, f32[4,56,256]{2,1,0:T(8,128)S(1)}, u32[]{:S(2)}, u32[]{:S(2)}) collective-permute-start(f32[4,56,256]{2,1,0:T(8,128)S(1)} %get-tuple-element.9), channel_id=1, source_target_pairs={{1,0},{2,1},{3,2},{0,3},{5,4},{6,5},{7,6},{4,7},{9,8},{10,9},{11,1... | collective-permute-start | bytes 688136 | tf_op jit(solution)/shard_map/ppermute | solution.py:366
  13.4 8.2 %collective-permute-start.2 = (f32[4,104,256]{2,1,0:T(8,128)S(1)}, f32[4,104,256]{2,1,0:T(8,128)S(1)}, u32[]{:S(2)}, u32[]{:S(2)}) collective-permute-start(f32[4,104,256]{2,1,0:T(8,128)S(1)} %get-tuple-element.10), channel_id=1, source_target_pairs={{0,4},{4,8},{8,12},{12,16},{16,20},{20,24},{24,28},{28,32},{32,36}... | collective-permute-start | bytes 1277960 | tf_op jit(solution)/shard_map/ppermute | solution.py:366
  16.6 7.8 %collective-permute-start.3 = (f32[4,104,256]{2,1,0:T(8,128)S(1)}, f32[4,104,256]{2,1,0:T(8,128)S(1)}, u32[]{:S(2)}, u32[]{:S(2)}) collective-permute-start(f32[4,104,256]{2,1,0:T(8,128)S(1)} %get-tuple-element.11), channel_id=1, source_target_pairs={{4,0},{8,4},{12,8},{16,12},{20,16},{24,20},{28,24},{32,28},{36,32}... | collective-permute-start | bytes 1277960 | tf_op jit(solution)/shard_map/ppermute | solution.py:366

commit v3 on v0

v3 whole, which is shorter than its diff:
```python
import functools
import jax
import jax.numpy as jnp
from jax import lax
from jax.experimental import pallas as pl
from jax.experimental.pallas import tpu as pltpu
from jax.sharding import PartitionSpec as P

LANES = 128
PACK = 24
POOL_PARTS = 2
WIDTH = 8192
SLOTS = 4
VMEM_LIMIT = 20 * 1024 * 1024


def split_pieces(block):
    high = block.astype(jnp.bfloat16)
    return high, (block - high.astype(jnp.float32)).astype(jnp.bfloat16)


def stacked_pieces(basis_ref, arrived_ref, c, start, width, order):
    rows = jnp.concatenate(
        [
            arrived_ref[b, c, 4 * jj : 4 * jj + 4, :]
            for b in range(start // 1024, (start + width) // 1024)
            for jj in range(8)
        ],
        axis=1,
    )
    small = split_pieces(rows)
    small = [small[p].astype(jnp.float32) for p in order] + [jnp.zeros_like(rows)] * (4 - len(order))
    small = jnp.concatenate(small, axis=0).astype(jnp.bfloat16)
    large = split_pieces(basis_ref[c, :, start : start + width])
    return jnp.concatenate([large[p] for p in order] + [small], axis=0)


def gram_kernel(width, scale, basis_ref, arrived_ref, out_ref):
    comps, rank_count, columns = basis_ref.shape
    parts = 2
    total = 0.0
    for c in range(comps):
        for start in range(0, columns, width):
            pieces = stacked_pieces(basis_ref, arrived_ref, c, start, width, (0, 1))
            total = total + lax.dot_general(
                pieces, pieces, (((1,), (1,)), ((), ())), preferred_element_type=jnp.float32
            )
    base = rank_count * parts
    rows = sum(total[rank_count * p : rank_count * (p + 1)] for p in range(parts))
    small = sum(total[base + 4 * p : base + 4 * (p + 1)] for p in range(parts))
    rows = jnp.concatenate([rows, small, jnp.zeros_like(small)], axis=0)
    left = sum(rows[:, rank_count * p : rank_count * (p + 1)] for p in range(parts))
    right = sum(rows[:, base + 4 * p : base + 4 * (p + 1)] for p in range(parts))
    rest = jnp.zeros((PACK, LANES - rank_count - 4), jnp.float32)
    gram = jnp.concatenate([left, right, rest], axis=1) * scale
    packed = gram[0:4]
    for n in range(1, 5):
        packed = packed + pltpu.roll(gram[4 * n : 4 * n + 4], n * PACK, 1)
    out_ref[...] = jnp.broadcast_to(packed[None], out_ref.shape)


def factor(tiles, count):
    row_at = [lax.broadcasted_iota(jnp.int32, (8, LANES), 0) + 8 * t for t in range(3)]
    lane_at = lax.broadcasted_iota(jnp.int32, (8, LANES), 1)
    work = [jnp.where(lane_at < PACK, tiles[t], 0.0) + jnp.where(lane_at == row_at[t] + 32, 1.0, 0.0) for t in range(3)]
    roots = []
    block = 4
    for j in range(0, count, block):
        t0, r0 = j // 8, j % 8
        rows = [jnp.broadcast_to(work[t0][r0 + q : r0 + q + 1], (8, LANES)) for q in range(block)]
        cols = [[jnp.broadcast_to(work[t][:, j + q : j + q + 1], (8, LANES)) for t in range(3)] for q in range(block)]
        pivots = [
            [jnp.broadcast_to(work[t0][r0 + q : r0 + q + 1, j + r : j + r + 1], (8, LANES)) for r in range(block)]
            for q in range(block)
        ]
        for q in range(block):
            inverse = 1.0 / pivots[q][q]
            roots.append(pivots[q][q])
            for r in range(q + 1, block):
                ratio = pivots[r][q] * inverse
                across = pivots[q][r] * inverse
                rows[r] = rows[r] - ratio * rows[q]
                for t in range(t0, 3):
                    cols[r][t] = cols[r][t] - cols[q][t] * across
                for u in range(q + 1, block):
                    pivots[r][u] = pivots[r][u] - ratio * pivots[q][u]
            for t in range(t0, 3):
                ratio = jnp.where(row_at[t] > j + q, cols[q][t] * inverse, 0.0)
                work[t] = work[t] - ratio * rows[q]
    for t in range(3):
        diagonal = jnp.ones((8, LANES), jnp.float32)
        for j in range(8 * t, min(count, 8 * t + 8)):
            diagonal = jnp.where(row_at[t] == j, roots[j], diagonal)
        work[t] = work[t] / jnp.sqrt(diagonal)
    upper = [jnp.where((lane_at >= row_at[t]) & (lane_at < PACK), work[t], 0.0) for t in range(3)]
    inverse = jnp.concatenate([pltpu.roll(work[t], LANES - 32, 1)[:, :PACK] for t in range(3)], axis=0)
    return upper, inverse


def apply_kernel(width, slots, basis_ref, arrived_ref, packed_ref, out_ref, core_ref, left_ref, slot_ref, sem):
    comps, rank_count, columns = basis_ref.shape
    count = out_ref.shape[1]
    packed = jnp.sum(packed_ref[...], axis=0)
    parts = [packed] + [pltpu.roll(packed, LANES - n * PACK, 1) for n in range(1, 5)] + [jnp.zeros_like(packed)]
    tiles = [jnp.concatenate(parts[2 * t : 2 * t + 2], axis=0) for t in range(3)]
    upper, inverse = factor(tiles, count)
    for t in range(3):
        core_ref[8 * t : 8 * t + 8, :] = upper[t]
    high, low = [piece.astype(jnp.float32) for piece in split_pieces(inverse)]
    order = (high, high, low)
    left = [piece[:, :rank_count] for piece in order] + [piece[:, rank_count:count] for piece in order]
    left.append(jnp.zeros((PACK, 16 - 4 * len(order)), jnp.float32))
    left_ref[...] = jnp.concatenate(left, axis=1).astype(jnp.bfloat16)

    blocks = [(c, start) for c in range(comps) for start in range(0, columns, width)]
    copies = []
    for n, (c, start) in enumerate(blocks):
        if n >= slots:
            copies[n - slots].wait()
        pieces = stacked_pieces(basis_ref, arrived_ref, c, start, width, (0, 1, 0))
        product = jnp.dot(left_ref[...], pieces, preferred_element_type=jnp.float32)
        slot = n % slots
        slot_ref[slot] = product[:count]
        copy = pltpu.make_async_copy(slot_ref.at[slot], out_ref.at[c, :, start : start + width], sem.at[slot])
        copy.start()
        copies.append(copy)
    for copy in copies[-slots:]:
        copy.wait()


def tail(basis, arrived, width, total_rows, devices):
    comps, rank_count, rows = basis.shape
    vmem = pl.BlockSpec(memory_space=pltpu.VMEM)
    copies = grid_kernel(
        functools.partial(gram_kernel, width, 1.0 / total_rows),
        "gram",
        (10**9, 10**7),
        in_specs=[vmem, vmem],
        out_specs=vmem,
        out_shape=jax.ShapeDtypeStruct((devices, 4, LANES), jnp.float32),
    )(basis, arrived)
    partial_sums = lax.all_to_all(copies, ("brick", "ana"), 0, 0, tiled=True)
    count = rank_count + 4
    return grid_kernel(
        functools.partial(apply_kernel, width, SLOTS),
        "apply",
        (10**9, 2 * 10**7),
        in_specs=[vmem] * 3,
        out_specs=[pl.BlockSpec(memory_space=pltpu.HBM), vmem],
        out_shape=[
            jax.ShapeDtypeStruct((comps, count, rows), jnp.float32),
            jax.ShapeDtypeStruct((PACK, LANES), jnp.float32),
        ],
        scratch_shapes=[
            pltpu.VMEM((PACK, rank_count * 3 + 16), jnp.bfloat16),
            pltpu.VMEM((SLOTS, count, width), jnp.float32),
            pltpu.SemaphoreType.DMA((SLOTS,)),
        ],
    )(basis, arrived, partial_sums)


ANA_ROWS = 56
BULK_ROWS = 96
FIX_ROWS = 16
MARGIN = 3


def depth_pair(field):
    lanes = field.shape[-1]
    lane_at = lax.broadcasted_iota(jnp.int32, field.shape, field.ndim - 1)
    after = jnp.where(lane_at == lanes - 1, 0.0, pltpu.roll(field, lanes - 1, field.ndim - 1))
    before = jnp.where(lane_at == 0, 0.0, pltpu.roll(field, 1, field.ndim - 1))
    return after, before


def row_pair(field, after_row, before_row):
    rows = field.shape[0]
    row_at = lax.broadcasted_iota(jnp.int32, field.shape, 0)
    after = jnp.where(row_at == rows - 1, after_row, pltpu.roll(field, rows - 1, 0))
    before = jnp.where(row_at == 0, before_row, pltpu.roll(field, 1, 0))
    return after, before


def inside(axis):
    at = lax.axis_index(axis)
    return at > 0, at < lax.axis_size(axis) - 1


def difference(pair):
    return pair[0] - pair[1]


def relaxed(field, around):
    return (field + around * (1.0 / 6.0)) * (1.0 / 6.0)


def ana_edge_kernel(tiles_ref, to_low_ref, to_high_ref, low_ref, high_ref, sem):
    snaps = to_low_ref.shape[0]
    fields, layers, rows, lanes = low_ref.shape
    last = tiles_ref.shape[2] - 1
    copies = [
        pltpu.make_async_copy(tiles_ref.at[:, :, at], ref, sem.at[n])
        for n, (at, ref) in enumerate(((0, low_ref), (last, high_ref)))
    ]
    for copy in copies:
        copy.start()
    flat = (fields * layers * rows, lanes)

    def column(ref, s, c, j):
        start = (s * 3 + c) * layers * rows + j
        return jnp.concatenate(
            [ref[pl.ds(start + 8 * half, layers, stride=rows), :] for half in range(2)], axis=1
        )

    zero_row = jnp.zeros((1, 2 * lanes), jnp.float32)
    for copy, side_ref, out_ref, edge, second, third, sign in (
        (copies[0], low_ref, to_low_ref, 0, 1, 2, 1.0),
        (copies[1], high_ref, to_high_ref, 7, 6, 5, -1.0),
    ):
        copy.wait()
        ref = side_ref.reshape(*flat)
        for s in range(snaps):
            speed = [column(ref, s, 0, j) for j in (edge, second)]
            cross = [column(ref, s, 1, j) for j in (edge, second, third)]
            deep = [column(ref, s, 2, j) for j in (edge, second)]
            beside = (sign * cross[1], sign * (cross[2] - cross[0]))
            out_ref[s, 0:16, :] = cross[0]
            for n in range(2):
                along = difference(row_pair(speed[n], zero_row, zero_row))
                out_ref[s, 16 + 16 * n : 32 + 16 * n, :] = -0.5 * (
                    along + beside[n] + difference(depth_pair(deep[n]))
                )
            out_ref[s, 48:56, :] = jnp.concatenate(
                [speed[0][0:1], speed[1][0:1], speed[0][15:16], speed[1][15:16]] + [zero_row] * 4,
                axis=0,
            )


def load_kernel(source_ref, _, along_ref, cross_ref, deep_ref, force_ref, to_low_ref, to_high_ref, sem):
    snaps, layers = force_ref.shape[:2]
    fields = (along_ref, cross_ref, deep_ref)
    copies = [
        pltpu.make_async_copy(source_ref.at[n], fields[n % 3].at[n // 3], sem.at[n]) for n in range(3 * snaps)
    ]
    for copy in copies:
        copy.start()
    for s in range(snaps):
        for copy in copies[3 * s : 3 * s + 3]:
            copy.wait()
        for i in range(layers):
            along = 0.0
            if i < layers - 1:
                along = along + along_ref[s, i + 1]
            if i > 0:
                along = along - along_ref[s, i - 1]
            cross = row_pair(cross_ref[s, i], 0.0, 0.0)
            force_ref[s, i] = -0.5 * (
                along + difference(cross) + difference(depth_pair(deep_ref[s, i]))
            )
        for out_ref, layer, second in ((to_low_ref, 0, 1), (to_high_ref, layers - 1, layers - 2)):
            out_ref[s, 0:32, :] = force_ref[s, second]
            out_ref[s, 32:64, :] = force_ref[s, layer]
            out_ref[s, 64:96, :] = along_ref[s, layer]


def fix_kernel(cross_ref, force_ref, from_low_ref, from_high_ref, to_low_ref, to_high_ref):
    layers = force_ref.shape[1]
    keep_low, keep_high = inside("ana")
    for s in range(to_low_ref.shape[0]):
        for out_ref, layer, second, pillar in ((to_low_ref, 0, 1, 48), (to_high_ref, layers - 1, layers - 2, 50)):

            def halo(side_ref, keep, row):
                return jnp.where(keep, side_ref[s, row : row + 1, :], 0.0)

            cross = cross_ref[s, layer]
            row = 16 + layer
            below = jnp.where(keep_low, from_low_ref[s, row : row + 1, :] - 0.5 * cross[0:1], 0.0)
            above = jnp.where(keep_high, from_high_ref[s, row : row + 1, :] + 0.5 * cross[31:32], 0.0)
            rows = [
                force_ref[s, layer, 0:1, :] + 0.5 * halo(from_low_ref, keep_low, layer),
                force_ref[s, layer, 31:32, :] - 0.5 * halo(from_high_ref, keep_high, layer),
                force_ref[s, second, 0:1, :] + 0.5 * halo(from_low_ref, keep_low, second),
                force_ref[s, second, 31:32, :] - 0.5 * halo(from_high_ref, keep_high, second),
                halo(from_low_ref, keep_low, pillar + 1),
                halo(from_low_ref, keep_low, pillar),
                halo(from_high_ref, keep_high, pillar),
                halo(from_high_ref, keep_high, pillar + 1),
                below,
                above,
            ]
            rows = rows + [jnp.zeros_like(below)] * (FIX_ROWS - len(rows))
            out_ref[s] = jnp.concatenate(rows, axis=0)


def sample_layers(s, parts, layers, fields, owner, weight_ref, pool_ref, out_ref, split_ref, pooled_ref, press, beside):
    count = len(layers)
    for n, i in enumerate(layers):
        centre = press(i)
        after_row, before_row = beside(i)
        gradient = (
            press(i + 1) - press(i - 1),
            difference(row_pair(centre, after_row, before_row)),
            difference(depth_pair(centre)),
        )
        weight = weight_ref[32 * i : 32 * i + 32, :]
        for c in range(3):
            kept = (fields[c][s, i] - 0.5 * gradient[c]) * weight
            row = 32 * (c * count + n)
            for p in range(parts):
                piece = kept.astype(jnp.bfloat16)
                split_ref[row : row + 32, 256 * p : 256 * p + 256] = piece
                if p < parts - 1:
                    kept = kept - piece.astype(jnp.float32)
    pooled = jnp.dot(split_ref[...], pool_ref[...], preferred_element_type=jnp.float32)
    pooled_ref[0] = pooled[:, :LANES]
    pooled_ref[1] = pooled[:, LANES:]
    rows = 3 * count * 32
    flat = pooled_ref.reshape(2 * rows, LANES)
    out_flat = out_ref.reshape(out_ref.shape[0] * 3 * 32, LANES)
    for n, i in enumerate(layers):
        for half in range(2):
            place = owner(2 * i + half)
            for c in range(3):
                start = 32 * (c * count + n) + 16 * half
                tile = flat[pl.ds(start, 8, stride=2), :] + flat[pl.ds(start + rows + 1, 8, stride=2), :]
                out_flat[pl.ds((place * 3 + c) * 32 + s, 8, stride=4), :] = tile


def inner_kernel(
    parts, owner_ref, along_ref, cross_ref, deep_ref, own_force_ref, weight_ref, pool_ref, low_ref, high_ref,
    force_ref, press_ref, out_ref, side_ref, split_ref, pooled_ref,
):
    layers = along_ref.shape[1]
    keep_low, keep_high = inside("ana")
    brick = lax.axis_index("brick")

    def snapshot(s, carry):
        def halo(ref, keep, start, size=1):
            return jnp.where(keep, ref[s, start : start + size, :], 0.0)

        row_at = lax.broadcasted_iota(jnp.int32, (8, along_ref.shape[3]), 0)
        for i in range(layers):
            first, last = own_force_ref[s, i, 0:8, :], own_force_ref[s, i, 24:32, :]
            force_ref[s, i, 0:8, :] = jnp.where(row_at == 0, first + 0.5 * halo(low_ref, keep_low, i), first)
            force_ref[s, i, 8:24, :] = own_force_ref[s, i, 8:24, :]
            force_ref[s, i, 24:32, :] = jnp.where(row_at == 7, last - 0.5 * halo(high_ref, keep_high, i), last)

        for side, ref, keep, row, sign in ((0, low_ref, keep_low, 0, -0.5), (1, high_ref, keep_high, 31, 0.5)):
            own_cross = jnp.concatenate([cross_ref[s, i, row : row + 1, :] for i in range(layers)], axis=0)
            own_force = jnp.concatenate([force_ref[s, i, row : row + 1, :] for i in range(layers)], axis=0)
            edge = ref[s, 16:32, :] + sign * own_cross
            zero_row = jnp.zeros((1, edge.shape[1]), jnp.float32)
            around = sum(row_pair(edge, zero_row, zero_row)) + ref[s, 32:48, :] + own_force
            around = around + sum(depth_pair(edge))
            side_ref[2 + side] = jnp.where(keep, edge, 0.0)
            side_ref[side] = jnp.where(keep, relaxed(edge, around), 0.0)

        for i in range(MARGIN - 1, layers - MARGIN + 1):
            field = force_ref[s, i]
            beside = row_pair(field, side_ref[3, i : i + 1, :], side_ref[2, i : i + 1, :])
            around = (force_ref[s, i + 1] + force_ref[s, i - 1]) + sum(beside) + sum(depth_pair(field))
            press_ref[s, i] = relaxed(field, around)

        sample_layers(
            s, parts, list(range(MARGIN, layers - MARGIN)), (along_ref, cross_ref, deep_ref),
            lambda k: owner_ref[brick, k], weight_ref, pool_ref,
            out_ref, split_ref, pooled_ref,
            lambda i: press_ref[s, i],
            lambda i: (side_ref[1, i : i + 1, :], side_ref[0, i : i + 1, :]),
        )
        return carry

    lax.fori_loop(0, along_ref.shape[0], snapshot, 0)


def outer_kernel(
    parts, owner_ref, along_ref, cross_ref, deep_ref, weight_ref, pool_ref, low_ref, high_ref, before_ref, after_ref,
    before_fix_ref, after_fix_ref, inner_force_ref, inner_press_ref, _, out_ref, force_ref, press_ref, side_force_ref, side_press_ref,
    split_ref, pooled_ref,
):
    layers = along_ref.shape[1]
    keep_before, keep_after = inside("brick")
    keep_low, keep_high = inside("ana")
    brick = lax.axis_index("brick")

    def snapshot(s, carry):
        def halo(ref, keep, start, size=1):
            return jnp.where(keep, ref[s, start : start + size, :], 0.0)

        def fixed(ref, fix_ref, start, row):
            field = ref[s, start : start + 32, :]
            row_at = lax.broadcasted_iota(jnp.int32, field.shape, 0)
            field = jnp.where(row_at == 0, fix_ref[s, row : row + 1, :], field)
            return jnp.where(row_at == 31, fix_ref[s, row + 1 : row + 2, :], field)

        first, last = along_ref[s, 0], along_ref[s, layers - 1]
        force_ref[0] = jnp.where(keep_before, fixed(before_ref, before_fix_ref, 0, 2), 0.0)
        force_ref[1] = jnp.where(keep_before, fixed(before_ref, before_fix_ref, 32, 0) - 0.5 * first, 0.0)
        force_ref[2] = inner_force_ref[s, 0] + 0.5 * halo(before_ref, keep_before, 64, 32)
        force_ref[3] = inner_force_ref[s, layers - 1] - 0.5 * halo(after_ref, keep_after, 64, 32)
        force_ref[4] = jnp.where(keep_after, fixed(after_ref, after_fix_ref, 32, 0) + 0.5 * last, 0.0)
        force_ref[5] = jnp.where(keep_after, fixed(after_ref, after_fix_ref, 0, 2), 0.0)

        def force(i):
            if i < 1:
                return force_ref[i + 2]
            if i > layers - 2:
                return force_ref[i - layers + 4]
            return inner_force_ref[s, i]

        for side, ref, keep, far, near, corner, row, sign in (
            (0, low_ref, keep_low, 4, 5, 8, 0, -0.5),
            (1, high_ref, keep_high, 7, 6, 9, 31, 0.5),
        ):
            own_cross = jnp.concatenate([cross_ref[s, i, row : row + 1, :] for i in range(layers)], axis=0)
            own_force = jnp.concatenate(
                [force_ref[2, row : row + 1, :]]
                + [inner_force_ref[s, i, row : row + 1, :] for i in range(1, layers - 1)]
                + [force_ref[3, row : row + 1, :]],
                axis=0,
            )
            row_at = lax.broadcasted_iota(jnp.int32, own_force.shape, 0)

            def ends(at):
                first = 0.5 * halo(before_fix_ref, keep_before, at)
                last = -0.5 * halo(after_fix_ref, keep_after, at)
                return jnp.where(row_at == 0, first, 0.0) + jnp.where(row_at == layers - 1, last, 0.0)

            edge = jnp.where(keep, ref[s, 16:32, :] + sign * own_cross + ends(near), 0.0)
            beyond = jnp.where(keep, ref[s, 32:48, :] + ends(far), 0.0)
            corner_before = jnp.where(keep_before, halo(before_fix_ref, keep, corner) - 0.5 * halo(ref, keep, 48), 0.0)
            corner_after = jnp.where(keep_after, halo(after_fix_ref, keep, corner) + 0.5 * halo(ref, keep, 50), 0.0)
            around = sum(row_pair(edge, corner_after, corner_before)) + beyond + own_force
            around = around + sum(depth_pair(edge))
            side_press_ref[side] = jnp.where(keep, relaxed(edge, around), 0.0)
            side_force_ref[side, 8:24, :] = edge
            side_force_ref[side, 7:8, :] = corner_before
            side_force_ref[side, 24:25, :] = corner_after

        low_layers, high_layers = list(range(-1, MARGIN - 1)), list(range(layers - MARGIN + 1, layers + 1))
        place = {i: n for n, i in enumerate(low_layers + high_layers)}
        for i in place:
            field = force(i)
            beside = row_pair(field, side_force_ref[1, 8 + i : 9 + i, :], side_force_ref[0, 8 + i : 9 + i, :])
            around = (force(i + 1) + force(i - 1)) + sum(beside) + sum(depth_pair(field))
            press = relaxed(field, around)
            if i == -1:
                press = jnp.where(keep_before, press, 0.0)
            if i == layers:
                press = jnp.where(keep_after, press, 0.0)
            press_ref[place[i]] = press

        sample_layers(
            s, parts, list(range(MARGIN)) + list(range(layers - MARGIN, layers)), (along_ref, cross_ref, deep_ref),
            lambda k: owner_ref[brick, k], weight_ref, pool_ref, out_ref, split_ref, pooled_ref,
            lambda i: press_ref[place[i]] if i in place else inner_press_ref[s, i],
            lambda i: (side_press_ref[1, i : i + 1, :], side_press_ref[0, i : i + 1, :]),
        )
        return carry

    lax.fori_loop(0, along_ref.shape[0], snapshot, 0)


def weight_kernel(parts, index_ref, out_ref, pool_ref, wide_ref):
    pool_ref[...] = pooling(parts)
    rows = index_ref.shape[0]
    at = lax.broadcasted_iota(jnp.int32, (rows, LANES), 0) * LANES + lax.broadcasted_iota(jnp.int32, (rows, LANES), 1)
    offset = (index_ref[...] - 4 * at).astype(jnp.float32).astype(jnp.bfloat16)
    source = lax.broadcasted_iota(jnp.int32, (LANES, 512), 0)
    target = lax.broadcasted_iota(jnp.int32, (LANES, 512), 1)
    expand = jnp.where(target // 4 == source, 1.0, 0.0).astype(jnp.bfloat16)
    wide = jnp.dot(offset, expand, preferred_element_type=jnp.float32)
    lane_at = lax.broadcasted_iota(jnp.int32, wide.shape, 1)
    hit = jnp.where(wide == (lane_at % 4).astype(jnp.float32), 1.0, 0.0)
    for half in range(2):
        for kt in range(2):
            wide_ref[kt, pl.ds(half, rows, stride=2), :] = hit[:, 256 * half + 128 * kt : 256 * half + 128 * kt + 128]
    for kt in range(2):
        out_ref[:, 128 * kt : 128 * kt + 128] = wide_ref[kt]


def pooling(parts):
    source = lax.broadcasted_iota(jnp.int32, (256 * parts, 256), 0) % 256
    target = lax.broadcasted_iota(jnp.int32, (256 * parts, 256), 1)
    low = (target < 64) & (source // 4 == target)
    high = (target >= 192) & (source // 4 == target - 192)
    return jnp.where(low | high, 1.0, 0.0).astype(jnp.bfloat16)


def exchange(to_before, to_after, axis):
    devices = lax.axis_size(axis)
    up = [(i, (i + 1) % devices) for i in range(devices)]
    down = [(j, i) for i, j in up]
    return lax.ppermute(to_after, axis, up), lax.ppermute(to_before, axis, down)


def grid_kernel(kernel, name, cost, **kwargs):
    flops, data = cost
    return pl.pallas_call(
        kernel,
        compiler_params=pltpu.CompilerParams(vmem_limit_bytes=VMEM_LIMIT),
        cost_estimate=pl.CostEstimate(flops=flops, bytes_accessed=data, transcendentals=0),
        name=name,
        **kwargs,
    )


def front(provisional, sample_index, owner_table):
    snaps, comps, layers, columns, depth = provisional.shape
    bricks = lax.axis_size("brick")
    smem = pl.BlockSpec(memory_space=pltpu.SMEM)
    vmem = pl.BlockSpec(memory_space=pltpu.VMEM)
    samples = layers * columns * depth // 4
    source = provisional.reshape(snaps * comps, layers, columns, depth)
    f32 = lambda *shape: jax.ShapeDtypeStruct(shape, jnp.float32)
    scratch = lambda *shape: pltpu.VMEM(shape, jnp.float32)

    tiles = source.reshape(snaps * comps, layers, columns // 8, 8, 2, LANES)
    tiles = tiles.transpose(0, 1, 2, 4, 3, 5).reshape(snaps * comps, layers, columns // 8, 16, LANES)
    to_low, to_high = grid_kernel(
        ana_edge_kernel,
        "ana_edges",
        (10**6, 4 * 10**6),
        in_specs=[pl.BlockSpec(memory_space=pltpu.HBM)],
        out_specs=[vmem] * 2,
        out_shape=[f32(snaps, ANA_ROWS, depth)] * 2,
        scratch_shapes=[scratch(snaps * comps, layers, 16, LANES)] * 2 + [pltpu.SemaphoreType.DMA((2,))],
    )(pltpu.with_memory_space_constraint(tiles, pltpu.HBM))
    from_low, from_high = exchange(to_low, to_high, "ana")

    weight, pool = grid_kernel(
        functools.partial(weight_kernel, POOL_PARTS),
        "weights",
        (10**6, 10**6),
        in_specs=[vmem],
        out_specs=[vmem] * 2,
        out_shape=[f32(layers * columns, depth), jax.ShapeDtypeStruct((256 * POOL_PARTS, 256), jnp.bfloat16)],
        scratch_shapes=[scratch(2, layers * columns, LANES)],
    )(sample_index.reshape(samples // LANES, LANES))

    *fields, own_force, to_before, to_after = grid_kernel(
        load_kernel,
        "load",
        (10**8, 6 * 10**6),
        in_specs=[pl.BlockSpec(memory_space=pltpu.HBM), pl.BlockSpec(memory_space=pl.ANY)],
        out_specs=[vmem] * 6,
        out_shape=[f32(snaps, layers, columns, depth)] * 4 + [f32(snaps, BULK_ROWS, depth)] * 2,
        scratch_shapes=[pltpu.SemaphoreType.DMA((snaps * comps,))],
    )(pltpu.with_memory_space_constraint(source, pltpu.HBM), to_low)
    from_before, from_after = exchange(to_before, to_after, "brick")

    to_before, to_after = grid_kernel(
        fix_kernel,
        "fix",
        (10**5, 10**6),
        in_specs=[vmem] * 4,
        out_specs=[vmem] * 2,
        out_shape=[f32(snaps, FIX_ROWS, depth)] * 2,
    )(fields[1], own_force, from_low, from_high)
    before_fix, after_fix = exchange(to_before, to_after, "brick")

    split_shape = lambda count: pltpu.VMEM((3 * 32 * count, 256 * POOL_PARTS), jnp.bfloat16)
    force, press, outgoing = grid_kernel(
        functools.partial(inner_kernel, POOL_PARTS),
        "inner_layers",
        (4 * 10**9, 2 * 10**7),
        in_specs=[smem] + [vmem] * 8,
        out_specs=[vmem] * 3,
        out_shape=[f32(snaps, layers, columns, depth)] * 2 + [f32(bricks, comps, 32, LANES)],
        scratch_shapes=[
            scratch(4, layers, depth),
            split_shape(layers - 2 * MARGIN),
            scratch(2, 3 * 32 * (layers - 2 * MARGIN), LANES),
        ],
    )(owner_table, *fields, own_force, weight, pool, from_low, from_high)
    return grid_kernel(
        functools.partial(outer_kernel, POOL_PARTS),
        "outer_layers",
        (3 * 10**9, 10**7),
        in_specs=[smem] + [vmem] * 14,
        out_specs=vmem,
        out_shape=f32(bricks, comps, 32, LANES),
        scratch_shapes=[
            scratch(6, columns, depth),
            scratch(2 * MARGIN, columns, depth),
            scratch(2, 32, depth),
            scratch(2, layers, depth),
            split_shape(2 * MARGIN),
            scratch(2, 3 * 32 * 2 * MARGIN, LANES),
        ],
        input_output_aliases={14: 0},
    )(owner_table, *fields, weight, pool, from_low, from_high, from_before, from_after, before_fix, after_fix, force, press, outgoing)


def per_device(provisional, sample_index, owner_table, weighted_basis):
    snaps = provisional.shape[0]
    rank_count = weighted_basis.shape[0]
    devices = lax.axis_size("brick") * lax.axis_size("ana")
    total_rows = 3.0 * sample_index.shape[2] * devices
    outgoing = front(provisional, sample_index, owner_table)
    arrived = lax.all_to_all(outgoing, "brick", split_axis=0, concat_axis=0, tiled=True)
    basis = jnp.transpose(weighted_basis, (1, 0, 2))
    new_basis, core = tail(basis, arrived, WIDTH, total_rows, devices)
    count = rank_count + snaps
    return (jnp.transpose(new_basis, (1, 0, 2)), core[:count, :count])


def solution(mesh):
    placed = (
        P(None, None, "brick", "ana", None),
        P("brick", "ana", None),
        P(),
        P(None, None, ("brick", "ana")),
    )
    return jax.shard_map(
        per_device,
        mesh=mesh,
        in_specs=placed,
        out_specs=(P(None, None, ("brick", "ana")), P()),
        check_vma=False,
    )
```

time: 236 us -> 81.6 us (0.35)
  local copies, waits for them, and re-layouts: 41.7 us -> 0.02 us
  starting transfers between devices: 48.6 us -> 10.5 us
  matrix products: 32.8 us -> 0 us
  waiting for transfers between devices: 25.1 us -> 0.02 us
  Pallas kernels: 0 us -> 22.6 us
  blocking collectives: 66.9 us -> 47.4 us
  other arithmetic: 19 us -> 0.01 us
    psum x1 -> x0, blocking collectives: 66.9 us -> none  [per_device(): lax.psum(jnp.dot(stacked, stacked.T, precision=lax.Precision.HIGHEST), ('...]
    all_to_all x0 -> x2, blocking collectives: none -> 47.4 us  [the longest x1 31.7 us: per_device(): lax.all_to_all(outgoing, 'brick', split_axis=0, concat_axis=0, tiled=True)]
    ppermute x12 -> x6, starting transfers between devices: 38.2 us -> 10.5 us  [the longest x3 6.52 us: exchange(): lax.ppermute(to_after, axis, up)]
    pallas_call x0 -> x8, Pallas kernels: none -> 22.6 us  [the longest x1 6.16 us: tail(): grid_kernel(functools.partial(apply_kernel, width, SLOTS), 'apply', (10 *...]
    another operation x1 -> x0, matrix products: 16.6 us -> none  [per_device(): jax.scipy.linalg.solve_triangular(lower_factor, stacked, lower=True)]
    dot_general x2 -> x0, matrix products: 16.2 us -> none  [the longest x1 13.3 us: per_device(): jnp.dot(stacked, stacked.T, precision=lax.Precision.HIGHEST)]
    all_to_all x1 -> x0, waiting for transfers between devices: 16.2 us -> none  [per_device(): lax.all_to_all(outgoing, 'brick', split_axis=2, concat_axis=2, tiled=True)]
    another operation x3 -> x0, local copies, waits for them, and re-layouts: 14.6 us -> none  [the longest x1 10.4 us: per_device(): jax.scipy.linalg.solve_triangular(lower_factor, stacked, lower=True)]
  transfers between devices with their start and end apart: 13 -> 6, of which waited for: 7 -> 0; matrix products, arithmetic and copies ran while one was open for 9% -> 0% of each run, Pallas kernels for 0% -> 10%
where the time goes in v3:
time: 81.6 us; the launch traced here: 81.4 us
  blocking collectives  47.4 us (58%)
  Pallas kernels  22.6 us (28%)
  starting transfers between devices  10.5 us (13%)
  between operations  0.92 us (1%)
    all_to_all x1, blocking collectives, per_device(): lax.all_to_all(outgoing, 'brick', split_axis=0, concat_axis=0, tiled=True)  31.7 us
    all_to_all x1, blocking collectives, tail(): partial_sums = lax.all_to_all(copies, ('brick', 'ana'), 0, 0, tiled=True)  15.7 us
    ppermute x3, starting transfers between devices, exchange(): lax.ppermute(to_after, axis, up)  6.52 us
    pallas_call x1, Pallas kernels, tail(): grid_kernel(functools.partial(apply_kernel, width, SLOTS), 'apply', (10 *...  6.16 us
    pallas_call x1, Pallas kernels, front(): grid_kernel(functools.partial(inner_kernel, POOL_PARTS), 'inner_layers',...  4.23 us
    ppermute x3, starting transfers between devices, exchange(): lax.ppermute(to_before, axis, down)  3.95 us
    pallas_call x1, Pallas kernels, tail(): grid_kernel(functools.partial(gram_kernel, width, 1.0 / total_rows), 'gra...  3.32 us
    pallas_call x1, Pallas kernels, front(): grid_kernel(load_kernel, 'load', (10 ** 8, 6 * 10 ** 6), in_specs=[pl.Blo...  3.25 us
  transfers between devices with their start and end apart: 6, of which 0 were waited for; matrix products, arithmetic and copies ran while one was open for 0% of the time, Pallas kernels for 10%

profile of v3, /device:TPU:1, one launch (start us, length us, event | category | flops | bytes accessed | tf_op | source)
XLA Modules:
  0.0 81.4 jit_solution(8628540408191911200)
XLA Ops:
  0.6 2.1 %ana_edges.1 = (f32[4,56,256]{2,1,0:T(8,128)S(1)}, f32[4,56,256]{2,1,0:T(8,128)S(1)}) custom-call(f32[12,16,4,16,128]{4,3,2,1,0:T(8,128)} %bitcast.15), custom_call_target="tpu_custom_call" | custom-call | flops 1000000 | bytes 4000000 | tf_op jit(solution)/shard_map/ana_edges/pallas_call | solution.py:520
  2.7 2.1 %collective-permute-start = (f32[4,56,256]{2,1,0:T(8,128)S(1)}, f32[4,56,256]{2,1,0:T(8,128)S(1)}, u32[]{:S(2)}, u32[]{:S(2)}) collective-permute-start(f32[4,56,256]{2,1,0:T(8,128)S(1)} %get-tuple-element.25), channel_id=1, source_target_pairs={{0,1},{1,2},{2,3},{3,0},{4,5},{5,6},{6,7},{7,4},{8,9},{9,10},{10,1... | collective-permute-start | bytes 688136 | tf_op jit(solution)/shard_map/ppermute | solution.py:494
  4.8 1.3 %collective-permute-start.1 = (f32[4,56,256]{2,1,0:T(8,128)S(1)}, f32[4,56,256]{2,1,0:T(8,128)S(1)}, u32[]{:S(2)}, u32[]{:S(2)}) collective-permute-start(f32[4,56,256]{2,1,0:T(8,128)S(1)} %get-tuple-element.19._), channel_id=1, source_target_pairs={{1,0},{2,1},{3,2},{0,3},{5,4},{6,5},{7,6},{4,7},{9,8},{10,9},{11,1... | collective-permute-start | bytes 688136 | tf_op jit(solution)/shard_map/ppermute | solution.py:494
  6.2 3.3 %load.1 = (f32[4,16,32,256]{3,2,1,0:T(8,128)S(1)}, f32[4,16,32,256]{3,2,1,0:T(8,128)S(1)}, f32[4,16,32,256]{3,2,1,0:T(8,128)S(1)}, f32[4,16,32,256]{3,2,1,0:T(8,...) custom-call(f32[12,16,32,256]{3,2,1,0:T(8,128)} %bitcast.16, f32[4,56,256]{2,1,0:T(8,128)S(1)} %get-tuple-element.19._), custom_call_target="tpu_custom_call" | custom-call | flops 100000000 | bytes 6000000 | tf_op jit(solution)/shard_map/load/pallas_call | solution.py:541
  9.4 2.6 %collective-permute-start.2 = (f32[4,96,256]{2,1,0:T(8,128)S(1)}, f32[4,96,256]{2,1,0:T(8,128)S(1)}, u32[]{:S(2)}, u32[]{:S(2)}) collective-permute-start(f32[4,96,256]{2,1,0:T(8,128)S(1)} %get-tuple-element.26), channel_id=1, source_target_pairs={{0,4},{4,8},{8,12},{12,16},{16,20},{20,24},{24,28},{28,32},{32,36}... | collective-permute-start | bytes 1179656 | tf_op jit(solution)/shard_map/ppermute | solution.py:494
  12.0 0.0 collective-permute-start.3
  12.0 0.3 weights.1
  12.4 0.0 collective-permute-done.from_low_ref.low_ref
  12.4 0.0 collective-permute-done.1.from_high_ref.high_ref
  12.4 0.0 copy-start.1
  12.4 0.1 fix.1
  12.5 1.8 %collective-permute-start.4 = (f32[4,16,256]{2,1,0:T(8,128)S(1)}, f32[4,16,256]{2,1,0:T(8,128)S(1)}, u32[]{:S(2)}, u32[]{:S(2)}) collective-permute-start(f32[4,16,256]{2,1,0:T(8,128)S(1)} %get-tuple-element.29), channel_id=1, source_target_pairs={{0,4},{4,8},{8,12},{12,16},{16,20},{20,24},{24,28},{28,32},{32,36}... | collective-permute-start | bytes 196616 | tf_op jit(solution)/shard_map/ppermute | solution.py:494
  14.3 2.6 %collective-permute-start.5 = (f32[4,16,256]{2,1,0:T(8,128)S(1)}, f32[4,16,256]{2,1,0:T(8,128)S(1)}, u32[]{:S(2)}, u32[]{:S(2)}) collective-permute-start(f32[4,16,256]{2,1,0:T(8,128)S(1)} %get-tuple-element.30), channel_id=1, source_target_pairs={{4,0},{8,4},{12,8},{16,12},{20,16},{24,20},{28,24},{32,28},{36,32}... | collective-permute-start | bytes 196616 | tf_op jit(solution)/shard_map/ppermute | solution.py:494
  16.9 4.2 %inner_layers.1 = (f32[4,16,32,256]{3,2,1,0:T(8,128)S(1)}, f32[4,16,32,256]{3,2,1,0:T(8,128)S(1)}, f32[32,3,32,128]{3,2,1,0:T(8,128)S(1)}) custom-call(s32[32,32]{1,0:T(8,128)S(1)} %copy-done.1, f32[4,16,32,256]{3,2,1,0:T(8,128)S(1)} %get-tuple-element.20.along_ref, f32[4,16,32,256]{3,2,1,0:T(8,128)S(1)} %get-tuple-element.21.cross_ref, ...), custom_call_target="tpu_custom_call" | custom-call | flops 4000000000 | bytes 20000000 | tf_op jit(solution)/shard_map/inner_layers/pallas_call | solution.py:563
  21.2 0.0 collective-permute-done.4.before_fix_ref
  21.2 0.0 collective-permute-done.5.after_fix_ref
  21.2 0.0 collective-permute-done.2.before_ref
  21.2 0.0 collective-permute-done.3.after_ref
  21.2 0.0 slice-start
  21.2 3.1 %outer_layers.1 = f32[32,3,32,128]{3,2,1,0:T(8,128)S(1)} custom-call(s32[32,32]{1,0:T(8,128)S(1)} %copy-done.1, f32[4,16,32,256]{3,2,1,0:T(8,128)S(1)} %get-tuple-element.20.along_ref, f32[4,16,32,256]{3,2,1,0:T(8,128)S(1)} %get-tuple-element.21.cross_ref, f32[4,16,32,256]{3,2,1,0:T(8,128)S(1)} %get-tuple-element.22.deep_ref, ...), custom_call_target="tpu_custom_call", output_to_operand_aliasing={{}: (14, {})} | custom-call | flops 3000000000 | bytes 10000000 | tf_op jit(solution)/shard_map/outer_layers/pallas_call | solution.py:576
  24.4 31.7 %all_to_all.10.arrived_ref = f32[32,3,32,128]{3,2,1,0:T(8,128)S(1)} all-to-all(f32[32,3,32,128]{3,2,1,0:T(8,128)S(1)} %outer_layers.1), channel_id=1, replica_groups=mesh['brick'=32,'ana'=4] {'brick'}, dimensions={0} | all-to-all | bytes 3145728 | tf_op jit(solution)/shard_map/all_to_all | solution.py:601
  56.1 3.3 %gram.1 = f32[128,4,128]{2,1,0:T(4,128)S(1)} custom-call(f32[3,16,32768]{2,1,0:T(8,128)S(1)} %bitcast.12, f32[32,3,32,128]{3,2,1,0:T(8,128)S(1)} %all_to_all.10.arrived_ref), custom_call_target="tpu_custom_call" | custom-call | flops 1000000000 | bytes 10000000 | tf_op jit(solution)/shard_map/gram/pallas_call | solution.py:134
  59.4 15.7 %all_to_all.11.packed_ref = f32[128,4,128]{2,1,0:T(4,128)S(1)} all-to-all(f32[128,4,128]{2,1,0:T(4,128)S(1)} %gram.1), channel_id=1, replica_groups=mesh['brick'=32,'ana'=4] {'brick','ana'}, dimensions={0} | all-to-all | bytes 524288 | tf_op jit(solution)/shard_map/all_to_all | solution.py:142
  75.1 6.2 %apply.1 = (f32[3,20,32768]{2,1,0:T(8,128)}, f32[24,128]{1,0:T(8,128)}) custom-call(f32[3,16,32768]{2,1,0:T(8,128)S(1)} %bitcast.13, f32[32,3,32,128]{3,2,1,0:T(8,128)S(1)} %all_to_all.10.arrived_ref, f32[128,4,128]{2,1,0:T(4,128)S(1)} %all_to_all.11.packed_ref), custom_call_target="tpu_custom_call" | custom-call | flops 1000000000 | bytes 20000000 | tf_op jit(solution)/shard_map/apply/pallas_call | solution.py:144
  (7 shorter events, 0.0 us)
Async XLA Ops:
  2.7 9.7 %collective-permute-start = (f32[4,56,256]{2,1,0:T(8,128)S(1)}, f32[4,56,256]{2,1,0:T(8,128)S(1)}, u32[]{:S(2)}, u32[]{:S(2)}) collective-permute-start(f32[4,56,256]{2,1,0:T(8,128)S(1)} %get-tuple-element.25), channel_id=1, source_target_pairs={{0,1},{1,2},{2,3},{3,0},{4,5},{5,6},{6,7},{7,4},{8,9},{9,10},{10,1... | collective-permute-start | bytes 688136 | tf_op jit(solution)/shard_map/ppermute | solution.py:494
  4.8 7.6 %collective-permute-start.1 = (f32[4,56,256]{2,1,0:T(8,128)S(1)}, f32[4,56,256]{2,1,0:T(8,128)S(1)}, u32[]{:S(2)}, u32[]{:S(2)}) collective-permute-start(f32[4,56,256]{2,1,0:T(8,128)S(1)} %get-tuple-element.19._), channel_id=1, source_target_pairs={{1,0},{2,1},{3,2},{0,3},{5,4},{6,5},{7,6},{4,7},{9,8},{10,9},{11,1... | collective-permute-start | bytes 688136 | tf_op jit(solution)/shard_map/ppermute | solution.py:494
  6.2 5.9 %copy-start = (s32[1,1,32768]{2,1,0:T(1,128)S(1)}, s32[1,1,32768]{2,1,0:T(1,128)}, u32[]{:S(2)}) copy-start(s32[1,1,32768]{2,1,0:T(1,128)} %param.5) | copy-start | bytes 393220
  9.4 11.7 %collective-permute-start.2 = (f32[4,96,256]{2,1,0:T(8,128)S(1)}, f32[4,96,256]{2,1,0:T(8,128)S(1)}, u32[]{:S(2)}, u32[]{:S(2)}) collective-permute-start(f32[4,96,256]{2,1,0:T(8,128)S(1)} %get-tuple-element.26), channel_id=1, source_target_pairs={{0,4},{4,8},{8,12},{12,16},{16,20},{20,24},{24,28},{28,32},{32,36}... | collective-permute-start | bytes 1179656 | tf_op jit(solution)/shard_map/ppermute | solution.py:494
  12.0 9.2 %collective-permute-start.3 = (f32[4,96,256]{2,1,0:T(8,128)S(1)}, f32[4,96,256]{2,1,0:T(8,128)S(1)}, u32[]{:S(2)}, u32[]{:S(2)}) collective-permute-start(f32[4,96,256]{2,1,0:T(8,128)S(1)} %get-tuple-element.27), channel_id=1, source_target_pairs={{4,0},{8,4},{12,8},{16,12},{20,16},{24,20},{28,24},{32,28},{36,32}... | collective-permute-start | bytes 1179656 | tf_op jit(solution)/shard_map/ppermute | solution.py:494
  12.4 4.5 %copy-start.1 = (s32[32,32]{1,0:T(8,128)S(1)}, s32[32,32]{1,0:T(8,128)}, u32[]{:S(2)}) copy-start(s32[32,32]{1,0:T(8,128)} %owner_ref.3) | copy-start | bytes 12292
  12.5 8.7 %collective-permute-start.4 = (f32[4,16,256]{2,1,0:T(8,128)S(1)}, f32[4,16,256]{2,1,0:T(8,128)S(1)}, u32[]{:S(2)}, u32[]{:S(2)}) collective-permute-start(f32[4,16,256]{2,1,0:T(8,128)S(1)} %get-tuple-element.29), channel_id=1, source_target_pairs={{0,4},{4,8},{8,12},{12,16},{16,20},{20,24},{24,28},{28,32},{32,36}... | collective-permute-start | bytes 196616 | tf_op jit(solution)/shard_map/ppermute | solution.py:494
  14.3 6.8 %collective-permute-start.5 = (f32[4,16,256]{2,1,0:T(8,128)S(1)}, f32[4,16,256]{2,1,0:T(8,128)S(1)}, u32[]{:S(2)}, u32[]{:S(2)}) collective-permute-start(f32[4,16,256]{2,1,0:T(8,128)S(1)} %get-tuple-element.30), channel_id=1, source_target_pairs={{4,0},{8,4},{12,8},{16,12},{20,16},{24,20},{28,24},{32,28},{36,32}... | collective-permute-start | bytes 196616 | tf_op jit(solution)/shard_map/ppermute | solution.py:494
  21.2 34.9 %slice-start = ((s8[6291456]{0:T(1024)(128)(4,1)}), s8[4194304]{0:T(1024)(128)(4,1)S(1)}, s32[]{:S(2)}) async-start(s8[6291456]{0:T(1024)(128)(4,1)} %bitcast.10), calls=%async_computation.2 | async-start | bytes 8388608
  21.2 34.9 %slice-start.1 = ((s8[6291456]{0:T(1024)(128)(4,1)}), s8[2097152]{0:T(1024)(128)(4,1)S(1)}, s32[]{:S(2)}) async-start(s8[6291456]{0:T(1024)(128)(4,1)} %bitcast.10), calls=%async_computation.3 | async-start | bytes 4194304

commit v4 on v3

--- a/solution.py
+++ b/solution.py
@@ -8,6 +8,7 @@
 
 LANES = 128
 PACK = 24
+GRAM = 20
 POOL_PARTS = 2
 WIDTH = 8192
 SLOTS = 4
@@ -19,25 +20,27 @@
     return high, (block - high.astype(jnp.float32)).astype(jnp.bfloat16)
 
 
+def sample_pieces(arrived_ref, c, start, width):
+    at = lax.broadcasted_iota(jnp.int32, (8, LANES), 0)
+    tiles = []
+    for b in range(start // 1024, (start + width) // 1024):
+        for n in range(0, 32, 8):
+            both = arrived_ref[b, c, n : n + 8, :]
+            high = both.astype(jnp.bfloat16).astype(jnp.float32)
+            low = both - high
+            tiles.append(jnp.where(at < 4, high, pltpu.roll(low, 4, 0)))
+            tiles.append(jnp.where(at < 4, pltpu.roll(high, 4, 0), low))
+    rows = jnp.concatenate(tiles, axis=1)
+    return jnp.concatenate([rows, rows], axis=0).astype(jnp.bfloat16)
+
+
 def stacked_pieces(basis_ref, arrived_ref, c, start, width, order):
-    rows = jnp.concatenate(
-        [
-            arrived_ref[b, c, 4 * jj : 4 * jj + 4, :]
-            for b in range(start // 1024, (start + width) // 1024)
-            for jj in range(8)
-        ],
-        axis=1,
-    )
-    small = split_pieces(rows)
-    small = [small[p].astype(jnp.float32) for p in order] + [jnp.zeros_like(rows)] * (4 - len(order))
-    small = jnp.concatenate(small, axis=0).astype(jnp.bfloat16)
     large = split_pieces(basis_ref[c, :, start : start + width])
-    return jnp.concatenate([large[p] for p in order] + [small], axis=0)
+    return jnp.concatenate([large[p] for p in order] + [sample_pieces(arrived_ref, c, start, width)], axis=0)
 
 
 def gram_kernel(width, scale, basis_ref, arrived_ref, out_ref):
     comps, rank_count, columns = basis_ref.shape
-    parts = 2
     total = 0.0
     for c in range(comps):
         for start in range(0, columns, width):
@@ -45,53 +48,48 @@
             total = total + lax.dot_general(
                 pieces, pieces, (((1,), (1,)), ((), ())), preferred_element_type=jnp.float32
             )
-    base = rank_count * parts
-    rows = sum(total[rank_count * p : rank_count * (p + 1)] for p in range(parts))
-    small = sum(total[base + 4 * p : base + 4 * (p + 1)] for p in range(parts))
-    rows = jnp.concatenate([rows, small, jnp.zeros_like(small)], axis=0)
-    left = sum(rows[:, rank_count * p : rank_count * (p + 1)] for p in range(parts))
-    right = sum(rows[:, base + 4 * p : base + 4 * (p + 1)] for p in range(parts))
-    rest = jnp.zeros((PACK, LANES - rank_count - 4), jnp.float32)
-    gram = jnp.concatenate([left, right, rest], axis=1) * scale
-    packed = gram[0:4]
-    for n in range(1, 5):
-        packed = packed + pltpu.roll(gram[4 * n : 4 * n + 4], n * PACK, 1)
+    total = jnp.concatenate([total, jnp.zeros((total.shape[0], LANES - total.shape[1]), jnp.float32)], axis=1)
+    lane_at = lax.broadcasted_iota(jnp.int32, total.shape, 1)
+    left = jnp.where(lane_at < 16, total, pltpu.roll(total, LANES - 20, 1)) + pltpu.roll(total, LANES - 16, 1)
+    left = jnp.where(lane_at < GRAM, left, 0.0) * scale
+    row_at = lax.broadcasted_iota(jnp.int32, (8, LANES), 0)
+    small = jnp.where(row_at < 4, left[32:40] + pltpu.roll(left[32:40], 4, 0), 0.0)
+    packed = left[0:8] + left[16:24]
+    packed = packed + pltpu.roll(left[8:16] + left[24:32], GRAM, 1) + pltpu.roll(small, 2 * GRAM, 1)
+    packed = packed[0:4] + pltpu.roll(packed, 3 * GRAM, 1)[4:8]
     out_ref[...] = jnp.broadcast_to(packed[None], out_ref.shape)
 
 
-def factor(tiles, count):
+def factor(tiles, count, block):
     row_at = [lax.broadcasted_iota(jnp.int32, (8, LANES), 0) + 8 * t for t in range(3)]
     lane_at = lax.broadcasted_iota(jnp.int32, (8, LANES), 1)
     work = [jnp.where(lane_at < PACK, tiles[t], 0.0) + jnp.where(lane_at == row_at[t] + 32, 1.0, 0.0) for t in range(3)]
-    roots = []
-    block = 4
+    diagonal = [jnp.ones((8, LANES), jnp.float32)] * 3
+
+    def spread(piece):
+        return jnp.broadcast_to(piece, (8, LANES))
+
     for j in range(0, count, block):
-        t0, r0 = j // 8, j % 8
-        rows = [jnp.broadcast_to(work[t0][r0 + q : r0 + q + 1], (8, LANES)) for q in range(block)]
-        cols = [[jnp.broadcast_to(work[t][:, j + q : j + q + 1], (8, LANES)) for t in range(3)] for q in range(block)]
-        pivots = [
-            [jnp.broadcast_to(work[t0][r0 + q : r0 + q + 1, j + r : j + r + 1], (8, LANES)) for r in range(block)]
-            for q in range(block)
-        ]
+        later = [t for t in range(3) if j + block < count and 8 * t + 8 > j + block]
+        rows = [spread(work[(j + q) // 8][(j + q) % 8 : (j + q) % 8 + 1]) for q in range(block)]
+        cols = [{t: spread(work[t][:, j + q : j + q + 1]) for t in later} for q in range(block)]
+        pivots = [[spread(rows[q][:, j + r : j + r + 1]) if r >= q else None for r in range(block)] for q in range(block)]
         for q in range(block):
             inverse = 1.0 / pivots[q][q]
-            roots.append(pivots[q][q])
             for r in range(q + 1, block):
-                ratio = pivots[r][q] * inverse
-                across = pivots[q][r] * inverse
+                ratio = pivots[q][r] * inverse
                 rows[r] = rows[r] - ratio * rows[q]
-                for t in range(t0, 3):
-                    cols[r][t] = cols[r][t] - cols[q][t] * across
-                for u in range(q + 1, block):
+                for t in later:
+                    cols[r][t] = cols[r][t] - ratio * cols[q][t]
+                for u in range(r, block):
                     pivots[r][u] = pivots[r][u] - ratio * pivots[q][u]
-            for t in range(t0, 3):
-                ratio = jnp.where(row_at[t] > j + q, cols[q][t] * inverse, 0.0)
+            for t in later:
+                ratio = jnp.where(row_at[t] >= j + block, cols[q][t] * inverse, 0.0)
                 work[t] = work[t] - ratio * rows[q]
-    for t in range(3):
-        diagonal = jnp.ones((8, LANES), jnp.float32)
-        for j in range(8 * t, min(count, 8 * t + 8)):
-            diagonal = jnp.where(row_at[t] == j, roots[j], diagonal)
-        work[t] = work[t] / jnp.sqrt(diagonal)
+            t = (j + q) // 8
+            work[t] = jnp.where(row_at[t] == j + q, rows[q], work[t])
+            diagonal[t] = jnp.where(row_at[t] == j + q, pivots[q][q], diagonal[t])
+    work = [work[t] / jnp.sqrt(diagonal[t]) for t in range(3)]
     upper = [jnp.where((lane_at >= row_at[t]) & (lane_at < PACK), work[t], 0.0) for t in range(3)]
     inverse = jnp.concatenate([pltpu.roll(work[t], LANES - 32, 1)[:, :PACK] for t in range(3)], axis=0)
     return upper, inverse
@@ -101,9 +99,11 @@
     comps, rank_count, columns = basis_ref.shape
     count = out_ref.shape[1]
     packed = jnp.sum(packed_ref[...], axis=0)
-    parts = [packed] + [pltpu.roll(packed, LANES - n * PACK, 1) for n in range(1, 5)] + [jnp.zeros_like(packed)]
-    tiles = [jnp.concatenate(parts[2 * t : 2 * t + 2], axis=0) for t in range(3)]
-    upper, inverse = factor(tiles, count)
+    packed = jnp.concatenate([packed, pltpu.roll(packed, LANES - 3 * GRAM, 1)], axis=0)
+    lane_at = lax.broadcasted_iota(jnp.int32, packed.shape, 1)
+    tiles = [packed, pltpu.roll(packed, LANES - GRAM, 1), pltpu.roll(packed, LANES - 2 * GRAM, 1)]
+    tiles = [jnp.where(lane_at < GRAM, tile, 0.0) for tile in tiles]
+    upper, inverse = factor(tiles, count, count // 2)
     for t in range(3):
         core_ref[8 * t : 8 * t + 8, :] = upper[t]
     high, low = [piece.astype(jnp.float32) for piece in split_pieces(inverse)]
@@ -198,10 +198,11 @@
     snaps = to_low_ref.shape[0]
     fields, layers, rows, lanes = low_ref.shape
     last = tiles_ref.shape[2] - 1
-    copies = [
-        pltpu.make_async_copy(tiles_ref.at[:, :, at], ref, sem.at[n])
-        for n, (at, ref) in enumerate(((0, low_ref), (last, high_ref)))
-    ]
+    copies = []
+    for s in range(snaps):
+        span = pl.ds(3 * s, 3)
+        for n, (at, ref) in enumerate(((0, low_ref), (last, high_ref))):
+            copies.append(pltpu.make_async_copy(tiles_ref.at[span, :, at], ref.at[span], sem.at[2 * s + n]))
     for copy in copies:
         copy.start()
     flat = (fields * layers * rows, lanes)
@@ -213,13 +214,12 @@
         )
 
     zero_row = jnp.zeros((1, 2 * lanes), jnp.float32)
-    for copy, side_ref, out_ref, edge, second, third, sign in (
-        (copies[0], low_ref, to_low_ref, 0, 1, 2, 1.0),
-        (copies[1], high_ref, to_high_ref, 7, 6, 5, -1.0),
-    ):
-        copy.wait()
-        ref = side_ref.reshape(*flat)
-        for s in range(snaps):
+    for s in range(snaps):
+        for n, (side_ref, out_ref, edge, second, third, sign) in enumerate(
+            ((low_ref, to_low_ref, 0, 1, 2, 1.0), (high_ref, to_high_ref, 7, 6, 5, -1.0))
+        ):
+            copies[2 * s + n].wait()
+            ref = side_ref.reshape(*flat)
             speed = [column(ref, s, 0, j) for j in (edge, second)]
             cross = [column(ref, s, 1, j) for j in (edge, second, third)]
             deep = [column(ref, s, 2, j) for j in (edge, second)]
@@ -524,7 +524,7 @@
         in_specs=[pl.BlockSpec(memory_space=pltpu.HBM)],
         out_specs=[vmem] * 2,
         out_shape=[f32(snaps, ANA_ROWS, depth)] * 2,
-        scratch_shapes=[scratch(snaps * comps, layers, 16, LANES)] * 2 + [pltpu.SemaphoreType.DMA((2,))],
+        scratch_shapes=[scratch(snaps * comps, layers, 16, LANES)] * 2 + [pltpu.SemaphoreType.DMA((2 * snaps,))],
     )(pltpu.with_memory_space_constraint(tiles, pltpu.HBM))
     from_low, from_high = exchange(to_low, to_high, "ana")
 

time: 81.6 us -> 80.7 us (0.989)
  Pallas kernels: 22.6 us -> 21.7 us
where the time goes in v4:
time: 80.7 us; the launch traced here: 80.5 us
  blocking collectives  47.4 us (59%)
  Pallas kernels  21.7 us (27%)
  starting transfers between devices  10.5 us (13%)
  between operations  0.92 us (1%)
    all_to_all x1, blocking collectives, per_device(): lax.all_to_all(outgoing, 'brick', split_axis=0, concat_axis=0, tiled=True)  31.7 us
    all_to_all x1, blocking collectives, tail(): partial_sums = lax.all_to_all(copies, ('brick', 'ana'), 0, 0, tiled=True)  15.7 us
    ppermute x3, starting transfers between devices, exchange(): lax.ppermute(to_after, axis, up)  6.52 us
    pallas_call x1, Pallas kernels, tail(): grid_kernel(functools.partial(apply_kernel, width, SLOTS), 'apply', (10 *...  5.81 us
    pallas_call x1, Pallas kernels, front(): grid_kernel(functools.partial(inner_kernel, POOL_PARTS), 'inner_layers',...  4.23 us
    ppermute x3, starting transfers between devices, exchange(): lax.ppermute(to_before, axis, down)  3.96 us
    pallas_call x1, Pallas kernels, front(): grid_kernel(load_kernel, 'load', (10 ** 8, 6 * 10 ** 6), in_specs=[pl.Blo...  3.25 us
    pallas_call x1, Pallas kernels, front(): grid_kernel(functools.partial(outer_kernel, POOL_PARTS), 'outer_layers',...  3.13 us
  transfers between devices with their start and end apart: 6, of which 0 were waited for; matrix products, arithmetic and copies ran while one was open for 0% of the time, Pallas kernels for 10%

profile of v4, /device:TPU:1, one launch (start us, length us, event | category | flops | bytes accessed | tf_op | source)
XLA Modules:
  0.0 80.5 jit_solution(3892858677709770963)
XLA Ops:
  0.6 2.0 %ana_edges.1 = (f32[4,56,256]{2,1,0:T(8,128)S(1)}, f32[4,56,256]{2,1,0:T(8,128)S(1)}) custom-call(f32[12,16,4,16,128]{4,3,2,1,0:T(8,128)} %bitcast.15), custom_call_target="tpu_custom_call" | custom-call | flops 1000000 | bytes 4000000 | tf_op jit(solution)/shard_map/ana_edges/pallas_call | solution.py:520
  2.6 2.1 %collective-permute-start = (f32[4,56,256]{2,1,0:T(8,128)S(1)}, f32[4,56,256]{2,1,0:T(8,128)S(1)}, u32[]{:S(2)}, u32[]{:S(2)}) collective-permute-start(f32[4,56,256]{2,1,0:T(8,128)S(1)} %get-tuple-element.25), channel_id=1, source_target_pairs={{0,1},{1,2},{2,3},{3,0},{4,5},{5,6},{6,7},{7,4},{8,9},{9,10},{10,1... | collective-permute-start | bytes 688136 | tf_op jit(solution)/shard_map/ppermute | solution.py:494
  4.8 1.3 %collective-permute-start.1 = (f32[4,56,256]{2,1,0:T(8,128)S(1)}, f32[4,56,256]{2,1,0:T(8,128)S(1)}, u32[]{:S(2)}, u32[]{:S(2)}) collective-permute-start(f32[4,56,256]{2,1,0:T(8,128)S(1)} %get-tuple-element.19._), channel_id=1, source_target_pairs={{1,0},{2,1},{3,2},{0,3},{5,4},{6,5},{7,6},{4,7},{9,8},{10,9},{11,1... | collective-permute-start | bytes 688136 | tf_op jit(solution)/shard_map/ppermute | solution.py:494
  6.1 3.3 %load.1 = (f32[4,16,32,256]{3,2,1,0:T(8,128)S(1)}, f32[4,16,32,256]{3,2,1,0:T(8,128)S(1)}, f32[4,16,32,256]{3,2,1,0:T(8,128)S(1)}, f32[4,16,32,256]{3,2,1,0:T(8,...) custom-call(f32[12,16,32,256]{3,2,1,0:T(8,128)} %bitcast.16, f32[4,56,256]{2,1,0:T(8,128)S(1)} %get-tuple-element.19._), custom_call_target="tpu_custom_call" | custom-call | flops 100000000 | bytes 6000000 | tf_op jit(solution)/shard_map/load/pallas_call | solution.py:541
  9.4 2.6 %collective-permute-start.2 = (f32[4,96,256]{2,1,0:T(8,128)S(1)}, f32[4,96,256]{2,1,0:T(8,128)S(1)}, u32[]{:S(2)}, u32[]{:S(2)}) collective-permute-start(f32[4,96,256]{2,1,0:T(8,128)S(1)} %get-tuple-element.26), channel_id=1, source_target_pairs={{0,4},{4,8},{8,12},{12,16},{16,20},{20,24},{24,28},{28,32},{32,36}... | collective-permute-start | bytes 1179656 | tf_op jit(solution)/shard_map/ppermute | solution.py:494
  12.0 0.0 collective-permute-start.3
  12.0 0.3 weights.1
  12.3 0.0 collective-permute-done.from_low_ref.low_ref
  12.3 0.0 collective-permute-done.1.from_high_ref.high_ref
  12.3 0.0 copy-start.1
  12.3 0.1 fix.1
  12.4 1.8 %collective-permute-start.4 = (f32[4,16,256]{2,1,0:T(8,128)S(1)}, f32[4,16,256]{2,1,0:T(8,128)S(1)}, u32[]{:S(2)}, u32[]{:S(2)}) collective-permute-start(f32[4,16,256]{2,1,0:T(8,128)S(1)} %get-tuple-element.29), channel_id=1, source_target_pairs={{0,4},{4,8},{8,12},{12,16},{16,20},{20,24},{24,28},{28,32},{32,36}... | collective-permute-start | bytes 196616 | tf_op jit(solution)/shard_map/ppermute | solution.py:494
  14.3 2.6 %collective-permute-start.5 = (f32[4,16,256]{2,1,0:T(8,128)S(1)}, f32[4,16,256]{2,1,0:T(8,128)S(1)}, u32[]{:S(2)}, u32[]{:S(2)}) collective-permute-start(f32[4,16,256]{2,1,0:T(8,128)S(1)} %get-tuple-element.30), channel_id=1, source_target_pairs={{4,0},{8,4},{12,8},{16,12},{20,16},{24,20},{28,24},{32,28},{36,32}... | collective-permute-start | bytes 196616 | tf_op jit(solution)/shard_map/ppermute | solution.py:494
  16.9 4.2 %inner_layers.1 = (f32[4,16,32,256]{3,2,1,0:T(8,128)S(1)}, f32[4,16,32,256]{3,2,1,0:T(8,128)S(1)}, f32[32,3,32,128]{3,2,1,0:T(8,128)S(1)}) custom-call(s32[32,32]{1,0:T(8,128)S(1)} %copy-done.1, f32[4,16,32,256]{3,2,1,0:T(8,128)S(1)} %get-tuple-element.20.along_ref, f32[4,16,32,256]{3,2,1,0:T(8,128)S(1)} %get-tuple-element.21.cross_ref, ...), custom_call_target="tpu_custom_call" | custom-call | flops 4000000000 | bytes 20000000 | tf_op jit(solution)/shard_map/inner_layers/pallas_call | solution.py:563
  21.1 0.0 collective-permute-done.4.before_fix_ref
  21.1 0.0 collective-permute-done.5.after_fix_ref
  21.1 0.0 collective-permute-done.3.after_ref
  21.1 0.0 slice-start
  21.1 0.0 slice-start.1
  21.2 3.1 %outer_layers.1 = f32[32,3,32,128]{3,2,1,0:T(8,128)S(1)} custom-call(s32[32,32]{1,0:T(8,128)S(1)} %copy-done.1, f32[4,16,32,256]{3,2,1,0:T(8,128)S(1)} %get-tuple-element.20.along_ref, f32[4,16,32,256]{3,2,1,0:T(8,128)S(1)} %get-tuple-element.21.cross_ref, f32[4,16,32,256]{3,2,1,0:T(8,128)S(1)} %get-tuple-element.22.deep_ref, ...), custom_call_target="tpu_custom_call", output_to_operand_aliasing={{}: (14, {})} | custom-call | flops 3000000000 | bytes 10000000 | tf_op jit(solution)/shard_map/outer_layers/pallas_call | solution.py:576
  24.3 31.7 %all_to_all.10.arrived_ref = f32[32,3,32,128]{3,2,1,0:T(8,128)S(1)} all-to-all(f32[32,3,32,128]{3,2,1,0:T(8,128)S(1)} %outer_layers.1), channel_id=1, replica_groups=mesh['brick'=32,'ana'=4] {'brick'}, dimensions={0} | all-to-all | bytes 3145728 | tf_op jit(solution)/shard_map/all_to_all | solution.py:601
  56.0 2.8 %gram.1 = f32[128,4,128]{2,1,0:T(4,128)S(1)} custom-call(f32[3,16,32768]{2,1,0:T(8,128)S(1)} %bitcast.12, f32[32,3,32,128]{3,2,1,0:T(8,128)S(1)} %all_to_all.10.arrived_ref), custom_call_target="tpu_custom_call" | custom-call | flops 1000000000 | bytes 10000000 | tf_op jit(solution)/shard_map/gram/pallas_call | solution.py:134
  58.9 15.7 %all_to_all.11.packed_ref = f32[128,4,128]{2,1,0:T(4,128)S(1)} all-to-all(f32[128,4,128]{2,1,0:T(4,128)S(1)} %gram.1), channel_id=1, replica_groups=mesh['brick'=32,'ana'=4] {'brick','ana'}, dimensions={0} | all-to-all | bytes 524288 | tf_op jit(solution)/shard_map/all_to_all | solution.py:142
  74.5 5.8 %apply.1 = (f32[3,20,32768]{2,1,0:T(8,128)}, f32[24,128]{1,0:T(8,128)}) custom-call(f32[3,16,32768]{2,1,0:T(8,128)S(1)} %bitcast.13, f32[32,3,32,128]{3,2,1,0:T(8,128)S(1)} %all_to_all.10.arrived_ref, f32[128,4,128]{2,1,0:T(4,128)S(1)} %all_to_all.11.packed_ref), custom_call_target="tpu_custom_call" | custom-call | flops 1000000000 | bytes 20000000 | tf_op jit(solution)/shard_map/apply/pallas_call | solution.py:144
  (7 shorter events, 0.0 us)
Async XLA Ops:
  2.6 9.7 %collective-permute-start = (f32[4,56,256]{2,1,0:T(8,128)S(1)}, f32[4,56,256]{2,1,0:T(8,128)S(1)}, u32[]{:S(2)}, u32[]{:S(2)}) collective-permute-start(f32[4,56,256]{2,1,0:T(8,128)S(1)} %get-tuple-element.25), channel_id=1, source_target_pairs={{0,1},{1,2},{2,3},{3,0},{4,5},{5,6},{6,7},{7,4},{8,9},{9,10},{10,1... | collective-permute-start | bytes 688136 | tf_op jit(solution)/shard_map/ppermute | solution.py:494
  4.8 7.6 %collective-permute-start.1 = (f32[4,56,256]{2,1,0:T(8,128)S(1)}, f32[4,56,256]{2,1,0:T(8,128)S(1)}, u32[]{:S(2)}, u32[]{:S(2)}) collective-permute-start(f32[4,56,256]{2,1,0:T(8,128)S(1)} %get-tuple-element.19._), channel_id=1, source_target_pairs={{1,0},{2,1},{3,2},{0,3},{5,4},{6,5},{7,6},{4,7},{9,8},{10,9},{11,1... | collective-permute-start | bytes 688136 | tf_op jit(solution)/shard_map/ppermute | solution.py:494
  6.1 5.9 %copy-start = (s32[1,1,32768]{2,1,0:T(1,128)S(1)}, s32[1,1,32768]{2,1,0:T(1,128)}, u32[]{:S(2)}) copy-start(s32[1,1,32768]{2,1,0:T(1,128)} %param.5) | copy-start | bytes 393220
  9.4 11.7 %collective-permute-start.2 = (f32[4,96,256]{2,1,0:T(8,128)S(1)}, f32[4,96,256]{2,1,0:T(8,128)S(1)}, u32[]{:S(2)}, u32[]{:S(2)}) collective-permute-start(f32[4,96,256]{2,1,0:T(8,128)S(1)} %get-tuple-element.26), channel_id=1, source_target_pairs={{0,4},{4,8},{8,12},{12,16},{16,20},{20,24},{24,28},{28,32},{32,36}... | collective-permute-start | bytes 1179656 | tf_op jit(solution)/shard_map/ppermute | solution.py:494
  12.0 9.2 %collective-permute-start.3 = (f32[4,96,256]{2,1,0:T(8,128)S(1)}, f32[4,96,256]{2,1,0:T(8,128)S(1)}, u32[]{:S(2)}, u32[]{:S(2)}) collective-permute-start(f32[4,96,256]{2,1,0:T(8,128)S(1)} %get-tuple-element.27), channel_id=1, source_target_pairs={{4,0},{8,4},{12,8},{16,12},{20,16},{24,20},{28,24},{32,28},{36,32}... | collective-permute-start | bytes 1179656 | tf_op jit(solution)/shard_map/ppermute | solution.py:494
  12.3 4.5 %copy-start.1 = (s32[32,32]{1,0:T(8,128)S(1)}, s32[32,32]{1,0:T(8,128)}, u32[]{:S(2)}) copy-start(s32[32,32]{1,0:T(8,128)} %owner_ref.3) | copy-start | bytes 12292
  12.4 8.7 %collective-permute-start.4 = (f32[4,16,256]{2,1,0:T(8,128)S(1)}, f32[4,16,256]{2,1,0:T(8,128)S(1)}, u32[]{:S(2)}, u32[]{:S(2)}) collective-permute-start(f32[4,16,256]{2,1,0:T(8,128)S(1)} %get-tuple-element.29), channel_id=1, source_target_pairs={{0,4},{4,8},{8,12},{12,16},{16,20},{20,24},{24,28},{28,32},{32,36}... | collective-permute-start | bytes 196616 | tf_op jit(solution)/shard_map/ppermute | solution.py:494
  14.3 6.9 %collective-permute-start.5 = (f32[4,16,256]{2,1,0:T(8,128)S(1)}, f32[4,16,256]{2,1,0:T(8,128)S(1)}, u32[]{:S(2)}, u32[]{:S(2)}) collective-permute-start(f32[4,16,256]{2,1,0:T(8,128)S(1)} %get-tuple-element.30), channel_id=1, source_target_pairs={{4,0},{8,4},{12,8},{16,12},{20,16},{24,20},{28,24},{32,28},{36,32}... | collective-permute-start | bytes 196616 | tf_op jit(solution)/shard_map/ppermute | solution.py:494
  21.1 34.9 %slice-start = ((s8[6291456]{0:T(1024)(128)(4,1)}), s8[4194304]{0:T(1024)(128)(4,1)S(1)}, s32[]{:S(2)}) async-start(s8[6291456]{0:T(1024)(128)(4,1)} %bitcast.10), calls=%async_computation.2 | async-start | bytes 8388608
  21.1 34.9 %slice-start.1 = ((s8[6291456]{0:T(1024)(128)(4,1)}), s8[2097152]{0:T(1024)(128)(4,1)S(1)}, s32[]{:S(2)}) async-start(s8[6291456]{0:T(1024)(128)(4,1)} %bitcast.10), calls=%async_computation.3 | async-start | bytes 4194304

commit v5 on v4

--- a/solution.py
+++ b/solution.py
@@ -163,6 +163,7 @@
 BULK_ROWS = 96
 FIX_ROWS = 16
 MARGIN = 3
+PADDED = 48
 
 
 def depth_pair(field):
@@ -188,6 +189,19 @@
 
 def difference(pair):
     return pair[0] - pair[1]
+
+
+def halves(row):
+    return [row[:, LANES * h : LANES * h + LANES] for h in range(2)]
+
+
+def put_rows(ref, at, start, rows):
+    for h, half in enumerate(halves(rows)):
+        ref[(*at, h, slice(8 + start, 8 + start + rows.shape[0]), slice(None))] = half
+
+
+def get_rows(ref, at, start, size):
+    return jnp.concatenate([ref[(*at, h, slice(8 + start, 8 + start + size), slice(None))] for h in range(2)], axis=1)
 
 
 def relaxed(field, around):
@@ -292,14 +306,13 @@
             out_ref[s] = jnp.concatenate(rows, axis=0)
 
 
-def sample_layers(s, parts, layers, fields, owner, weight_ref, pool_ref, out_ref, split_ref, pooled_ref, press, beside):
+def sample_layers(s, parts, layers, fields, owner, weight_ref, pool_ref, out_ref, split_ref, pooled_ref, press):
     count = len(layers)
     for n, i in enumerate(layers):
-        centre = press(i)
-        after_row, before_row = beside(i)
+        centre = get_rows(*press(i), 0, 32)
         gradient = (
-            press(i + 1) - press(i - 1),
-            difference(row_pair(centre, after_row, before_row)),
+            get_rows(*press(i + 1), 0, 32) - get_rows(*press(i - 1), 0, 32),
+            get_rows(*press(i), 1, 32) - get_rows(*press(i), -1, 32),
             difference(depth_pair(centre)),
         )
         weight = weight_ref[32 * i : 32 * i + 32, :]
@@ -316,38 +329,38 @@
     pooled_ref[1] = pooled[:, LANES:]
     rows = 3 * count * 32
     flat = pooled_ref.reshape(2 * rows, LANES)
-    out_flat = out_ref.reshape(out_ref.shape[0] * 3 * 32, LANES)
     for n, i in enumerate(layers):
         for half in range(2):
             place = owner(2 * i + half)
             for c in range(3):
                 start = 32 * (c * count + n) + 16 * half
                 tile = flat[pl.ds(start, 8, stride=2), :] + flat[pl.ds(start + rows + 1, 8, stride=2), :]
-                out_flat[pl.ds((place * 3 + c) * 32 + s, 8, stride=4), :] = tile
+                out_ref[place, c, pl.ds(s, 8, stride=4), :] = tile
 
 
 def inner_kernel(
     parts, owner_ref, along_ref, cross_ref, deep_ref, own_force_ref, weight_ref, pool_ref, low_ref, high_ref,
-    force_ref, press_ref, out_ref, side_ref, split_ref, pooled_ref,
+    force_ref, press_ref, out_ref, sides_ref, split_ref, pooled_ref,
 ):
     layers = along_ref.shape[1]
     keep_low, keep_high = inside("ana")
     brick = lax.axis_index("brick")
 
-    def snapshot(s, carry):
+    def snapshot(s):
+        side_ref = sides_ref.at[s]
         def halo(ref, keep, start, size=1):
             return jnp.where(keep, ref[s, start : start + size, :], 0.0)
 
         row_at = lax.broadcasted_iota(jnp.int32, (8, along_ref.shape[3]), 0)
         for i in range(layers):
             first, last = own_force_ref[s, i, 0:8, :], own_force_ref[s, i, 24:32, :]
-            force_ref[s, i, 0:8, :] = jnp.where(row_at == 0, first + 0.5 * halo(low_ref, keep_low, i), first)
-            force_ref[s, i, 8:24, :] = own_force_ref[s, i, 8:24, :]
-            force_ref[s, i, 24:32, :] = jnp.where(row_at == 7, last - 0.5 * halo(high_ref, keep_high, i), last)
+            put_rows(force_ref, (s, i), 0, jnp.where(row_at == 0, first + 0.5 * halo(low_ref, keep_low, i), first))
+            put_rows(force_ref, (s, i), 8, own_force_ref[s, i, 8:24, :])
+            put_rows(force_ref, (s, i), 24, jnp.where(row_at == 7, last - 0.5 * halo(high_ref, keep_high, i), last))
 
         for side, ref, keep, row, sign in ((0, low_ref, keep_low, 0, -0.5), (1, high_ref, keep_high, 31, 0.5)):
             own_cross = jnp.concatenate([cross_ref[s, i, row : row + 1, :] for i in range(layers)], axis=0)
-            own_force = jnp.concatenate([force_ref[s, i, row : row + 1, :] for i in range(layers)], axis=0)
+            own_force = jnp.concatenate([get_rows(force_ref, (s, i), row, 1) for i in range(layers)], axis=0)
             edge = ref[s, 16:32, :] + sign * own_cross
             zero_row = jnp.zeros((1, edge.shape[1]), jnp.float32)
             around = sum(row_pair(edge, zero_row, zero_row)) + ref[s, 32:48, :] + own_force
@@ -355,27 +368,30 @@
             side_ref[2 + side] = jnp.where(keep, edge, 0.0)
             side_ref[side] = jnp.where(keep, relaxed(edge, around), 0.0)
 
+        for i in range(layers):
+            put_rows(force_ref, (s, i), -1, side_ref[2, i : i + 1, :])
+            put_rows(force_ref, (s, i), 32, side_ref[3, i : i + 1, :])
         for i in range(MARGIN - 1, layers - MARGIN + 1):
-            field = force_ref[s, i]
-            beside = row_pair(field, side_ref[3, i : i + 1, :], side_ref[2, i : i + 1, :])
-            around = (force_ref[s, i + 1] + force_ref[s, i - 1]) + sum(beside) + sum(depth_pair(field))
-            press_ref[s, i] = relaxed(field, around)
+            field = get_rows(force_ref, (s, i), 0, 32)
+            around = get_rows(force_ref, (s, i + 1), 0, 32) + get_rows(force_ref, (s, i - 1), 0, 32)
+            around = around + (get_rows(force_ref, (s, i), 1, 32) + get_rows(force_ref, (s, i), -1, 32))
+            put_rows(press_ref, (s, i), 0, relaxed(field, around + sum(depth_pair(field))))
+            put_rows(press_ref, (s, i), -1, side_ref[0, i : i + 1, :])
+            put_rows(press_ref, (s, i), 32, side_ref[1, i : i + 1, :])
 
         sample_layers(
             s, parts, list(range(MARGIN, layers - MARGIN)), (along_ref, cross_ref, deep_ref),
             lambda k: owner_ref[brick, k], weight_ref, pool_ref,
-            out_ref, split_ref, pooled_ref,
-            lambda i: press_ref[s, i],
-            lambda i: (side_ref[1, i : i + 1, :], side_ref[0, i : i + 1, :]),
+            out_ref, split_ref.at[s], pooled_ref.at[s],
+            lambda i: (press_ref, (s, i)),
         )
-        return carry
-
-    lax.fori_loop(0, along_ref.shape[0], snapshot, 0)
+    for s in range(along_ref.shape[0]):
+        snapshot(s)
 
 
 def outer_kernel(
     parts, owner_ref, along_ref, cross_ref, deep_ref, weight_ref, pool_ref, low_ref, high_ref, before_ref, after_ref,
-    before_fix_ref, after_fix_ref, inner_force_ref, inner_press_ref, _, out_ref, force_ref, press_ref, side_force_ref, side_press_ref,
+    before_fix_ref, after_fix_ref, inner_force_ref, inner_press_ref, _, out_ref, forces_ref, presses_ref, side_forces_ref, side_presses_ref,
     split_ref, pooled_ref,
 ):
     layers = along_ref.shape[1]
@@ -383,7 +399,9 @@
     keep_low, keep_high = inside("ana")
     brick = lax.axis_index("brick")
 
-    def snapshot(s, carry):
+    def snapshot(s):
+        force_ref, press_ref = forces_ref.at[s], presses_ref.at[s]
+        side_force_ref, side_press_ref = side_forces_ref.at[s], side_presses_ref.at[s]
         def halo(ref, keep, start, size=1):
             return jnp.where(keep, ref[s, start : start + size, :], 0.0)
 
@@ -394,19 +412,23 @@
             return jnp.where(row_at == 31, fix_ref[s, row + 1 : row + 2, :], field)
 
         first, last = along_ref[s, 0], along_ref[s, layers - 1]
-        force_ref[0] = jnp.where(keep_before, fixed(before_ref, before_fix_ref, 0, 2), 0.0)
-        force_ref[1] = jnp.where(keep_before, fixed(before_ref, before_fix_ref, 32, 0) - 0.5 * first, 0.0)
-        force_ref[2] = inner_force_ref[s, 0] + 0.5 * halo(before_ref, keep_before, 64, 32)
-        force_ref[3] = inner_force_ref[s, layers - 1] - 0.5 * halo(after_ref, keep_after, 64, 32)
-        force_ref[4] = jnp.where(keep_after, fixed(after_ref, after_fix_ref, 32, 0) + 0.5 * last, 0.0)
-        force_ref[5] = jnp.where(keep_after, fixed(after_ref, after_fix_ref, 0, 2), 0.0)
+        edges = (
+            jnp.where(keep_before, fixed(before_ref, before_fix_ref, 0, 2), 0.0),
+            jnp.where(keep_before, fixed(before_ref, before_fix_ref, 32, 0) - 0.5 * first, 0.0),
+            get_rows(inner_force_ref, (s, 0), 0, 32) + 0.5 * halo(before_ref, keep_before, 64, 32),
+            get_rows(inner_force_ref, (s, layers - 1), 0, 32) - 0.5 * halo(after_ref, keep_after, 64, 32),
+            jnp.where(keep_after, fixed(after_ref, after_fix_ref, 32, 0) + 0.5 * last, 0.0),
+            jnp.where(keep_after, fixed(after_ref, after_fix_ref, 0, 2), 0.0),
+        )
+        for n, edge in enumerate(edges):
+            put_rows(force_ref, (n,), 0, edge)
 
         def force(i):
             if i < 1:
-                return force_ref[i + 2]
+                return force_ref, (i + 2,)
             if i > layers - 2:
-                return force_ref[i - layers + 4]
-            return inner_force_ref[s, i]
+                return force_ref, (i - layers + 4,)
+            return inner_force_ref, (s, i)
 
         for side, ref, keep, far, near, corner, row, sign in (
             (0, low_ref, keep_low, 4, 5, 8, 0, -0.5),
@@ -414,9 +436,7 @@
         ):
             own_cross = jnp.concatenate([cross_ref[s, i, row : row + 1, :] for i in range(layers)], axis=0)
             own_force = jnp.concatenate(
-                [force_ref[2, row : row + 1, :]]
-                + [inner_force_ref[s, i, row : row + 1, :] for i in range(1, layers - 1)]
-                + [force_ref[3, row : row + 1, :]],
+                [get_rows(*force(i), row, 1) for i in range(layers)],
                 axis=0,
             )
             row_at = lax.broadcasted_iota(jnp.int32, own_force.shape, 0)
@@ -439,26 +459,30 @@
 
         low_layers, high_layers = list(range(-1, MARGIN - 1)), list(range(layers - MARGIN + 1, layers + 1))
         place = {i: n for n, i in enumerate(low_layers + high_layers)}
+        for i in (-1, 0, layers - 1, layers):
+            put_rows(*force(i), -1, side_force_ref[0, 8 + i : 9 + i, :])
+            put_rows(*force(i), 32, side_force_ref[1, 8 + i : 9 + i, :])
         for i in place:
-            field = force(i)
-            beside = row_pair(field, side_force_ref[1, 8 + i : 9 + i, :], side_force_ref[0, 8 + i : 9 + i, :])
-            around = (force(i + 1) + force(i - 1)) + sum(beside) + sum(depth_pair(field))
-            press = relaxed(field, around)
+            field = get_rows(*force(i), 0, 32)
+            around = get_rows(*force(i + 1), 0, 32) + get_rows(*force(i - 1), 0, 32)
+            around = around + (get_rows(*force(i), 1, 32) + get_rows(*force(i), -1, 32))
+            press = relaxed(field, around + sum(depth_pair(field)))
             if i == -1:
                 press = jnp.where(keep_before, press, 0.0)
             if i == layers:
                 press = jnp.where(keep_after, press, 0.0)
-            press_ref[place[i]] = press
+            put_rows(press_ref, (place[i],), 0, press)
+            if 0 <= i < layers:
+                put_rows(press_ref, (place[i],), -1, side_press_ref[0, i : i + 1, :])
+                put_rows(press_ref, (place[i],), 32, side_press_ref[1, i : i + 1, :])
 
         sample_layers(
             s, parts, list(range(MARGIN)) + list(range(layers - MARGIN, layers)), (along_ref, cross_ref, deep_ref),
-            lambda k: owner_ref[brick, k], weight_ref, pool_ref, out_ref, split_ref, pooled_ref,
-            lambda i: press_ref[place[i]] if i in place else inner_press_ref[s, i],
-            lambda i: (side_press_ref[1, i : i + 1, :], side_press_ref[0, i : i + 1, :]),
+            lambda k: owner_ref[brick, k], weight_ref, pool_ref, out_ref, split_ref.at[s], pooled_ref.at[s],
+            lambda i: (press_ref, (place[i],)) if i in place else (inner_press_ref, (s, i)),
         )
-        return carry
-
-    lax.fori_loop(0, along_ref.shape[0], snapshot, 0)
+    for s in range(along_ref.shape[0]):
+        snapshot(s)
 
 
 def weight_kernel(parts, index_ref, out_ref, pool_ref, wide_ref):
@@ -559,18 +583,18 @@
     )(fields[1], own_force, from_low, from_high)
     before_fix, after_fix = exchange(to_before, to_after, "brick")
 
-    split_shape = lambda count: pltpu.VMEM((3 * 32 * count, 256 * POOL_PARTS), jnp.bfloat16)
+    split_shape = lambda count: pltpu.VMEM((snaps, 3 * 32 * count, 256 * POOL_PARTS), jnp.bfloat16)
     force, press, outgoing = grid_kernel(
         functools.partial(inner_kernel, POOL_PARTS),
         "inner_layers",
         (4 * 10**9, 2 * 10**7),
         in_specs=[smem] + [vmem] * 8,
         out_specs=[vmem] * 3,
-        out_shape=[f32(snaps, layers, columns, depth)] * 2 + [f32(bricks, comps, 32, LANES)],
+        out_shape=[f32(snaps, layers, 2, PADDED, LANES)] * 2 + [f32(bricks, comps, 32, LANES)],
         scratch_shapes=[
-            scratch(4, layers, depth),
+            scratch(snaps, 4, layers, depth),
             split_shape(layers - 2 * MARGIN),
-            scratch(2, 3 * 32 * (layers - 2 * MARGIN), LANES),
+            scratch(snaps, 2, 3 * 32 * (layers - 2 * MARGIN), LANES),
         ],
     )(owner_table, *fields, own_force, weight, pool, from_low, from_high)
     return grid_kernel(
@@ -581,12 +605,12 @@
         out_specs=vmem,
         out_shape=f32(bricks, comps, 32, LANES),
         scratch_shapes=[
-            scratch(6, columns, depth),
-            scratch(2 * MARGIN, columns, depth),
-            scratch(2, 32, depth),
-            scratch(2, layers, depth),
+            scratch(snaps, 6, 2, PADDED, LANES),
+            scratch(snaps, 2 * MARGIN, 2, PADDED, LANES),
+            scratch(snaps, 2, 32, depth),
+            scratch(snaps, 2, layers, depth),
             split_shape(2 * MARGIN),
-            scratch(2, 3 * 32 * 2 * MARGIN, LANES),
+            scratch(snaps, 2, 3 * 32 * 2 * MARGIN, LANES),
         ],
         input_output_aliases={14: 0},
     )(owner_table, *fields, weight, pool, from_low, from_high, from_before, from_after, before_fix, after_fix, force, press, outgoing)

time: 80.7 us -> 80.1 us (level)
  Pallas kernels: 21.7 us -> 20.6 us
  transfers between devices with their start and end apart: 6 -> 6, of which waited for: 0 -> 0; matrix products, arithmetic and copies ran while one was open for 0% -> 0% of each run, Pallas kernels for 10% -> 9%
where the time goes in v5:
time: 80.1 us; the launch traced here: 80 us
  blocking collectives  47.9 us (60%)
  Pallas kernels  20.6 us (26%)
  starting transfers between devices  10.5 us (13%)
  between operations  0.92 us (1%)
    all_to_all x1, blocking collectives, per_device(): lax.all_to_all(outgoing, 'brick', split_axis=0, concat_axis=0, tiled=True)  32.3 us
    all_to_all x1, blocking collectives, tail(): partial_sums = lax.all_to_all(copies, ('brick', 'ana'), 0, 0, tiled=True)  15.6 us
    ppermute x3, starting transfers between devices, exchange(): lax.ppermute(to_after, axis, up)  6.52 us
    pallas_call x1, Pallas kernels, tail(): grid_kernel(functools.partial(apply_kernel, width, SLOTS), 'apply', (10 *...  5.8 us
    ppermute x3, starting transfers between devices, exchange(): lax.ppermute(to_before, axis, down)  3.96 us
    pallas_call x1, Pallas kernels, front(): grid_kernel(functools.partial(inner_kernel, POOL_PARTS), 'inner_layers',...  3.69 us
    pallas_call x1, Pallas kernels, front(): grid_kernel(load_kernel, 'load', (10 ** 8, 6 * 10 ** 6), in_specs=[pl.Blo...  3.25 us
    pallas_call x1, Pallas kernels, tail(): grid_kernel(functools.partial(gram_kernel, width, 1.0 / total_rows), 'gra...  2.82 us
  transfers between devices with their start and end apart: 6, of which 0 were waited for; matrix products, arithmetic and copies ran while one was open for 0% of the time, Pallas kernels for 9%

profile of v5, /device:TPU:1, one launch (start us, length us, event | category | flops | bytes accessed | tf_op | source)
XLA Modules:
  0.0 80.0 jit_solution(1191223759225244221)
XLA Ops:
  0.6 2.0 %ana_edges.1 = (f32[4,56,256]{2,1,0:T(8,128)S(1)}, f32[4,56,256]{2,1,0:T(8,128)S(1)}) custom-call(f32[12,16,4,16,128]{4,3,2,1,0:T(8,128)} %bitcast.15), custom_call_target="tpu_custom_call" | custom-call | flops 1000000 | bytes 4000000 | tf_op jit(solution)/shard_map/ana_edges/pallas_call | solution.py:544
  2.6 2.1 %collective-permute-start = (f32[4,56,256]{2,1,0:T(8,128)S(1)}, f32[4,56,256]{2,1,0:T(8,128)S(1)}, u32[]{:S(2)}, u32[]{:S(2)}) collective-permute-start(f32[4,56,256]{2,1,0:T(8,128)S(1)} %get-tuple-element.25), channel_id=1, source_target_pairs={{0,1},{1,2},{2,3},{3,0},{4,5},{5,6},{6,7},{7,4},{8,9},{9,10},{10,1... | collective-permute-start | bytes 688136 | tf_op jit(solution)/shard_map/ppermute | solution.py:518
  4.8 1.3 %collective-permute-start.1 = (f32[4,56,256]{2,1,0:T(8,128)S(1)}, f32[4,56,256]{2,1,0:T(8,128)S(1)}, u32[]{:S(2)}, u32[]{:S(2)}) collective-permute-start(f32[4,56,256]{2,1,0:T(8,128)S(1)} %get-tuple-element.19._), channel_id=1, source_target_pairs={{1,0},{2,1},{3,2},{0,3},{5,4},{6,5},{7,6},{4,7},{9,8},{10,9},{11,1... | collective-permute-start | bytes 688136 | tf_op jit(solution)/shard_map/ppermute | solution.py:518
  6.1 3.3 %load.1 = (f32[4,16,32,256]{3,2,1,0:T(8,128)S(1)}, f32[4,16,32,256]{3,2,1,0:T(8,128)S(1)}, f32[4,16,32,256]{3,2,1,0:T(8,128)S(1)}, f32[4,16,32,256]{3,2,1,0:T(8,...) custom-call(f32[12,16,32,256]{3,2,1,0:T(8,128)} %bitcast.16, f32[4,56,256]{2,1,0:T(8,128)S(1)} %get-tuple-element.19._), custom_call_target="tpu_custom_call" | custom-call | flops 100000000 | bytes 6000000 | tf_op jit(solution)/shard_map/load/pallas_call | solution.py:565
  9.4 2.6 %collective-permute-start.2 = (f32[4,96,256]{2,1,0:T(8,128)S(1)}, f32[4,96,256]{2,1,0:T(8,128)S(1)}, u32[]{:S(2)}, u32[]{:S(2)}) collective-permute-start(f32[4,96,256]{2,1,0:T(8,128)S(1)} %get-tuple-element.26), channel_id=1, source_target_pairs={{0,4},{4,8},{8,12},{12,16},{16,20},{20,24},{24,28},{28,32},{32,36}... | collective-permute-start | bytes 1179656 | tf_op jit(solution)/shard_map/ppermute | solution.py:518
  12.0 0.0 collective-permute-start.3
  12.0 0.3 weights.1
  12.3 0.0 collective-permute-done.from_low_ref.low_ref
  12.3 0.0 collective-permute-done.1.from_high_ref.high_ref
  12.3 0.0 copy-start.1
  12.3 0.1 fix.1
  12.4 1.8 %collective-permute-start.4 = (f32[4,16,256]{2,1,0:T(8,128)S(1)}, f32[4,16,256]{2,1,0:T(8,128)S(1)}, u32[]{:S(2)}, u32[]{:S(2)}) collective-permute-start(f32[4,16,256]{2,1,0:T(8,128)S(1)} %get-tuple-element.29), channel_id=1, source_target_pairs={{0,4},{4,8},{8,12},{12,16},{16,20},{20,24},{24,28},{28,32},{32,36}... | collective-permute-start | bytes 196616 | tf_op jit(solution)/shard_map/ppermute | solution.py:518
  14.3 2.6 %collective-permute-start.5 = (f32[4,16,256]{2,1,0:T(8,128)S(1)}, f32[4,16,256]{2,1,0:T(8,128)S(1)}, u32[]{:S(2)}, u32[]{:S(2)}) collective-permute-start(f32[4,16,256]{2,1,0:T(8,128)S(1)} %get-tuple-element.30), channel_id=1, source_target_pairs={{4,0},{8,4},{12,8},{16,12},{20,16},{24,20},{28,24},{32,28},{36,32}... | collective-permute-start | bytes 196616 | tf_op jit(solution)/shard_map/ppermute | solution.py:518
  16.9 3.7 %inner_layers.1 = (f32[4,16,2,48,128]{4,3,2,1,0:T(8,128)S(1)}, f32[4,16,2,48,128]{4,3,2,1,0:T(8,128)S(1)}, f32[32,3,32,128]{3,2,1,0:T(8,128)S(1)}) custom-call(s32[32,32]{1,0:T(8,128)S(1)} %copy-done.1, f32[4,16,32,256]{3,2,1,0:T(8,128)S(1)} %get-tuple-element.20.along_ref, f32[4,16,32,256]{3,2,1,0:T(8,128)S(1)} %get-tuple-element.21.cross_ref, ...), custom_call_target="tpu_custom_call" | custom-call | flops 4000000000 | bytes 20000000 | tf_op jit(solution)/shard_map/inner_layers/pallas_call | solution.py:587
  20.6 0.0 collective-permute-done.4.before_fix_ref
  20.6 0.0 collective-permute-done.5.after_fix_ref
  20.6 0.0 collective-permute-done.2.before_ref
  20.6 0.0 collective-permute-done.3.after_ref
  20.6 0.0 slice-start
  20.6 2.6 %outer_layers.1 = f32[32,3,32,128]{3,2,1,0:T(8,128)S(1)} custom-call(s32[32,32]{1,0:T(8,128)S(1)} %copy-done.1, f32[4,16,32,256]{3,2,1,0:T(8,128)S(1)} %get-tuple-element.20.along_ref, f32[4,16,32,256]{3,2,1,0:T(8,128)S(1)} %get-tuple-element.21.cross_ref, f32[4,16,32,256]{3,2,1,0:T(8,128)S(1)} %get-tuple-element.22.deep_ref, ...), custom_call_target="tpu_custom_call", output_to_operand_aliasing={{}: (14, {})} | custom-call | flops 3000000000 | bytes 10000000 | tf_op jit(solution)/shard_map/outer_layers/pallas_call | solution.py:600
  23.2 32.3 %all_to_all.10.arrived_ref = f32[32,3,32,128]{3,2,1,0:T(8,128)S(1)} all-to-all(f32[32,3,32,128]{3,2,1,0:T(8,128)S(1)} %outer_layers.1), channel_id=1, replica_groups=mesh['brick'=32,'ana'=4] {'brick'}, dimensions={0} | all-to-all | bytes 3145728 | tf_op jit(solution)/shard_map/all_to_all | solution.py:625
  55.5 2.8 %gram.1 = f32[128,4,128]{2,1,0:T(4,128)S(1)} custom-call(f32[3,16,32768]{2,1,0:T(8,128)S(1)} %bitcast.12, f32[32,3,32,128]{3,2,1,0:T(8,128)S(1)} %all_to_all.10.arrived_ref), custom_call_target="tpu_custom_call" | custom-call | flops 1000000000 | bytes 10000000 | tf_op jit(solution)/shard_map/gram/pallas_call | solution.py:134
  58.3 15.6 %all_to_all.11.packed_ref = f32[128,4,128]{2,1,0:T(4,128)S(1)} all-to-all(f32[128,4,128]{2,1,0:T(4,128)S(1)} %gram.1), channel_id=1, replica_groups=mesh['brick'=32,'ana'=4] {'brick','ana'}, dimensions={0} | all-to-all | bytes 524288 | tf_op jit(solution)/shard_map/all_to_all | solution.py:142
  74.0 5.8 %apply.1 = (f32[3,20,32768]{2,1,0:T(8,128)}, f32[24,128]{1,0:T(8,128)}) custom-call(f32[3,16,32768]{2,1,0:T(8,128)S(1)} %bitcast.13, f32[32,3,32,128]{3,2,1,0:T(8,128)S(1)} %all_to_all.10.arrived_ref, f32[128,4,128]{2,1,0:T(4,128)S(1)} %all_to_all.11.packed_ref), custom_call_target="tpu_custom_call" | custom-call | flops 1000000000 | bytes 20000000 | tf_op jit(solution)/shard_map/apply/pallas_call | solution.py:144
  (7 shorter events, 0.0 us)
Async XLA Ops:
  2.6 9.7 %collective-permute-start = (f32[4,56,256]{2,1,0:T(8,128)S(1)}, f32[4,56,256]{2,1,0:T(8,128)S(1)}, u32[]{:S(2)}, u32[]{:S(2)}) collective-permute-start(f32[4,56,256]{2,1,0:T(8,128)S(1)} %get-tuple-element.25), channel_id=1, source_target_pairs={{0,1},{1,2},{2,3},{3,0},{4,5},{5,6},{6,7},{7,4},{8,9},{9,10},{10,1... | collective-permute-start | bytes 688136 | tf_op jit(solution)/shard_map/ppermute | solution.py:518
  4.8 7.6 %collective-permute-start.1 = (f32[4,56,256]{2,1,0:T(8,128)S(1)}, f32[4,56,256]{2,1,0:T(8,128)S(1)}, u32[]{:S(2)}, u32[]{:S(2)}) collective-permute-start(f32[4,56,256]{2,1,0:T(8,128)S(1)} %get-tuple-element.19._), channel_id=1, source_target_pairs={{1,0},{2,1},{3,2},{0,3},{5,4},{6,5},{7,6},{4,7},{9,8},{10,9},{11,1... | collective-permute-start | bytes 688136 | tf_op jit(solution)/shard_map/ppermute | solution.py:518
  6.1 5.9 %copy-start = (s32[1,1,32768]{2,1,0:T(1,128)S(1)}, s32[1,1,32768]{2,1,0:T(1,128)}, u32[]{:S(2)}) copy-start(s32[1,1,32768]{2,1,0:T(1,128)} %param.5) | copy-start | bytes 393220
  9.4 11.2 %collective-permute-start.2 = (f32[4,96,256]{2,1,0:T(8,128)S(1)}, f32[4,96,256]{2,1,0:T(8,128)S(1)}, u32[]{:S(2)}, u32[]{:S(2)}) collective-permute-start(f32[4,96,256]{2,1,0:T(8,128)S(1)} %get-tuple-element.26), channel_id=1, source_target_pairs={{0,4},{4,8},{8,12},{12,16},{16,20},{20,24},{24,28},{28,32},{32,36}... | collective-permute-start | bytes 1179656 | tf_op jit(solution)/shard_map/ppermute | solution.py:518
  12.0 8.6 %collective-permute-start.3 = (f32[4,96,256]{2,1,0:T(8,128)S(1)}, f32[4,96,256]{2,1,0:T(8,128)S(1)}, u32[]{:S(2)}, u32[]{:S(2)}) collective-permute-start(f32[4,96,256]{2,1,0:T(8,128)S(1)} %get-tuple-element.27), channel_id=1, source_target_pairs={{4,0},{8,4},{12,8},{16,12},{20,16},{24,20},{28,24},{32,28},{36,32}... | collective-permute-start | bytes 1179656 | tf_op jit(solution)/shard_map/ppermute | solution.py:518
  12.3 4.5 %copy-start.1 = (s32[32,32]{1,0:T(8,128)S(1)}, s32[32,32]{1,0:T(8,128)}, u32[]{:S(2)}) copy-start(s32[32,32]{1,0:T(8,128)} %owner_ref.3) | copy-start | bytes 12292
  12.4 8.1 %collective-permute-start.4 = (f32[4,16,256]{2,1,0:T(8,128)S(1)}, f32[4,16,256]{2,1,0:T(8,128)S(1)}, u32[]{:S(2)}, u32[]{:S(2)}) collective-permute-start(f32[4,16,256]{2,1,0:T(8,128)S(1)} %get-tuple-element.29), channel_id=1, source_target_pairs={{0,4},{4,8},{8,12},{12,16},{16,20},{20,24},{24,28},{28,32},{32,36}... | collective-permute-start | bytes 196616 | tf_op jit(solution)/shard_map/ppermute | solution.py:518
  14.3 6.3 %collective-permute-start.5 = (f32[4,16,256]{2,1,0:T(8,128)S(1)}, f32[4,16,256]{2,1,0:T(8,128)S(1)}, u32[]{:S(2)}, u32[]{:S(2)}) collective-permute-start(f32[4,16,256]{2,1,0:T(8,128)S(1)} %get-tuple-element.30), channel_id=1, source_target_pairs={{4,0},{8,4},{12,8},{16,12},{20,16},{24,20},{28,24},{32,28},{36,32}... | collective-permute-start | bytes 196616 | tf_op jit(solution)/shard_map/ppermute | solution.py:518
  20.6 34.9 %slice-start = ((s8[6291456]{0:T(1024)(128)(4,1)}), s8[4194304]{0:T(1024)(128)(4,1)S(1)}, s32[]{:S(2)}) async-start(s8[6291456]{0:T(1024)(128)(4,1)} %bitcast.10), calls=%async_computation.2 | async-start | bytes 8388608
  20.6 34.9 %slice-start.1 = ((s8[6291456]{0:T(1024)(128)(4,1)}), s8[2097152]{0:T(1024)(128)(4,1)S(1)}, s32[]{:S(2)}) async-start(s8[6291456]{0:T(1024)(128)(4,1)} %bitcast.10), calls=%async_computation.3 | async-start | bytes 4194304

commit v6 on v5

--- a/solution.py
+++ b/solution.py
@@ -112,16 +112,21 @@
     left.append(jnp.zeros((PACK, 16 - 4 * len(order)), jnp.float32))
     left_ref[...] = jnp.concatenate(left, axis=1).astype(jnp.bfloat16)
 
-    blocks = [(c, start) for c in range(comps) for start in range(0, columns, width)]
+    blocks = [(c, start, width) for c in range(comps) for start in range(0, columns, width)]
+    c, start, size = blocks[-1]
+    blocks = [(0, 0, 2048), (0, 2048, width - 2048)] + blocks[1:-1]
+    blocks = blocks + [(c, start, size - 2048), (c, start + size - 2048, 2048)]
     copies = []
-    for n, (c, start) in enumerate(blocks):
+    for n, (c, start, size) in enumerate(blocks):
         if n >= slots:
             copies[n - slots].wait()
-        pieces = stacked_pieces(basis_ref, arrived_ref, c, start, width, (0, 1, 0))
+        pieces = stacked_pieces(basis_ref, arrived_ref, c, start, size, (0, 1, 0))
         product = jnp.dot(left_ref[...], pieces, preferred_element_type=jnp.float32)
         slot = n % slots
-        slot_ref[slot] = product[:count]
-        copy = pltpu.make_async_copy(slot_ref.at[slot], out_ref.at[c, :, start : start + width], sem.at[slot])
+        slot_ref[slot, :, 0:size] = product[:count]
+        copy = pltpu.make_async_copy(
+            slot_ref.at[slot, :, pl.ds(0, size)], out_ref.at[c, :, pl.ds(start, size)], sem.at[slot]
+        )
         copy.start()
         copies.append(copy)
     for copy in copies[-slots:]:

time: 80.1 us -> 80.1 us (level)
  no operation moved by 1% of the time
where the time goes in v6:
time: 80.1 us; the launch traced here: 79.9 us
  blocking collectives  47.9 us (60%)
  Pallas kernels  20.6 us (26%)
  starting transfers between devices  10.5 us (13%)
  between operations  0.92 us (1%)
    all_to_all x1, blocking collectives, per_device(): lax.all_to_all(outgoing, 'brick', split_axis=0, concat_axis=0, tiled=True)  32.3 us
    all_to_all x1, blocking collectives, tail(): partial_sums = lax.all_to_all(copies, ('brick', 'ana'), 0, 0, tiled=True)  15.7 us
    ppermute x3, starting transfers between devices, exchange(): lax.ppermute(to_after, axis, up)  6.52 us
    pallas_call x1, Pallas kernels, tail(): grid_kernel(functools.partial(apply_kernel, width, SLOTS), 'apply', (10 *...  5.78 us
    ppermute x3, starting transfers between devices, exchange(): lax.ppermute(to_before, axis, down)  3.96 us
    pallas_call x1, Pallas kernels, front(): grid_kernel(functools.partial(inner_kernel, POOL_PARTS), 'inner_layers',...  3.69 us
    pallas_call x1, Pallas kernels, front(): grid_kernel(load_kernel, 'load', (10 ** 8, 6 * 10 ** 6), in_specs=[pl.Blo...  3.25 us
    pallas_call x1, Pallas kernels, tail(): grid_kernel(functools.partial(gram_kernel, width, 1.0 / total_rows), 'gra...  2.82 us
  transfers between devices with their start and end apart: 6, of which 0 were waited for; matrix products, arithmetic and copies ran while one was open for 0% of the time, Pallas kernels for 9%

profile of v6, /device:TPU:1, one launch (start us, length us, event | category | flops | bytes accessed | tf_op | source)
XLA Modules:
  0.0 79.9 jit_solution(14099922100937523863)
XLA Ops:
  0.6 2.0 %ana_edges.1 = (f32[4,56,256]{2,1,0:T(8,128)S(1)}, f32[4,56,256]{2,1,0:T(8,128)S(1)}) custom-call(f32[12,16,4,16,128]{4,3,2,1,0:T(8,128)} %bitcast.15), custom_call_target="tpu_custom_call" | custom-call | flops 1000000 | bytes 4000000 | tf_op jit(solution)/shard_map/ana_edges/pallas_call | solution.py:549
  2.6 2.1 %collective-permute-start = (f32[4,56,256]{2,1,0:T(8,128)S(1)}, f32[4,56,256]{2,1,0:T(8,128)S(1)}, u32[]{:S(2)}, u32[]{:S(2)}) collective-permute-start(f32[4,56,256]{2,1,0:T(8,128)S(1)} %get-tuple-element.25), channel_id=1, source_target_pairs={{0,1},{1,2},{2,3},{3,0},{4,5},{5,6},{6,7},{7,4},{8,9},{9,10},{10,1... | collective-permute-start | bytes 688136 | tf_op jit(solution)/shard_map/ppermute | solution.py:523
  4.8 1.3 %collective-permute-start.1 = (f32[4,56,256]{2,1,0:T(8,128)S(1)}, f32[4,56,256]{2,1,0:T(8,128)S(1)}, u32[]{:S(2)}, u32[]{:S(2)}) collective-permute-start(f32[4,56,256]{2,1,0:T(8,128)S(1)} %get-tuple-element.19._), channel_id=1, source_target_pairs={{1,0},{2,1},{3,2},{0,3},{5,4},{6,5},{7,6},{4,7},{9,8},{10,9},{11,1... | collective-permute-start | bytes 688136 | tf_op jit(solution)/shard_map/ppermute | solution.py:523
  6.1 3.3 %load.1 = (f32[4,16,32,256]{3,2,1,0:T(8,128)S(1)}, f32[4,16,32,256]{3,2,1,0:T(8,128)S(1)}, f32[4,16,32,256]{3,2,1,0:T(8,128)S(1)}, f32[4,16,32,256]{3,2,1,0:T(8,...) custom-call(f32[12,16,32,256]{3,2,1,0:T(8,128)} %bitcast.16, f32[4,56,256]{2,1,0:T(8,128)S(1)} %get-tuple-element.19._), custom_call_target="tpu_custom_call" | custom-call | flops 100000000 | bytes 6000000 | tf_op jit(solution)/shard_map/load/pallas_call | solution.py:570
  9.4 2.6 %collective-permute-start.2 = (f32[4,96,256]{2,1,0:T(8,128)S(1)}, f32[4,96,256]{2,1,0:T(8,128)S(1)}, u32[]{:S(2)}, u32[]{:S(2)}) collective-permute-start(f32[4,96,256]{2,1,0:T(8,128)S(1)} %get-tuple-element.26), channel_id=1, source_target_pairs={{0,4},{4,8},{8,12},{12,16},{16,20},{20,24},{24,28},{28,32},{32,36}... | collective-permute-start | bytes 1179656 | tf_op jit(solution)/shard_map/ppermute | solution.py:523
  12.0 0.0 collective-permute-start.3
  12.0 0.3 weights.1
  12.3 0.0 collective-permute-done.from_low_ref.low_ref
  12.3 0.0 collective-permute-done.1.from_high_ref.high_ref
  12.3 0.0 copy-start.1
  12.3 0.1 fix.1
  12.4 1.8 %collective-permute-start.4 = (f32[4,16,256]{2,1,0:T(8,128)S(1)}, f32[4,16,256]{2,1,0:T(8,128)S(1)}, u32[]{:S(2)}, u32[]{:S(2)}) collective-permute-start(f32[4,16,256]{2,1,0:T(8,128)S(1)} %get-tuple-element.29), channel_id=1, source_target_pairs={{0,4},{4,8},{8,12},{12,16},{16,20},{20,24},{24,28},{28,32},{32,36}... | collective-permute-start | bytes 196616 | tf_op jit(solution)/shard_map/ppermute | solution.py:523
  14.3 2.6 %collective-permute-start.5 = (f32[4,16,256]{2,1,0:T(8,128)S(1)}, f32[4,16,256]{2,1,0:T(8,128)S(1)}, u32[]{:S(2)}, u32[]{:S(2)}) collective-permute-start(f32[4,16,256]{2,1,0:T(8,128)S(1)} %get-tuple-element.30), channel_id=1, source_target_pairs={{4,0},{8,4},{12,8},{16,12},{20,16},{24,20},{28,24},{32,28},{36,32}... | collective-permute-start | bytes 196616 | tf_op jit(solution)/shard_map/ppermute | solution.py:523
  16.9 3.7 %inner_layers.1 = (f32[4,16,2,48,128]{4,3,2,1,0:T(8,128)S(1)}, f32[4,16,2,48,128]{4,3,2,1,0:T(8,128)S(1)}, f32[32,3,32,128]{3,2,1,0:T(8,128)S(1)}) custom-call(s32[32,32]{1,0:T(8,128)S(1)} %copy-done.1, f32[4,16,32,256]{3,2,1,0:T(8,128)S(1)} %get-tuple-element.20.along_ref, f32[4,16,32,256]{3,2,1,0:T(8,128)S(1)} %get-tuple-element.21.cross_ref, ...), custom_call_target="tpu_custom_call" | custom-call | flops 4000000000 | bytes 20000000 | tf_op jit(solution)/shard_map/inner_layers/pallas_call | solution.py:592
  20.6 0.0 collective-permute-done.4.before_fix_ref
  20.6 0.0 collective-permute-done.5.after_fix_ref
  20.6 0.0 collective-permute-done.2.before_ref
  20.6 0.0 slice-start
  20.6 0.0 slice-start.1
  20.6 2.6 %outer_layers.1 = f32[32,3,32,128]{3,2,1,0:T(8,128)S(1)} custom-call(s32[32,32]{1,0:T(8,128)S(1)} %copy-done.1, f32[4,16,32,256]{3,2,1,0:T(8,128)S(1)} %get-tuple-element.20.along_ref, f32[4,16,32,256]{3,2,1,0:T(8,128)S(1)} %get-tuple-element.21.cross_ref, f32[4,16,32,256]{3,2,1,0:T(8,128)S(1)} %get-tuple-element.22.deep_ref, ...), custom_call_target="tpu_custom_call", output_to_operand_aliasing={{}: (14, {})} | custom-call | flops 3000000000 | bytes 10000000 | tf_op jit(solution)/shard_map/outer_layers/pallas_call | solution.py:605
  23.2 32.3 %all_to_all.10.arrived_ref = f32[32,3,32,128]{3,2,1,0:T(8,128)S(1)} all-to-all(f32[32,3,32,128]{3,2,1,0:T(8,128)S(1)} %outer_layers.1), channel_id=1, replica_groups=mesh['brick'=32,'ana'=4] {'brick'}, dimensions={0} | all-to-all | bytes 3145728 | tf_op jit(solution)/shard_map/all_to_all | solution.py:630
  55.5 2.8 %gram.1 = f32[128,4,128]{2,1,0:T(4,128)S(1)} custom-call(f32[3,16,32768]{2,1,0:T(8,128)S(1)} %bitcast.12, f32[32,3,32,128]{3,2,1,0:T(8,128)S(1)} %all_to_all.10.arrived_ref), custom_call_target="tpu_custom_call" | custom-call | flops 1000000000 | bytes 10000000 | tf_op jit(solution)/shard_map/gram/pallas_call | solution.py:139
  58.3 15.7 %all_to_all.11.packed_ref = f32[128,4,128]{2,1,0:T(4,128)S(1)} all-to-all(f32[128,4,128]{2,1,0:T(4,128)S(1)} %gram.1), channel_id=1, replica_groups=mesh['brick'=32,'ana'=4] {'brick','ana'}, dimensions={0} | all-to-all | bytes 524288 | tf_op jit(solution)/shard_map/all_to_all | solution.py:147
  74.0 5.8 %apply.1 = (f32[3,20,32768]{2,1,0:T(8,128)}, f32[24,128]{1,0:T(8,128)}) custom-call(f32[3,16,32768]{2,1,0:T(8,128)S(1)} %bitcast.13, f32[32,3,32,128]{3,2,1,0:T(8,128)S(1)} %all_to_all.10.arrived_ref, f32[128,4,128]{2,1,0:T(4,128)S(1)} %all_to_all.11.packed_ref), custom_call_target="tpu_custom_call" | custom-call | flops 1000000000 | bytes 20000000 | tf_op jit(solution)/shard_map/apply/pallas_call | solution.py:149
  (7 shorter events, 0.0 us)
Async XLA Ops:
  2.6 9.7 %collective-permute-start = (f32[4,56,256]{2,1,0:T(8,128)S(1)}, f32[4,56,256]{2,1,0:T(8,128)S(1)}, u32[]{:S(2)}, u32[]{:S(2)}) collective-permute-start(f32[4,56,256]{2,1,0:T(8,128)S(1)} %get-tuple-element.25), channel_id=1, source_target_pairs={{0,1},{1,2},{2,3},{3,0},{4,5},{5,6},{6,7},{7,4},{8,9},{9,10},{10,1... | collective-permute-start | bytes 688136 | tf_op jit(solution)/shard_map/ppermute | solution.py:523
  4.8 7.6 %collective-permute-start.1 = (f32[4,56,256]{2,1,0:T(8,128)S(1)}, f32[4,56,256]{2,1,0:T(8,128)S(1)}, u32[]{:S(2)}, u32[]{:S(2)}) collective-permute-start(f32[4,56,256]{2,1,0:T(8,128)S(1)} %get-tuple-element.19._), channel_id=1, source_target_pairs={{1,0},{2,1},{3,2},{0,3},{5,4},{6,5},{7,6},{4,7},{9,8},{10,9},{11,1... | collective-permute-start | bytes 688136 | tf_op jit(solution)/shard_map/ppermute | solution.py:523
  6.1 5.9 %copy-start = (s32[1,1,32768]{2,1,0:T(1,128)S(1)}, s32[1,1,32768]{2,1,0:T(1,128)}, u32[]{:S(2)}) copy-start(s32[1,1,32768]{2,1,0:T(1,128)} %param.5) | copy-start | bytes 393220
  9.4 11.2 %collective-permute-start.2 = (f32[4,96,256]{2,1,0:T(8,128)S(1)}, f32[4,96,256]{2,1,0:T(8,128)S(1)}, u32[]{:S(2)}, u32[]{:S(2)}) collective-permute-start(f32[4,96,256]{2,1,0:T(8,128)S(1)} %get-tuple-element.26), channel_id=1, source_target_pairs={{0,4},{4,8},{8,12},{12,16},{16,20},{20,24},{24,28},{28,32},{32,36}... | collective-permute-start | bytes 1179656 | tf_op jit(solution)/shard_map/ppermute | solution.py:523
  12.0 8.6 %collective-permute-start.3 = (f32[4,96,256]{2,1,0:T(8,128)S(1)}, f32[4,96,256]{2,1,0:T(8,128)S(1)}, u32[]{:S(2)}, u32[]{:S(2)}) collective-permute-start(f32[4,96,256]{2,1,0:T(8,128)S(1)} %get-tuple-element.27), channel_id=1, source_target_pairs={{4,0},{8,4},{12,8},{16,12},{20,16},{24,20},{28,24},{32,28},{36,32}... | collective-permute-start | bytes 1179656 | tf_op jit(solution)/shard_map/ppermute | solution.py:523
  12.3 4.5 %copy-start.1 = (s32[32,32]{1,0:T(8,128)S(1)}, s32[32,32]{1,0:T(8,128)}, u32[]{:S(2)}) copy-start(s32[32,32]{1,0:T(8,128)} %owner_ref.3) | copy-start | bytes 12292
  12.4 8.1 %collective-permute-start.4 = (f32[4,16,256]{2,1,0:T(8,128)S(1)}, f32[4,16,256]{2,1,0:T(8,128)S(1)}, u32[]{:S(2)}, u32[]{:S(2)}) collective-permute-start(f32[4,16,256]{2,1,0:T(8,128)S(1)} %get-tuple-element.29), channel_id=1, source_target_pairs={{0,4},{4,8},{8,12},{12,16},{16,20},{20,24},{24,28},{28,32},{32,36}... | collective-permute-start | bytes 196616 | tf_op jit(solution)/shard_map/ppermute | solution.py:523
  14.3 6.3 %collective-permute-start.5 = (f32[4,16,256]{2,1,0:T(8,128)S(1)}, f32[4,16,256]{2,1,0:T(8,128)S(1)}, u32[]{:S(2)}, u32[]{:S(2)}) collective-permute-start(f32[4,16,256]{2,1,0:T(8,128)S(1)} %get-tuple-element.30), channel_id=1, source_target_pairs={{4,0},{8,4},{12,8},{16,12},{20,16},{24,20},{28,24},{32,28},{36,32}... | collective-permute-start | bytes 196616 | tf_op jit(solution)/shard_map/ppermute | solution.py:523
  20.6 34.9 %slice-start = ((s8[6291456]{0:T(1024)(128)(4,1)}), s8[4194304]{0:T(1024)(128)(4,1)S(1)}, s32[]{:S(2)}) async-start(s8[6291456]{0:T(1024)(128)(4,1)} %bitcast.10), calls=%async_computation.2 | async-start | bytes 8388608
  20.6 34.9 %slice-start.1 = ((s8[6291456]{0:T(1024)(128)(4,1)}), s8[2097152]{0:T(1024)(128)(4,1)S(1)}, s32[]{:S(2)}) async-start(s8[6291456]{0:T(1024)(128)(4,1)} %bitcast.10), calls=%async_computation.3 | async-start | bytes 4194304
